TPU v7x, 32 devices: a whole 2x2x4 slice. The times are simulated.
32 devices in a mesh: col: 4 (over y, x), row: 8 (over z, core).
Axes of the slice: x: 2, y: 2, z: 4, core: 2. Of those that a mesh axis runs over, the one named last changes fastest.
Arguments:
- corner_top_left: bfloat16 [400, 800], P('col', 'row'), may hold values from -0.625 to 0.625
- corner_top_right: bfloat16 [400, 800], P('col', 'row'), may hold values from -0.625 to 0.625
- corner_bottom_left: bfloat16 [400, 800], P('col', 'row'), may hold values from -0.625 to 0.625
- edge_top: bfloat16 [400, 20000], P('col', 'row'), may hold values from -6 to 6
- edge_right: bfloat16 [400, 20000], P('col', 'row'), may hold values from -6 to 6
- edge_bottom: bfloat16 [400, 20000], P('col', 'row'), may hold values from -6 to 6
- edge_left: bfloat16 [400, 20000], P('col', 'row'), may hold values from -6 to 6
- tensors: bfloat16 [8, 625, 625], replicated, may hold values from -0.25 to 0.25
- pattern: int32 [4, 8], P('col', 'row'), may hold values from 0 to 7, as said below
- sketch_below: float32 [100, 100], replicated, may hold values from -0.4375 to 0.4375
- sketch_above: float32 [100, 100], replicated, may hold values from -0.4375 to 0.4375
- sketch_right: float32 [100, 100], replicated, may hold values from -0.4375 to 0.4375
- sketch_left: float32 [100, 100], replicated, may hold values from -0.4375 to 0.4375
Outputs:
- left_corner_top: bfloat16 [400, 800], P('col', 'row')
- left_edge: bfloat16 [400, 20000], P('col', 'row')
- left_corner_bottom: bfloat16 [400, 800], P('col', 'row')
- top_corner_left: bfloat16 [400, 800], P('col', 'row')
- top_edge: bfloat16 [400, 20000], P('col', 'row')
- top_corner_right: bfloat16 [400, 800], P('col', 'row')
Inputs may be any that keep to these rules, and one draw needn't show every extreme that they name: `pattern`: each of the 8 tensors sits at exactly 4 sites.
All inputs are finite; a program needn't handle non-finite values.
Results may differ from a plain program's by a relative error of at most 0.039.
Values may be sent and summed in bfloat16 or wider, within the bound.
No kernel may reach another device: no remote copies, remote signals or barrier semaphores. Data moves between devices by JAX's collectives and lax.ppermute only.
A program may use at most 192 MiB of HBM per device.

v0:
```python
import functools

import jax
import jax.numpy as jnp
import numpy as np
from jax import lax
from jax.experimental import pallas as pl
from jax.experimental.pallas import tpu as pltpu
from jax.sharding import PartitionSpec as P

LANES = 128
ROWS = 8
HALF_TILE = 16
GROUP = 10
CUTS = 4
QUARTERS = 4
MIB = 1 << 20
F32 = jnp.float32
BF16 = jnp.bfloat16

NN = (((1,), (0,)), ((), ()))
NT = (((1,), (1,)), ((), ()))
TN = (((0,), (0,)), ((), ()))


def product(left, right, dims=NN):
    return lax.dot_general(left, right, dims, preferred_element_type=F32)


def halves(values):
    high = values.astype(BF16)
    return high, (values - high.astype(F32)).astype(BF16)


def product_split(left, right, dims=NN):
    left_high, left_low = halves(left)
    right_high, right_low = halves(right)
    axis_left, axis_right = dims[0][0][0], dims[0][1][0]
    both = jnp.concatenate([left_high, left_low], axis_left)
    twice = jnp.concatenate([right_high, right_high], axis_right)
    return product(both, twice, dims) + product(left_high, right_low, dims)


def index_of(shape, axis):
    return lax.broadcasted_iota(jnp.int32, shape, axis)


def square_of(ref, bond):
    shape = (LANES, LANES)
    keep = (index_of(shape, 0) < bond) & (index_of(shape, 1) < bond)
    return jnp.where(keep, ref[...].astype(F32), 0.0)


def spread(ref, bond, site):
    shape = (LANES, LANES)
    row, lane = index_of(shape, 0), index_of(shape, 1)
    keep = (row < bond) & (lane < bond)
    pieces = []
    for k in range(site):
        tile, offset = divmod(k * bond, LANES)
        piece = ref[:, tile * LANES : (tile + 1) * LANES].astype(F32)
        if offset:
            piece = pltpu.roll(piece, LANES - offset, 1)
        if offset + bond > LANES:
            more = ref[:, (tile + 1) * LANES : (tile + 2) * LANES].astype(F32)
            piece = jnp.where(lane < LANES - offset, piece, pltpu.roll(more, LANES - offset, 1))
        pieces.append(jnp.where(keep, piece, 0.0).astype(BF16))
    return pieces


def gather_dense(tiles, ref, bond):
    lane = index_of((LANES, LANES), 1)
    total = len(tiles) * bond
    for tile in range(-(-total // LANES)):
        begin = tile * LANES
        value = None
        for k in range(begin // bond, min(len(tiles) - 1, (begin + LANES - 1) // bond) + 1):
            shift = k * bond - begin
            piece = pltpu.roll(tiles[k], shift % LANES, 1) if shift % LANES else tiles[k]
            value = piece if value is None else jnp.where(lane >= shift, piece, value)
        ref[:, begin : begin + LANES] = value.astype(ref.dtype)


def pack(tiles, ref, bond):
    quarter = bond // QUARTERS
    lane = index_of((LANES, LANES), 1)
    for group in range(len(tiles) // (QUARTERS + 1)):
        first = group * (QUARTERS + 1)
        for m in range(QUARTERS):
            piece = pltpu.roll(tiles[first + QUARTERS], bond - m * quarter, 1)
            slot = group * QUARTERS + m
            value = jnp.where(lane < bond, tiles[first + m], piece)
            ref[:, slot * LANES : (slot + 1) * LANES] = value.astype(ref.dtype)


def unpack(ref, bond, site):
    quarter = bond // QUARTERS
    shape = (LANES, LANES)
    row, lane = index_of(shape, 0), index_of(shape, 1)
    keep = (row < bond) & (lane < bond)
    tiles = []
    for group in range(site // (QUARTERS + 1)):
        last = None
        for m in range(QUARTERS):
            slot = group * QUARTERS + m
            value = ref[:, slot * LANES : (slot + 1) * LANES].astype(F32)
            tiles.append(jnp.where(keep, value, 0.0).astype(BF16))
            piece = pltpu.roll(value, LANES - bond + m * quarter, 1)
            last = piece if last is None else jnp.where(lane >= m * quarter, piece, last)
        tiles.append(jnp.where(keep, last, 0.0).astype(BF16))
    return tiles


def sketched(stack, sketch):
    return product(jnp.concatenate([stack, stack], 1), jnp.concatenate(halves(sketch), 0))


def inverse_factors(grams, bond):
    count = -(-bond // ROWS) * ROWS
    shape = (count, LANES)
    row, lane = index_of(shape, 0), index_of(shape, 1)
    inside = (row < bond) & (lane < bond)
    eye = jnp.where(row == lane, 1.0, 0.0)
    work = [jnp.where(inside, gram[:count], eye) for gram in grams]
    done = [[] for _ in grams]
    for first in range(0, count, ROWS):
        height = count - first
        row, lane = index_of((height, LANES), 0), index_of((height, LANES), 1)
        block = (lane >= first) & (lane < first + ROWS)
        start = jnp.where(row == lane - first, 1.0, 0.0)
        small_row, small_lane = index_of((ROWS, LANES), 0), index_of((ROWS, LANES), 1)
        columns = []
        for n, matrix in enumerate(work):
            columns.append(
                [
                    jnp.broadcast_to(matrix[:, first + j : first + j + 1], (height, LANES))
                    for j in range(ROWS)
                ]
            )
            work[n] = jnp.where(block, start, matrix)
        pivots = [jnp.ones((ROWS, LANES), F32) for _ in work]
        for j in range(ROWS):
            for n in range(len(work)):
                column = columns[n]
                pivot = column[j][j : j + 1, :]
                factor = jnp.where(row > j, column[j] * (1.0 / pivot), 0.0)
                work[n] = work[n] - factor * work[n][j : j + 1, :]
                for later in range(j + 1, ROWS):
                    column[later] = column[later] - factor * column[later][j : j + 1, :]
                pivots[n] = jnp.where(small_row == j, pivot, pivots[n])
        for n in range(len(work)):
            scaled = work[n][:ROWS] * lax.rsqrt(pivots[n])
            done[n].append(jnp.where(small_lane <= small_row + first, scaled, 0.0))
            work[n] = work[n][ROWS:]
    tail = jnp.zeros((LANES - count, LANES), F32)
    keep = (index_of((LANES, LANES), 0) < bond) & (index_of((LANES, LANES), 1) < bond)
    return [jnp.where(keep, jnp.concatenate(parts + [tail], 0), 0.0) for parts in done]


def gram_and(values, other):
    both = product(values, jnp.concatenate([values, other], 1), TN)
    return both[:, :LANES], both[:, LANES:]


def frame_from(values, inverse):
    high, low = halves(inverse)
    both = jnp.concatenate([values, values], 1)
    return product(both, jnp.concatenate([high, low], 1), NT)


def scaled_corner(values, bond):
    mean = jnp.sum(values * values) / (bond * bond)
    return (values / jnp.sqrt(mean + 1e-06)).astype(BF16)


def half_tiles(corner, pieces):
    return [product(corner, piece) for piece in pieces]


def fill(stack, tiles):
    for k, tile in enumerate(tiles):
        stack[k * LANES : (k + 1) * LANES, :] = tile.astype(stack.dtype)


def store_frame_rows(sketch, inverse, rows_ref, plain, tail, site):
    main = site - 1
    bond_rows = plain.shape[0] // main
    both = jnp.concatenate(halves(inverse), 1)[:bond_rows]
    for k in range(site):
        piece = sketch[k * LANES : (k + 1) * LANES, :]
        tile = product(both, jnp.concatenate([piece, piece], 1), NT)
        if k < main:
            plain[pl.ds(k, bond_rows, stride=main), :] = tile
        else:
            for group in range(tail.shape[0] // HALF_TILE):
                begin = group * HALF_TILE
                tail[begin : begin + GROUP, :] = tile[group * GROUP : (group + 1) * GROUP]
    rows_ref[: plain.shape[0], :] = plain[...].astype(BF16)
    rows_ref[plain.shape[0] :, :] = tail[...].astype(BF16)


def halves_kernel(bond, site, c1, t1, c4, t3, upper_packed, lower_packed):
    for corner, edge, packed in ((c1, t1, upper_packed), (c4, t3, lower_packed)):
        pack(half_tiles(square_of(corner, bond).astype(BF16), spread(edge, bond, site)), packed, bond)


def prepare_kernel(
    bond, site, c2, t2, t4, t1, above, below, right, upper_packed, lower_packed,
    t4_wide, t1_out, upper, upper_sketch, lower, lower_sketch, side_packed, side, side_sketch,
):
    t1_out[...] = t1[...]
    tiles = half_tiles(square_of(c2, bond).astype(BF16), spread(t2, bond, site))
    fill(side, tiles)
    pack(tiles, side_packed, bond)
    fill(upper, unpack(upper_packed, bond, site))
    fill(lower, unpack(lower_packed, bond, site))
    upper_sketch[...] = sketched(upper[...], square_of(above, bond))
    lower_sketch[...] = sketched(lower[...], square_of(below, bond))
    side_sketch[...] = sketched(side[...], square_of(right, bond))
    for k, piece in enumerate(spread(t4, bond, site)):
        t4_wide[:, k * LANES : (k + 1) * LANES] = piece


def vertical_kernel(
    bond, site, upper_packed, lower_packed, above, below, upper, upper_sketch, lower, lower_sketch,
    pattern, rows_ref, frame_out, corner_top, corner_bottom, pattern_out, stack, over, under, plain, tail,
):
    pattern_out[0] = pattern[0]
    fill(stack, unpack(upper_packed, bond, site))
    under[...] = (lower_sketch[...] + sketched(stack[...], square_of(above, bond))).astype(BF16)
    fill(stack, unpack(lower_packed, bond, site))
    over[...] = (upper_sketch[...] + sketched(stack[...], square_of(below, bond))).astype(BF16)
    gram_over, mixed_over = gram_and(over[...], upper[...])
    gram_under, mixed_under = gram_and(under[...], lower[...])
    inverse_over, inverse_under = inverse_factors([gram_over, gram_under], bond)
    store_frame_rows(over, inverse_over, rows_ref, plain, tail, site)
    frame_out[...] = frame_from(under[...], inverse_under).astype(BF16)
    corner_top[...] = scaled_corner(product_split(inverse_over, mixed_over), bond)
    corner_bottom[...] = scaled_corner(product_split(inverse_under, mixed_under), bond)


def horizontal_kernel(
    bond, site, c1, c4, edge, left, side, side_sketch, inverse_ref, frame_out, half, total
):
    corner = square_of(c1, bond).T.astype(BF16)
    fill(half, half_tiles(corner, [edge[:, k * LANES : (k + 1) * LANES] for k in range(site)]))
    total[...] = (side_sketch[...] + sketched(half[...], square_of(left, bond))).astype(BF16)
    gram, mixed = gram_and(total[...], side[...])
    (inverse,) = inverse_factors([gram], bond)
    inverse_ref[:, :LANES] = inverse
    inverse_ref[:, LANES:] = square_of(c4, bond)
    frame = frame_from(total[...], inverse)
    pack([frame[k * LANES : (k + 1) * LANES, :] for k in range(site)], frame_out, bond)
    corner_right = scaled_corner(product_split(inverse, mixed), bond)
    frame_out[:, frame_out.shape[1] - LANES :] = corner_right


def early_kernel(bond, site, side_packed, right, t1, after, side_sketch, t1_wide, stack):
    for k, piece in enumerate(spread(t1, bond, site)):
        t1_wide[:, k * LANES : (k + 1) * LANES] = piece
    fill(stack, unpack(side_packed, bond, site))
    side_sketch[...] = sketched(stack[...], square_of(right, bond))


def arrive_kernel(
    bond, site, payload, side_sketch, left, inverse_ref,
    rows_ref, corner_left, forward, half, total, plain, tail,
):
    start = payload.shape[1] - LANES
    corner = square_of(payload.at[:, start:], bond).T.astype(BF16)
    fill(half, half_tiles(corner, spread(payload, bond, site)))
    total[...] = (side_sketch[...] + sketched(half[...], square_of(left, bond))).astype(BF16)
    inverse = inverse_ref[:, :LANES]
    store_frame_rows(total, inverse, rows_ref, plain, tail, site)
    mixed = product(half[...], total[...], TN)
    corner_left[...] = scaled_corner(product_split(mixed, inverse, NT), bond)
    forward[:, : payload.shape[1]] = payload[...]
    forward[:, payload.shape[1] :] = inverse_ref[:, LANES:].astype(BF16)


def finish_kernel(bond, payload, frame, left_corner, left_edge, left_bottom, top_right):
    start = payload.shape[1] - 2 * LANES
    left_edge[...] = payload[:, :start]
    left_corner[...] = payload[:, start : start + LANES]
    left_bottom[...] = payload[:, start + LANES :]
    top_right[...] = frame[:, frame.shape[1] - LANES :]


def absorb_kernel(bond, site, first, rows_ref, edge, tensor, frame, *refs):
    mixed_even, mixed_odd, spare_even, spare_odd, pushed_even, pushed_odd, last, result = refs[-8:]
    if first:
        corner, dense, wide = refs[:3]
        frame_out = frame
    else:
        dense, frame_out = refs[0], refs[1]
        fill(frame_out, unpack(frame, bond, site))
    main = site - 1
    groups = bond // GROUP
    tall = GROUP * main
    slot = spare_even.shape[0] // HALF_TILE
    spare_even[...] = jnp.zeros_like(spare_even)
    spare_odd[...] = jnp.zeros_like(spare_odd)
    ahead = tall + bond * main
    result[ahead:, :] = jnp.zeros((result.shape[0] - ahead, LANES), F32)

    def frames_of(group):
        body = rows_ref[pl.ds(pl.multiple_of(group * tall, tall), tall), :]
        begin = rows_ref.shape[0] - groups * HALF_TILE + group * HALF_TILE
        tail = rows_ref[pl.ds(pl.multiple_of(begin, HALF_TILE), HALF_TILE), :]
        return jnp.concatenate([body, tail], 0)

    def mix(frames, mixed, spare, unit):
        j = 2 * unit
        sides = min(2, site - j)
        both = product(frames, edge[:, j * LANES : (j + sides) * LANES])
        for side in range(sides):
            lanes = slice(side * LANES, (side + 1) * LANES)
            spare[pl.ds(j + side, HALF_TILE, stride=slot), :] = both[tall:, lanes]
        for p in range(GROUP):
            parts = [
                both[p * main : (p + 1) * main, side * LANES : (side + 1) * LANES]
                for side in range(sides)
            ]
            end = (j + sides) * main
            if sides == 1:
                end = mixed.shape[0]
                parts.append(spare[p * slot : (p + 1) * slot, :])
                parts.append(jnp.zeros((end - j * main - main - slot, LANES), F32))
            mixed[j * main : end, p * LANES : (p + 1) * LANES] = (
                jnp.concatenate(parts, 0).astype(BF16)
            )

    def push(group, mixed, pushed, pair):
        out = product(tensor[...], mixed[:, 2 * pair * LANES : (2 * pair + 2) * LANES])
        for k in range(site):
            parts = [
                out[k * main : (k + 1) * main, side * LANES : (side + 1) * LANES]
                for side in range(2)
            ]
            pushed[2 * pair * main : (2 * pair + 2) * main, k * LANES : (k + 1) * LANES] = (
                jnp.concatenate(parts, 0).astype(BF16)
            )
        for side in range(2):
            place = group * GROUP + 2 * pair + side
            last[pl.ds(place, site, stride=LANES), :] = out[
                site * main : site * main + site, side * LANES : (side + 1) * LANES
            ]

    def cuts():
        step = -(-site // CUTS) // 2 * 2
        starts = [n * step for n in range(CUTS)] + [site]
        return [slice(low * LANES, high * LANES) for low, high in zip(starts, starts[1:])]

    def close(group, total):
        result[pl.ds(pl.multiple_of((group + 1) * tall, tall), tall), :] = total

    units = (site + 1) // 2

    def stage(group, mixed, pushed, mixed_next, spare_next, pushed_before):
        frames = frames_of(jnp.minimum(group + 1, groups - 1))
        total = jnp.zeros((tall, LANES), F32)
        pairs = GROUP // 2
        parts = cuts()
        for n in range(pairs):
            push(group, mixed, pushed, n)
            for unit in range(n * units // pairs, (n + 1) * units // pairs):
                mix(frames, mixed_next, spare_next, unit)
            if n < CUTS:
                total = total + product(pushed_before[:, parts[n]], frame_out[parts[n], :])
        close(group - 1, total)

    frames = frames_of(0)
    for unit in range(units):
        mix(frames, mixed_even, spare_even, unit)

    def step(index, carry):
        stage(2 * index, mixed_even, pushed_even, mixed_odd, spare_odd, pushed_odd)
        stage(2 * index + 1, mixed_odd, pushed_odd, mixed_even, spare_even, pushed_even)
        return carry

    lax.fori_loop(0, groups // 2, step, 0)
    close(groups - 1, product(pushed_odd[...], frame_out[...]))
    tiles = [result[pl.ds(tall + k, LANES, stride=main), :] for k in range(main)]
    total = jnp.zeros((LANES, LANES), F32)
    for k in range(site):
        rows = pl.ds(k * LANES, LANES)
        total = total + product(last[rows, :].astype(BF16), frame_out[rows, :])
    tiles.append(jnp.where(index_of(total.shape, 0) < bond, total, 0.0))
    squares = tiles[0] * tiles[0]
    for tile in tiles[1:]:
        squares = squares + tile * tile
    scale = 1.0 / jnp.sqrt(jnp.sum(squares) / (bond * bond * site) + 1e-06)
    tiles = [tile * scale for tile in tiles]
    gather_dense(tiles, dense, bond)
    if first:
        for k, tile in enumerate(tiles):
            wide[:, k * LANES : (k + 1) * LANES] = tile.astype(BF16)
        dense[:, dense.shape[1] - LANES :] = square_of(corner, bond).astype(BF16)


def arrange_kernel(pattern, tensors, rows, columns, after, out, tensor, semaphore):
    copy = pltpu.make_async_copy(tensors.at[pattern[0]], tensor, semaphore)
    copy.start()
    square = tensor.shape[0]
    pick_rows = jnp.where(index_of((rows.shape[0], square), 1) == rows[...], 1.0, 0.0).astype(BF16)
    pick_columns = jnp.where(index_of((square, columns.shape[1]), 0) == columns[...], 1.0, 0.0)
    copy.wait()
    turned = product(pick_rows, tensor[...], NT).astype(BF16)
    out[...] = product(turned, pick_columns.astype(BF16)).astype(BF16)


def places(site):
    main = site - 1
    size = -(-site * site // LANES) * LANES
    rows = np.full((2, size), -1, np.int32)
    columns = np.full((2, size), -1, np.int32)
    for other in range(site):
        for inner in range(site):
            at = other * main + inner if inner < main else site * main + other
            rows[0, at] = other * site + inner
            rows[1, at] = inner * site + other
            columns[0, at] = inner * site + other
            columns[1, at] = other * site + inner
    return rows, columns


def block_of(arg):
    shape = arg.shape
    if len(shape) == 1:
        return pl.BlockSpec(memory_space=pltpu.SMEM)
    if shape[0] % 16 == 0 and shape[1] % LANES == 0:
        return pl.BlockSpec(memory_space=pltpu.VMEM)
    return pl.BlockSpec(tuple(-(-size // LANES) * LANES for size in shape), lambda i: (0, 0))


def cost(microseconds):
    return pl.CostEstimate(
        flops=microseconds * 1_000_000_000, bytes_accessed=microseconds * 1_000_000, transcendentals=0
    )


def call(kernel, args, outs, scratch, limit, microseconds, unread=0):
    specs = [block_of(arg) for arg in args]
    if unread:
        specs[-unread:] = [pl.BlockSpec(memory_space=pl.ANY)] * unread
    return pl.pallas_call(
        kernel,
        grid=(1,),
        in_specs=specs,
        out_specs=[block_of(out) for out in outs],
        out_shape=outs,
        scratch_shapes=scratch,
        compiler_params=pltpu.CompilerParams(vmem_limit_bytes=limit * MIB),
        cost_estimate=cost(microseconds),
    )(*args)


def shape_of(shape, dtype=BF16):
    return jax.ShapeDtypeStruct(shape, dtype)


def shift(value, axis, steps):
    count = lax.axis_size(axis)
    pairs = [(source, (source + steps) % count) for source in range(count)]
    return lax.ppermute(value, axis, pairs)


def shift_both(value, steps_col, steps_row):
    columns, rows = lax.axis_size("col"), lax.axis_size("row")
    pairs = []
    for x in range(columns):
        for y in range(rows):
            target = (x + steps_col) % columns * rows + (y + steps_row) % rows
            pairs.append((x * rows + y, target))
    return lax.ppermute(value, ("col", "row"), pairs)


def body(c1, c2, c4, t1, t2, t3, t4, tensors, pattern, below, above, right, left):
    bond = c1.shape[0]
    site = t1.shape[1] // bond
    square = site * site
    tall = site * LANES
    bond_rows = -(-bond // ROWS) * ROWS
    body_rows = bond_rows * (site - 1)
    tail_rows = bond // GROUP * HALF_TILE
    frame_rows = shape_of((body_rows + tail_rows, LANES))
    packed = shape_of((bond, site // (QUARTERS + 1) * QUARTERS * LANES))
    dense = shape_of((bond, site * bond))
    wide = shape_of((LANES, tall))
    stack = shape_of((tall, LANES))
    stack_f32 = shape_of((tall, LANES), F32)
    corner = shape_of((bond, bond))
    payload = shape_of((bond, -(-site * bond // LANES) * LANES + LANES))
    half_bf16 = pltpu.VMEM((tall, LANES), BF16)
    frame_scratch = [pltpu.VMEM((body_rows, LANES), F32), pltpu.VMEM((tail_rows, LANES), F32)]
    rows, columns = places(site)

    def arrange(which, index, after):
        height, depth = rows.shape[1], columns.shape[1]
        vmem = pl.BlockSpec(memory_space=pltpu.VMEM)
        return pl.pallas_call(
            arrange_kernel,
            in_specs=[
                pl.BlockSpec(memory_space=pltpu.SMEM),
                pl.BlockSpec(memory_space=pltpu.HBM),
                vmem,
                vmem,
                pl.BlockSpec(memory_space=pl.ANY),
            ],
            out_specs=vmem,
            out_shape=shape_of((height, depth)),
            scratch_shapes=[pltpu.VMEM((square, square), BF16), pltpu.SemaphoreType.DMA],
            compiler_params=pltpu.CompilerParams(vmem_limit_bytes=16 * MIB),
            cost_estimate=cost(3),
        )(
            index,
            tensors,
            rows[which].reshape(height, 1),
            columns[which].reshape(1, depth),
            after,
        )

    def absorb(first, rows_in, edge, tensor, frame, *more):
        main = site - 1
        mixed = pltpu.VMEM((tensor.shape[1], GROUP * LANES), BF16)
        spare = pltpu.VMEM((HALF_TILE * (-(-site // ROWS) * ROWS), LANES), F32)
        pushed = pltpu.VMEM((GROUP * main, tall), BF16)
        return call(
            functools.partial(absorb_kernel, bond, site, first),
            (rows_in, edge, tensor, frame) + more,
            [payload, wide] if first else [dense],
            ([] if first else [half_bf16])
            + [mixed, mixed, spare, spare, pushed, pushed]
            + [pltpu.VMEM((tall, LANES), F32), pltpu.VMEM(((LANES + GROUP) * main, LANES), F32)],
            28,
            25,
        )

    upper_packed, lower_packed = call(
        functools.partial(halves_kernel, bond, site),
        (c1, t1, c4, t3),
        [packed, packed],
        [],
        60,
        2,
    )
    upper_next = shift(upper_packed, "row", -1)
    lower_back = shift(lower_packed, "row", 1)
    pattern = pattern.reshape(1)
    pattern_back = shift(pattern, "row", 1)
    tensor_left = arrange(0, pattern, upper_packed)
    prepared = call(
        functools.partial(prepare_kernel, bond, site),
        (c2, t2, t4, t1, above, below, right, upper_packed, lower_packed),
        [wide, dense, stack, stack_f32, stack, stack_f32, packed, stack, stack_f32],
        [],
        16,
        2,
    )
    t4_wide, t1_held, upper, upper_sketch, lower, lower_sketch, side_packed, side, side_sketch = prepared
    t1_back = shift(t1_held, "row", 1)
    side_back = shift_both(side_packed, 1, 1)
    rows_left, frame_below, corner_top, corner_bottom, pattern_held = call(
        functools.partial(vertical_kernel, bond, site),
        (upper_next, lower_back, above, below, upper, upper_sketch, lower, lower_sketch)
        + (pattern_back,),
        [frame_rows, stack, corner, corner, shape_of((1,), jnp.int32)],
        [half_bf16, half_bf16, half_bf16] + frame_scratch,
        20,
        8,
    )
    left_new, edge_wide = absorb(True, rows_left, t4_wide, tensor_left, frame_below, corner_top)
    left_back = shift_both(left_new, 1, 1)
    inverse, frame_right = call(
        functools.partial(horizontal_kernel, bond, site),
        (corner_top, corner_bottom, edge_wide, left, side, side_sketch),
        [shape_of((LANES, 2 * LANES), F32), shape_of((bond, packed.shape[1] + LANES))],
        [half_bf16, half_bf16],
        16,
        5,
    )
    inverse_back = shift_both(inverse, 1, 1)
    frame_back = shift(frame_right, "row", 1)
    tensor_top = arrange(1, pattern_held, inverse)
    early_sketch, t1_wide = call(
        functools.partial(early_kernel, bond, site),
        (side_back, right, t1_back, inverse),
        [stack_f32, wide],
        [half_bf16],
        16,
        2,
        1,
    )
    rows_top, top_left, forward = call(
        functools.partial(arrive_kernel, bond, site),
        (left_back, early_sketch, left, inverse_back),
        [frame_rows, corner, shape_of((bond, payload.shape[1] + LANES))],
        [half_bf16, half_bf16] + frame_scratch,
        16,
        4,
    )
    left_here = shift(forward, "row", -1)
    (top_edge,) = absorb(False, rows_top, t1_wide, tensor_top, frame_back)
    left_corner, left_edge, left_bottom, top_right = call(
        functools.partial(finish_kernel, bond),
        (left_here, frame_back),
        [corner, dense, corner, corner],
        [],
        8,
        1,
    )
    return (left_corner, left_edge, left_bottom, top_left, top_edge, top_right)


def solution(mesh):
    block, whole = P("col", "row"), P()
    in_specs = (block,) * 7 + (whole, block) + (whole,) * 4
    return jax.shard_map(
        body, mesh=mesh, in_specs=in_specs, out_specs=(block,) * 6, check_vma=False
    )
```

profile of v0, /device:TPU:0, one launch (start us, length us, event | category | flops | bytes accessed | tf_op | source)
XLA Modules:
  0.0 109.6 jit_solution(5971202042257401139)
XLA Ops:
  0.6 0.0 copy-start
  0.6 0.0 copy-start.10
  0.7 0.0 copy-start.1
  0.7 0.0 copy-start.2
  0.7 0.0 copy-start.7
  0.7 0.0 copy-start.6
  0.7 0.0 copy-start.8
  0.7 3.5 %shard_map.208 = (bf16[100,2560]{1,0:T(8,128)(2,1)}, bf16[100,2560]{1,0:T(8,128)(2,1)}) custom-call(bf16[100,100]{1,0:T(8,128)(2,1)} %c1.1, bf16[100,2500]{1,0:T(8,128)(2,1)} %t1.3, bf16[100,100]{1,0:T(8,128)(2,1)} %c4.1, bf16[100,2500]{1,0:T(8,128)(2,1)} %t3.1), custom_call_target="tpu_custom_call" | custom-call | flops 2000000000 | bytes 2000000 | tf_op jit(solution)/shard_map/pallas_call | solution.py:446
  4.2 4.5 %collective-permute-start = (bf16[100,2560]{1,0:T(8,128)(2,1)}, bf16[100,2560]{1,0:T(8,128)(2,1)S(1)}, u32[]{:S(2)}, u32[]{:S(2)}) collective-permute-start(bf16[100,2560]{1,0:T(8,128)(2,1)} %get-tuple-element.35.upper_packed.after), channel_id=1, source_target_pairs={{0,7},{1,0},{2,1},{3,2},{4,3},{5,4},{6,5},{7,6},{8,15},{9,8},{10,9... | collective-permute-start | bytes 1536008 | tf_op jit(solution)/shard_map/ppermute | solution.py:465
  8.7 0.0 collective-permute-start.1
  8.7 0.0 collective-permute-start.2
  8.7 0.0 copy-done
  8.7 0.0 copy-done.10
  8.7 0.0 copy-done.1
  8.7 0.0 copy-done.2
  8.7 0.0 copy-done.7
  8.7 0.0 copy-done.6
  8.7 0.0 copy-done.8
  8.8 0.0 copy-start.3
  8.8 1.0 copy-done.3
  9.8 1.0 copy-done.4
  10.8 2.0 %shard_map.209 = (bf16[128,3200]{1,0:T(8,128)(2,1)S(1)}, bf16[100,2500]{1,0:T(8,128)(2,1)S(1)}, bf16[3200,128]{1,0:T(8,128)(2,1)S(1)}, f32[3200,128]{1,0:T(8,128...) custom-call(bf16[100,100]{1,0:T(8,128)(2,1)S(1)} %copy-done.10, ...), custom_call_target="tpu_custom_call" | custom-call | flops 2000000000 | bytes 2000000 | tf_op jit(solution)/shard_map/pallas_call | solution.py:446
  12.9 0.0 copy-start.15
  12.9 1.2 %copy-done.15 = f32[3200,128]{1,0:T(8,128)} copy-done((f32[3200,128]{1,0:T(8,128)}, f32[3200,128]{1,0:T(8,128)S(1)}, u32[]{:S(2)}) %copy-start.15) | copy-done | bytes 1638424
  14.0 0.9 copy-done.17
  15.0 0.9 copy-done.19
  15.8 0.9 copy-done.21
  16.7 0.2 collective-permute-start.4
  17.0 1.0 collective-permute-start.5
  18.6 0.0 copy-start.5
  18.6 0.0 copy-start.12
  18.6 0.0 copy-start.14
  18.7 3.7 %copy.23.tensors = bf16[8,625,625]{2,1,0:T(8,128)(2,1)S(1)} copy(bf16[8,625,625]{2,0,1:T(8,128)(2,1)} %param.24) | data formatting | bytes 12500000 | tf_op args[7]
  22.4 0.0 copy-done.5
  22.4 0.0 copy-done.12
  22.4 0.0 copy-done.14
  22.4 0.0 copy-start.16
  22.4 0.0 copy-start.20
  22.4 0.0 copy-start.22
  22.4 2.2 %shard_map.211.tensor = bf16[640,640]{1,0:T(8,128)(2,1)S(1)} custom-call(s32[1]{0:T(128)} %bitcast.1.pattern, bf16[8,625,625]{2,1,0:T(8,128)(2,1)S(1)} %copy.23.tensors, s32[640,1]{1,0:T(8,128)S(1)} %copy-done.12, s32[1,640]{1,0:T(1,128)S(1)} %copy-done.14, bf16[100,2560]{1,0:T(8,128)(2,1)S(1)} %copy-done.5), custom_call_target="tpu_custom_call" | custom-call | flops 3000000000 | bytes 3000000 | tf_op jit(solution)/shard_map/pallas_call | solution.py:501
  24.6 0.0 collective-permute-done.2.pattern
  24.6 0.0 collective-permute-done.upper_packed
  24.7 0.0 collective-permute-done.1.lower_packed
  24.7 0.0 copy-done.16
  24.7 8.2 %shard_map.210 = (bf16[2656,128]{1,0:T(8,128)(2,1)S(1)}, bf16[3200,128]{1,0:T(8,128)(2,1)S(1)}, bf16[100,100]{1,0:T(8,128)(2,1)S(1)}, bf16[100,100]{1,0:T(8,128)(2,1)S(1)}, s32[1]{0:T(128)}) custom-call(bf16[100,2560]{1,0:T(8,128)(2,1)S(1)} %collective-permute-done.upper_packed, bf16[100,2560]{1,0:T(8,128)(2,1)S(1)} %collective-permute-done.1.lower_packed, ...), custom_call_target="tpu_custom_call" | custom-call | flops 8000000000 | bytes 8000000 | tf_op jit(solution)/shard_map/pallas_call | solution.py:446
  33.0 0.0 copy-done.18
  33.0 0.0 copy-start.9
  33.0 25.2 %shard_map.212 = (bf16[100,2688]{1,0:T(8,128)(2,1)S(1)}, bf16[128,3200]{1,0:T(8,128)(2,1)S(1)}) custom-call(bf16[2656,128]{1,0:T(8,128)(2,1)S(1)} %get-tuple-element.41.rows_ref, bf16[128,3200]{1,0:T(8,128)(2,1)S(1)} %copy-done.18, bf16[640,640]{1,0:T(8,128)(2,1)S(1)} %shard_map.211.tensor, bf16[3200,128]{1,0:T(8,128)(2,1)S(1)} %get-tuple-element.43.frame, ...), custom_call_target="tpu_custom_call" | custom-call | flops 24999999488 | bytes 25000000 | tf_op jit(solution)/shard_map/pallas_call | solution.py:446
  58.2 1.8 %collective-permute-start.3 = (bf16[100,2688]{1,0:T(8,128)(2,1)S(1)}, bf16[100,2688]{1,0:T(8,128)(2,1)S(1)}, u32[]{:S(2)}, u32[]{:S(2)}) collective-permute-start(bf16[100,2688]{1,0:T(8,128)(2,1)S(1)} %get-tuple-element.45), channel_id=1, source_target_pairs={{0,9},{1,10},{2,11},{3,12},{4,13},{5,14},{6,15},{7,8},{8,17},{9,18... | collective-permute-start | bytes 1612808 | tf_op jit(solution)/shard_map/ppermute | solution.py:475
  60.0 5.6 %shard_map.213 = (f32[128,256]{1,0:T(8,128)S(1)}, bf16[100,2688]{1,0:T(8,128)(2,1)S(1)}) custom-call(bf16[100,100]{1,0:T(8,128)(2,1)S(1)} %get-tuple-element.44.refs_0_.c1, bf16[100,100]{1,0:T(8,128)(2,1)S(1)} %get-tuple-element.48.c4, bf16[128,3200]{1,0:T(8,128)(2,1)S(1)} %get-tuple-element.49.edge, f32[100,100]{1,0:T(8,128)S(1)} %copy-done.9, ...), custom_call_target="tpu_custom_call" | custom-call | flops 5000000000 | bytes 5000000 | tf_op jit(solution)/shard_map/pallas_call | solution.py:446
  65.6 2.0 %collective-permute-start.6 = (f32[128,256]{1,0:T(8,128)S(1)}, f32[128,256]{1,0:T(8,128)S(1)}, u32[]{:S(2)}, u32[]{:S(2)}) collective-permute-start(f32[128,256]{1,0:T(8,128)S(1)} %get-tuple-element.52.after), channel_id=1, source_target_pairs={{0,9},{1,10},{2,11},{3,12},{4,13},{5,14},{6,15},{7,8},{8,17},{9,18... | collective-permute-start | bytes 393224 | tf_op jit(solution)/shard_map/ppermute | solution.py:475
  67.6 0.7 collective-permute-start.8
  68.3 3.1 %shard_map.217.tensor = bf16[640,640]{1,0:T(8,128)(2,1)S(1)} custom-call(s32[1]{0:T(128)} %get-tuple-element.62.pattern, bf16[8,625,625]{2,1,0:T(8,128)(2,1)S(1)} %copy.23.tensors, s32[640,1]{1,0:T(8,128)S(1)} %copy-done.11, s32[1,640]{1,0:T(1,128)S(1)} %copy-done.13, f32[128,256]{1,0:T(8,128)S(1)} %get-tuple-element.52.after), custom_call_target="tpu_custom_call" | custom-call | flops 3000000000 | bytes 3000000 | tf_op jit(solution)/shard_map/pallas_call | solution.py:501
  71.4 0.0 collective-permute-done.5.t1
  71.4 0.0 collective-permute-done.4.side_packed
  71.4 0.8 shard_map.214
  72.2 3.6 %collective-permute-done.6.inverse_ref = f32[128,256]{1,0:T(8,128)S(1)} collective-permute-done((f32[128,256]{1,0:T(8,128)S(1)}, f32[128,256]{1,0:T(8,128)S(1)}, u32[]{:S(2)}, u32[]{:S(2)}) %collective-permute-start.6) | collective-permute-done | bytes 131104 | tf_op jit(solution)/shard_map/ppermute | solution.py:475
  75.9 0.0 collective-permute-done.3.payload
  75.9 3.0 %shard_map.215 = (bf16[2656,128]{1,0:T(8,128)(2,1)S(1)}, bf16[100,100]{1,0:T(8,128)(2,1)}, bf16[100,2816]{1,0:T(8,128)(2,1)S(1)}) custom-call(bf16[100,2688]{1,0:T(8,128)(2,1)S(1)} %collective-permute-done.3.payload, f32[3200,128]{1,0:T(8,128)S(1)} %get-tuple-element.53.side_sketch, f32[100,100]{1,0:T(8,128)S(1)} %copy-done.9, ...), custom_call_target="tpu_custom_call" | custom-call | flops 4000000000 | bytes 4000000 | tf_op jit(solution)/shard_map/pallas_call | solution.py:446
  78.9 4.3 %collective-permute-start.7 = (bf16[100,2816]{1,0:T(8,128)(2,1)S(1)}, bf16[100,2816]{1,0:T(8,128)(2,1)S(1)}, u32[]{:S(2)}, u32[]{:S(2)}) collective-permute-start(bf16[100,2816]{1,0:T(8,128)(2,1)S(1)} %get-tuple-element.54), channel_id=1, source_target_pairs={{0,7},{1,0},{2,1},{3,2},{4,3},{5,4},{6,5},{7,6},{8,15},{9,8},{10,9... | collective-permute-start | bytes 1689608 | tf_op jit(solution)/shard_map/ppermute | solution.py:465
  83.1 0.0 collective-permute-done.8.frame
  83.1 25.6 %shard_map.218 = bf16[100,2500]{1,0:T(8,128)(2,1)} custom-call(bf16[2656,128]{1,0:T(8,128)(2,1)S(1)} %get-tuple-element.60.rows_ref, bf16[128,3200]{1,0:T(8,128)(2,1)S(1)} %get-tuple-element.61.edge, bf16[640,640]{1,0:T(8,128)(2,1)S(1)} %shard_map.217.tensor, bf16[100,2688]{1,0:T(8,128)(2,1)S(1)} %collective-permute-done.8.frame), custom_call_target="tpu_custom_call" | custom-call | flops 24999999488 | bytes 25000000 | tf_op jit(solution)/shard_map/pallas_call | solution.py:446
  108.7 0.0 collective-permute-done.7.payload
  108.7 0.9 shard_map.216
  (12 shorter events, 0.0 us)
Async XLA Ops:
  0.6 8.1 %copy-start = (bf16[100,2500]{1,0:T(8,128)(2,1)S(1)}, bf16[100,2500]{1,0:T(8,128)(2,1)}, u32[]{:S(2)}) copy-start(bf16[100,2500]{1,0:T(8,128)(2,1)} %t1.3) | copy-start | bytes 1500004
  0.6 8.1 %copy-start.10 = (bf16[100,100]{1,0:T(8,128)(2,1)S(1)}, bf16[100,100]{1,0:T(8,128)(2,1)}, u32[]{:S(2)}) copy-start(bf16[100,100]{1,0:T(8,128)(2,1)} %c2.1) | copy-start | bytes 60004
  0.7 8.1 %copy-start.1 = (bf16[100,2500]{1,0:T(8,128)(2,1)S(1)}, bf16[100,2500]{1,0:T(8,128)(2,1)}, u32[]{:S(2)}) copy-start(bf16[100,2500]{1,0:T(8,128)(2,1)} %t2.1) | copy-start | bytes 1500004
  0.7 8.1 %copy-start.2 = (bf16[100,2500]{1,0:T(8,128)(2,1)S(1)}, bf16[100,2500]{1,0:T(8,128)(2,1)}, u32[]{:S(2)}) copy-start(bf16[100,2500]{1,0:T(8,128)(2,1)} %t4.1) | copy-start | bytes 1500004
  0.7 8.1 %copy-start.7 = (f32[100,100]{1,0:T(8,128)S(1)}, f32[100,100]{1,0:T(8,128)}, u32[]{:S(2)}) copy-start(f32[100,100]{1,0:T(8,128)} %below.3) | copy-start | bytes 120004
  0.7 8.1 %copy-start.6 = (f32[100,100]{1,0:T(8,128)S(1)}, f32[100,100]{1,0:T(8,128)}, u32[]{:S(2)}) copy-start(f32[100,100]{1,0:T(8,128)} %above.3) | copy-start | bytes 120004
  0.7 8.1 %copy-start.8 = (f32[100,100]{1,0:T(8,128)S(1)}, f32[100,100]{1,0:T(8,128)}, u32[]{:S(2)}) copy-start(f32[100,100]{1,0:T(8,128)} %right.3) | copy-start | bytes 120004
  4.2 20.4 %collective-permute-start = (bf16[100,2560]{1,0:T(8,128)(2,1)}, bf16[100,2560]{1,0:T(8,128)(2,1)S(1)}, u32[]{:S(2)}, u32[]{:S(2)}) collective-permute-start(bf16[100,2560]{1,0:T(8,128)(2,1)} %get-tuple-element.35.upper_packed.after), channel_id=1, source_target_pairs={{0,7},{1,0},{2,1},{3,2},{4,3},{5,4},{6,5},{7,6},{8,15},{9,8},{10,9... | collective-permute-start | bytes 1536008 | tf_op jit(solution)/shard_map/ppermute | solution.py:465
  8.7 16.0 %collective-permute-start.1 = (bf16[100,2560]{1,0:T(8,128)(2,1)}, bf16[100,2560]{1,0:T(8,128)(2,1)S(1)}, u32[]{:S(2)}, u32[]{:S(2)}) collective-permute-start(bf16[100,2560]{1,0:T(8,128)(2,1)} %get-tuple-element.36.lower_packed), channel_id=1, source_target_pairs={{0,1},{1,2},{2,3},{3,4},{4,5},{5,6},{6,7},{7,0},{8,9},{9,10},{10,1... | collective-permute-start | bytes 1536008 | tf_op jit(solution)/shard_map/ppermute | solution.py:465
  8.7 15.9 %collective-permute-start.2 = (s32[1]{0:T(128)}, s32[1]{0:T(128)}, u32[]{:S(2)}, u32[]{:S(2)}) collective-permute-start(s32[1]{0:T(128)} %bitcast), channel_id=1, source_target_pairs={{0,1},{1,2},{2,3},{3,4},{4,5},{5,6},{6,7},{7,0},{8,9},{9,10},{10,1... | collective-permute-start | bytes 20 | tf_op jit(solution)/shard_map/ppermute | solution.py:465
  8.8 1.0 copy-start.3
  9.8 1.0 copy-start.4
  12.9 1.2 %copy-start.15 = (f32[3200,128]{1,0:T(8,128)}, f32[3200,128]{1,0:T(8,128)S(1)}, u32[]{:S(2)}) copy-start(f32[3200,128]{1,0:T(8,128)S(1)} %get-tuple-element.40.lower_sketch) | copy-start | bytes 4915204
  14.0 0.9 copy-start.17
  14.9 0.9 copy-start.19
  15.8 0.9 copy-start.21
  16.7 54.7 %collective-permute-start.4 = (bf16[100,2560]{1,0:T(8,128)(2,1)S(1)}, bf16[100,2560]{1,0:T(8,128)(2,1)S(1)}, u32[]{:S(2)}, u32[]{:S(2)}) collective-permute-start(bf16[100,2560]{1,0:T(8,128)(2,1)S(1)} %get-tuple-element.46), channel_id=1, source_target_pairs={{0,9},{1,10},{2,11},{3,12},{4,13},{5,14},{6,15},{7,8},{8,17},{9,18... | collective-permute-start | bytes 1536008 | tf_op jit(solution)/shard_map/ppermute | solution.py:475
  17.0 54.4 %collective-permute-start.5 = (bf16[100,2500]{1,0:T(8,128)(2,1)S(1)}, bf16[100,2500]{1,0:T(8,128)(2,1)S(1)}, u32[]{:S(2)}, u32[]{:S(2)}) collective-permute-start(bf16[100,2500]{1,0:T(8,128)(2,1)S(1)} %get-tuple-element.47), channel_id=1, source_target_pairs={{0,1},{1,2},{2,3},{3,4},{4,5},{5,6},{6,7},{7,0},{8,9},{9,10},{10,1... | collective-permute-start | bytes 1500008 | tf_op jit(solution)/shard_map/ppermute | solution.py:465
  18.6 3.8 %copy-start.5 = (bf16[100,2560]{1,0:T(8,128)(2,1)S(1)}, bf16[100,2560]{1,0:T(8,128)(2,1)}, u32[]{:S(2)}) copy-start(bf16[100,2560]{1,0:T(8,128)(2,1)} %get-tuple-element.35.upper_packed.after) | copy-start | bytes 1536004
  18.6 3.8 %copy-start.12 = (s32[640,1]{1,0:T(8,128)S(1)}, s32[640,1]{1,0:T(8,128)}, u32[]{:S(2)}) copy-start(s32[640,1]{1,0:T(8,128)} %constant.8.clone.rows) | copy-start | bytes 7684
  18.6 3.8 %copy-start.14 = (s32[1,640]{1,0:T(1,128)S(1)}, s32[1,640]{1,0:T(1,128)}, u32[]{:S(2)}) copy-start(s32[1,640]{1,0:T(1,128)} %constant.9.clone.columns) | copy-start | bytes 7684
  22.4 2.3 %copy-start.16 = (f32[3200,128]{1,0:T(8,128)S(1)}, f32[3200,128]{1,0:T(8,128)}, u32[]{:S(2)}) copy-start(f32[3200,128]{1,0:T(8,128)} %copy-done.15) | copy-start | bytes 4915204
  22.4 2.3 %copy-start.20 = (bf16[3200,128]{1,0:T(8,128)(2,1)S(1)}, bf16[3200,128]{1,0:T(8,128)(2,1)}, u32[]{:S(2)}) copy-start(bf16[3200,128]{1,0:T(8,128)(2,1)} %copy-done.19) | copy-start | bytes 2457604
  22.4 2.3 %copy-start.22 = (bf16[3200,128]{1,0:T(8,128)(2,1)S(1)}, bf16[3200,128]{1,0:T(8,128)(2,1)}, u32[]{:S(2)}) copy-start(bf16[3200,128]{1,0:T(8,128)(2,1)} %copy-done.21) | copy-start | bytes 2457604
  24.7 8.3 %copy-start.18 = (bf16[128,3200]{1,0:T(8,128)(2,1)S(1)}, bf16[128,3200]{1,0:T(8,128)(2,1)}, u32[]{:S(2)}) copy-start(bf16[128,3200]{1,0:T(8,128)(2,1)} %copy-done.17) | copy-start | bytes 2457604
  33.0 27.0 %copy-start.9 = (f32[100,100]{1,0:T(8,128)S(1)}, f32[100,100]{1,0:T(8,128)}, u32[]{:S(2)}) copy-start(f32[100,100]{1,0:T(8,128)} %left.3) | copy-start | bytes 120004
  58.2 17.7 %collective-permute-start.3 = (bf16[100,2688]{1,0:T(8,128)(2,1)S(1)}, bf16[100,2688]{1,0:T(8,128)(2,1)S(1)}, u32[]{:S(2)}, u32[]{:S(2)}) collective-permute-start(bf16[100,2688]{1,0:T(8,128)(2,1)S(1)} %get-tuple-element.45), channel_id=1, source_target_pairs={{0,9},{1,10},{2,11},{3,12},{4,13},{5,14},{6,15},{7,8},{8,17},{9,18... | collective-permute-start | bytes 1612808 | tf_op jit(solution)/shard_map/ppermute | solution.py:475
  60.0 8.3 %copy-start.11 = (s32[640,1]{1,0:T(8,128)S(1)}, s32[640,1]{1,0:T(8,128)}, u32[]{:S(2)}) copy-start(s32[640,1]{1,0:T(8,128)} %constant.10.clone.rows) | copy-start | bytes 7684
  60.0 8.3 %copy-start.13 = (s32[1,640]{1,0:T(1,128)S(1)}, s32[1,640]{1,0:T(1,128)}, u32[]{:S(2)}) copy-start(s32[1,640]{1,0:T(1,128)} %constant.11.clone.columns) | copy-start | bytes 7684
  65.6 10.2 %collective-permute-start.6 = (f32[128,256]{1,0:T(8,128)S(1)}, f32[128,256]{1,0:T(8,128)S(1)}, u32[]{:S(2)}, u32[]{:S(2)}) collective-permute-start(f32[128,256]{1,0:T(8,128)S(1)} %get-tuple-element.52.after), channel_id=1, source_target_pairs={{0,9},{1,10},{2,11},{3,12},{4,13},{5,14},{6,15},{7,8},{8,17},{9,18... | collective-permute-start | bytes 393224 | tf_op jit(solution)/shard_map/ppermute | solution.py:475
  67.6 15.5 %collective-permute-start.8 = (bf16[100,2688]{1,0:T(8,128)(2,1)S(1)}, bf16[100,2688]{1,0:T(8,128)(2,1)S(1)}, u32[]{:S(2)}, u32[]{:S(2)}) collective-permute-start(bf16[100,2688]{1,0:T(8,128)(2,1)S(1)} %get-tuple-element.55), channel_id=1, source_target_pairs={{0,1},{1,2},{2,3},{3,4},{4,5},{5,6},{6,7},{7,0},{8,9},{9,10},{10,1... | collective-permute-start | bytes 1612808 | tf_op jit(solution)/shard_map/ppermute | solution.py:465
  78.9 29.9 %collective-permute-start.7 = (bf16[100,2816]{1,0:T(8,128)(2,1)S(1)}, bf16[100,2816]{1,0:T(8,128)(2,1)S(1)}, u32[]{:S(2)}, u32[]{:S(2)}) collective-permute-start(bf16[100,2816]{1,0:T(8,128)(2,1)S(1)} %get-tuple-element.54), channel_id=1, source_target_pairs={{0,7},{1,0},{2,1},{3,2},{4,3},{5,4},{6,5},{7,6},{8,15},{9,8},{10,9... | collective-permute-start | bytes 1689608 | tf_op jit(solution)/shard_map/ppermute | solution.py:465
where the time goes:
time: 110 us
  Pallas kernels  80.1 us (73%)
  starting transfers between devices  14.5 us (13%)
  local copies, waits for them, and re-layouts  9.74 us (9%)
  waiting for transfers between devices  3.65 us (3%)
  between operations  1.63 us (1%)
    pallas_call x9, Pallas kernels, call(): pl.pallas_call(kernel, grid=(1,), in_specs=specs, out_specs=[block_of(out...  74.8 us
    ppermute x6, starting transfers between devices, shift(): return lax.ppermute(value, axis, pairs)  10.4 us
    unnamed x47, local copies, waits for them, and re-layouts  9.74 us
    pallas_call x2, Pallas kernels, arrange(): pl.pallas_call(arrange_kernel, in_specs=[pl.BlockSpec(memory_space=pltpu....  5.28 us
    ppermute x3, starting transfers between devices, shift_both(): return lax.ppermute(value, ('col', 'row'), pairs)  4.06 us
    ppermute x3, waiting for transfers between devices, shift_both(): return lax.ppermute(value, ('col', 'row'), pairs)  3.64 us
  transfers between devices with their start and end apart: 9, of which 1 were waited for; matrix products, arithmetic and copies ran while one was open for 3% of the time, Pallas kernels for 69%

commit v1 on v0

--- a/solution.py
+++ b/solution.py
@@ -157,15 +157,25 @@
     return [jnp.where(keep, jnp.concatenate(parts + [tail], 0), 0.0) for parts in done]
 
 
-def gram_and(values, other):
-    both = product(values, jnp.concatenate([values, other], 1), TN)
-    return both[:, :LANES], both[:, LANES:]
-
-
-def frame_from(values, inverse):
-    high, low = halves(inverse)
-    both = jnp.concatenate([values, values], 1)
-    return product(both, jnp.concatenate([high, low], 1), NT)
+def store_halves(values, high, low):
+    high[...], low[...] = halves(values)
+
+
+def gram_of(high, low):
+    both = product(high[...], jnp.concatenate([high[...], low[...]], 1), TN)
+    mixed = both[:, LANES:]
+    return both[:, :LANES] + mixed + mixed.T
+
+
+def overlap(other, high, low):
+    both = product(other, jnp.concatenate([high[...], low[...]], 1), TN)
+    return both[:, :LANES] + both[:, LANES:]
+
+
+def frame_from(high, low, inverse):
+    inverse_high, inverse_low = halves(inverse)
+    left = jnp.concatenate([high[...], low[...], high[...]], 1)
+    return product(left, jnp.concatenate([inverse_high, inverse_high, inverse_low], 1), NT)
 
 
 def scaled_corner(values, bond):
@@ -182,13 +192,14 @@
         stack[k * LANES : (k + 1) * LANES, :] = tile.astype(stack.dtype)
 
 
-def store_frame_rows(sketch, inverse, rows_ref, plain, tail, site):
+def store_frame_rows(high, low, inverse, rows_ref, plain, tail, site):
     main = site - 1
     bond_rows = plain.shape[0] // main
-    both = jnp.concatenate(halves(inverse), 1)[:bond_rows]
+    inverse_high, inverse_low = halves(inverse)
+    left = jnp.concatenate([inverse_high, inverse_high, inverse_low], 1)[:bond_rows]
     for k in range(site):
-        piece = sketch[k * LANES : (k + 1) * LANES, :]
-        tile = product(both, jnp.concatenate([piece, piece], 1), NT)
+        rows = slice(k * LANES, (k + 1) * LANES)
+        tile = product(left, jnp.concatenate([high[rows, :], low[rows, :], high[rows, :]], 1), NT)
         if k < main:
             plain[pl.ds(k, bond_rows, stride=main), :] = tile
         else:
@@ -223,35 +234,34 @@
 
 def vertical_kernel(
     bond, site, upper_packed, lower_packed, above, below, upper, upper_sketch, lower, lower_sketch,
-    pattern, rows_ref, frame_out, corner_top, corner_bottom, pattern_out, stack, over, under, plain, tail,
+    rows_ref, frame_out, corner_top, corner_bottom, stack, over, over_low, under, under_low, plain, tail,
 ):
-    pattern_out[0] = pattern[0]
     fill(stack, unpack(upper_packed, bond, site))
-    under[...] = (lower_sketch[...] + sketched(stack[...], square_of(above, bond))).astype(BF16)
+    store_halves(lower_sketch[...] + sketched(stack[...], square_of(above, bond)), under, under_low)
     fill(stack, unpack(lower_packed, bond, site))
-    over[...] = (upper_sketch[...] + sketched(stack[...], square_of(below, bond))).astype(BF16)
-    gram_over, mixed_over = gram_and(over[...], upper[...])
-    gram_under, mixed_under = gram_and(under[...], lower[...])
-    inverse_over, inverse_under = inverse_factors([gram_over, gram_under], bond)
-    store_frame_rows(over, inverse_over, rows_ref, plain, tail, site)
-    frame_out[...] = frame_from(under[...], inverse_under).astype(BF16)
-    corner_top[...] = scaled_corner(product_split(inverse_over, mixed_over), bond)
-    corner_bottom[...] = scaled_corner(product_split(inverse_under, mixed_under), bond)
+    store_halves(upper_sketch[...] + sketched(stack[...], square_of(below, bond)), over, over_low)
+    grams = [gram_of(over, over_low), gram_of(under, under_low)]
+    mixed_over = overlap(upper[...], over, over_low)
+    mixed_under = overlap(lower[...], under, under_low)
+    inverse_over, inverse_under = inverse_factors(grams, bond)
+    store_frame_rows(over, over_low, inverse_over, rows_ref, plain, tail, site)
+    frame_out[...] = frame_from(under, under_low, inverse_under).astype(BF16)
+    corner_top[...] = scaled_corner(product_split(inverse_over, mixed_over, NT), bond)
+    corner_bottom[...] = scaled_corner(product_split(inverse_under, mixed_under, NT), bond)
 
 
 def horizontal_kernel(
-    bond, site, c1, c4, edge, left, side, side_sketch, inverse_ref, frame_out, half, total
+    bond, site, c1, edge, left, side, side_sketch, inverse_ref, frame_out, half, total, total_low
 ):
     corner = square_of(c1, bond).T.astype(BF16)
     fill(half, half_tiles(corner, [edge[:, k * LANES : (k + 1) * LANES] for k in range(site)]))
-    total[...] = (side_sketch[...] + sketched(half[...], square_of(left, bond))).astype(BF16)
-    gram, mixed = gram_and(total[...], side[...])
-    (inverse,) = inverse_factors([gram], bond)
-    inverse_ref[:, :LANES] = inverse
-    inverse_ref[:, LANES:] = square_of(c4, bond)
-    frame = frame_from(total[...], inverse)
+    store_halves(side_sketch[...] + sketched(half[...], square_of(left, bond)), total, total_low)
+    mixed = overlap(side[...], total, total_low)
+    (inverse,) = inverse_factors([gram_of(total, total_low)], bond)
+    inverse_ref[...] = inverse[: inverse_ref.shape[0]]
+    frame = frame_from(total, total_low, inverse)
     pack([frame[k * LANES : (k + 1) * LANES, :] for k in range(site)], frame_out, bond)
-    corner_right = scaled_corner(product_split(inverse, mixed), bond)
+    corner_right = scaled_corner(product_split(inverse, mixed, NT), bond)
     frame_out[:, frame_out.shape[1] - LANES :] = corner_right
 
 
@@ -264,18 +274,18 @@
 
 def arrive_kernel(
     bond, site, payload, side_sketch, left, inverse_ref,
-    rows_ref, corner_left, forward, half, total, plain, tail,
+    rows_ref, corner_left, forward, half, total, total_low, plain, tail,
 ):
-    start = payload.shape[1] - LANES
-    corner = square_of(payload.at[:, start:], bond).T.astype(BF16)
+    start = payload.shape[1] - 2 * LANES
+    corner = square_of(payload.at[:, start : start + LANES], bond).T.astype(BF16)
     fill(half, half_tiles(corner, spread(payload, bond, site)))
-    total[...] = (side_sketch[...] + sketched(half[...], square_of(left, bond))).astype(BF16)
-    inverse = inverse_ref[:, :LANES]
-    store_frame_rows(total, inverse, rows_ref, plain, tail, site)
-    mixed = product(half[...], total[...], TN)
+    store_halves(side_sketch[...] + sketched(half[...], square_of(left, bond)), total, total_low)
+    rest = jnp.zeros((LANES - inverse_ref.shape[0], LANES), F32)
+    inverse = jnp.concatenate([inverse_ref[...], rest], 0)
+    store_frame_rows(total, total_low, inverse, rows_ref, plain, tail, site)
+    mixed = overlap(half[...], total, total_low)
     corner_left[...] = scaled_corner(product_split(mixed, inverse, NT), bond)
-    forward[:, : payload.shape[1]] = payload[...]
-    forward[:, payload.shape[1] :] = inverse_ref[:, LANES:].astype(BF16)
+    forward[...] = payload[...]
 
 
 def finish_kernel(bond, payload, frame, left_corner, left_edge, left_bottom, top_right):
@@ -289,7 +299,7 @@
 def absorb_kernel(bond, site, first, rows_ref, edge, tensor, frame, *refs):
     mixed_even, mixed_odd, spare_even, spare_odd, pushed_even, pushed_odd, last, result = refs[-8:]
     if first:
-        corner, dense, wide = refs[:3]
+        corner, bottom, dense, wide = refs[:4]
         frame_out = frame
     else:
         dense, frame_out = refs[0], refs[1]
@@ -395,16 +405,25 @@
     if first:
         for k, tile in enumerate(tiles):
             wide[:, k * LANES : (k + 1) * LANES] = tile.astype(BF16)
-        dense[:, dense.shape[1] - LANES :] = square_of(corner, bond).astype(BF16)
-
-
-def arrange_kernel(pattern, tensors, rows, columns, after, out, tensor, semaphore):
-    copy = pltpu.make_async_copy(tensors.at[pattern[0]], tensor, semaphore)
-    copy.start()
+        start = dense.shape[1] - 2 * LANES
+        dense[:, start : start + LANES] = square_of(corner, bond).astype(BF16)
+        dense[:, start + LANES :] = square_of(bottom, bond).astype(BF16)
+
+
+def pick_kernel(pattern, tensors, out, *tiles):
+    height, count, width = tensors.shape
+    values = tensors[...].astype(F32).reshape(height * count, width)
+    for n, tile in enumerate(tiles):
+        end = min(width, (n + 1) * LANES)
+        tile[:, : end - n * LANES] = values[:, n * LANES : end]
+        rows = tile[pl.ds(pattern[0], height, stride=count), :]
+        out[:, n * LANES : end] = rows[:, : end - n * LANES].astype(BF16)
+
+
+def arrange_kernel(tensor, rows, columns, after, out):
     square = tensor.shape[0]
     pick_rows = jnp.where(index_of((rows.shape[0], square), 1) == rows[...], 1.0, 0.0).astype(BF16)
     pick_columns = jnp.where(index_of((square, columns.shape[1]), 0) == columns[...], 1.0, 0.0)
-    copy.wait()
     turned = product(pick_rows, tensor[...], NT).astype(BF16)
     out[...] = product(turned, pick_columns.astype(BF16)).astype(BF16)
 
@@ -490,31 +509,39 @@
     stack = shape_of((tall, LANES))
     stack_f32 = shape_of((tall, LANES), F32)
     corner = shape_of((bond, bond))
-    payload = shape_of((bond, -(-site * bond // LANES) * LANES + LANES))
+    payload = shape_of((bond, -(-site * bond // LANES) * LANES + 2 * LANES))
     half_bf16 = pltpu.VMEM((tall, LANES), BF16)
     frame_scratch = [pltpu.VMEM((body_rows, LANES), F32), pltpu.VMEM((tail_rows, LANES), F32)]
     rows, columns = places(site)
 
-    def arrange(which, index, after):
+    def pick(index):
+        count = tensors.shape[0]
+        return pl.pallas_call(
+            pick_kernel,
+            grid=(-(-square // LANES),),
+            in_specs=[
+                pl.BlockSpec(memory_space=pltpu.SMEM),
+                pl.BlockSpec((LANES, count, square), lambda i: (i, 0, 0)),
+            ],
+            out_specs=pl.BlockSpec((LANES, square), lambda i: (i, 0)),
+            out_shape=shape_of((square, square)),
+            scratch_shapes=[pltpu.VMEM((LANES * count, LANES), F32)] * -(-square // LANES),
+            compiler_params=pltpu.CompilerParams(vmem_limit_bytes=16 * MIB),
+            cost_estimate=cost(2),
+        )(index, tensors.transpose(1, 0, 2))
+
+    def arrange(which, tensor, after):
         height, depth = rows.shape[1], columns.shape[1]
         vmem = pl.BlockSpec(memory_space=pltpu.VMEM)
         return pl.pallas_call(
             arrange_kernel,
-            in_specs=[
-                pl.BlockSpec(memory_space=pltpu.SMEM),
-                pl.BlockSpec(memory_space=pltpu.HBM),
-                vmem,
-                vmem,
-                pl.BlockSpec(memory_space=pl.ANY),
-            ],
+            in_specs=[vmem, vmem, vmem, pl.BlockSpec(memory_space=pl.ANY)],
             out_specs=vmem,
             out_shape=shape_of((height, depth)),
-            scratch_shapes=[pltpu.VMEM((square, square), BF16), pltpu.SemaphoreType.DMA],
             compiler_params=pltpu.CompilerParams(vmem_limit_bytes=16 * MIB),
-            cost_estimate=cost(3),
+            cost_estimate=cost(2),
         )(
-            index,
-            tensors,
+            tensor,
             rows[which].reshape(height, 1),
             columns[which].reshape(1, depth),
             after,
@@ -546,9 +573,8 @@
     )
     upper_next = shift(upper_packed, "row", -1)
     lower_back = shift(lower_packed, "row", 1)
-    pattern = pattern.reshape(1)
-    pattern_back = shift(pattern, "row", 1)
-    tensor_left = arrange(0, pattern, upper_packed)
+    tensor = pick(pattern.reshape(1))
+    tensor_left = arrange(0, tensor, upper_packed)
     prepared = call(
         functools.partial(prepare_kernel, bond, site),
         (c2, t2, t4, t1, above, below, right, upper_packed, lower_packed),
@@ -560,28 +586,28 @@
     t4_wide, t1_held, upper, upper_sketch, lower, lower_sketch, side_packed, side, side_sketch = prepared
     t1_back = shift(t1_held, "row", 1)
     side_back = shift_both(side_packed, 1, 1)
-    rows_left, frame_below, corner_top, corner_bottom, pattern_held = call(
+    tensor_back = shift(tensor, "row", 1)
+    rows_left, frame_below, corner_top, corner_bottom = call(
         functools.partial(vertical_kernel, bond, site),
-        (upper_next, lower_back, above, below, upper, upper_sketch, lower, lower_sketch)
-        + (pattern_back,),
-        [frame_rows, stack, corner, corner, shape_of((1,), jnp.int32)],
-        [half_bf16, half_bf16, half_bf16] + frame_scratch,
+        (upper_next, lower_back, above, below, upper, upper_sketch, lower, lower_sketch),
+        [frame_rows, stack, corner, corner],
+        [half_bf16] * 5 + frame_scratch,
         20,
         8,
     )
-    left_new, edge_wide = absorb(True, rows_left, t4_wide, tensor_left, frame_below, corner_top)
+    left_new, edge_wide = absorb(True, rows_left, t4_wide, tensor_left, frame_below, corner_top, corner_bottom)
     left_back = shift_both(left_new, 1, 1)
     inverse, frame_right = call(
         functools.partial(horizontal_kernel, bond, site),
-        (corner_top, corner_bottom, edge_wide, left, side, side_sketch),
-        [shape_of((LANES, 2 * LANES), F32), shape_of((bond, packed.shape[1] + LANES))],
-        [half_bf16, half_bf16],
+        (corner_top, edge_wide, left, side, side_sketch),
+        [shape_of((-(-bond // HALF_TILE) * HALF_TILE, LANES), F32), shape_of((bond, packed.shape[1] + LANES))],
+        [half_bf16] * 3,
         16,
         5,
     )
     inverse_back = shift_both(inverse, 1, 1)
     frame_back = shift(frame_right, "row", 1)
-    tensor_top = arrange(1, pattern_held, inverse)
+    tensor_top = arrange(1, tensor_back, inverse)
     early_sketch, t1_wide = call(
         functools.partial(early_kernel, bond, site),
         (side_back, right, t1_back, inverse),
@@ -594,8 +620,8 @@
     rows_top, top_left, forward = call(
         functools.partial(arrive_kernel, bond, site),
         (left_back, early_sketch, left, inverse_back),
-        [frame_rows, corner, shape_of((bond, payload.shape[1] + LANES))],
-        [half_bf16, half_bf16] + frame_scratch,
+        [frame_rows, corner, payload],
+        [half_bf16] * 3 + frame_scratch,
         16,
         4,
     )

time: 110 us -> 103 us (0.936)
  local copies, waits for them, and re-layouts: 9.74 us -> 2.55 us
  waiting for transfers between devices: 3.65 us -> 8.65 us
  starting transfers between devices: 14.5 us -> 10.3 us
    unnamed x47 -> x30, local copies, waits for them, and re-layouts: 9.74 us -> 2.55 us
    ppermute x3, starting transfers between devices: 4.06 us -> 0.62 us  [shift_both(): return lax.ppermute(value, ('col', 'row'), pairs)]
    ppermute x6, waiting for transfers between devices: 0.02 us -> 3.27 us  [shift(): return lax.ppermute(value, axis, pairs)]
    ppermute x3, waiting for transfers between devices: 3.64 us -> 5.38 us  [shift_both(): return lax.ppermute(value, ('col', 'row'), pairs)]
    pallas_call x2 -> x3, Pallas kernels: 5.28 us -> 5.06 us  [the longest x2 3.4 us: arrange(): pl.pallas_call(arrange_kernel, in_specs=[vmem, vmem, vmem, pl.BlockSpec(m...]
  transfers between devices with their start and end apart: 9 -> 9, of which waited for: 1 -> 3; matrix products, arithmetic and copies ran while one was open for 3% -> 0% of each run, Pallas kernels for 69% -> 73%
where the time goes in v1:
time: 103 us
  Pallas kernels  80 us (78%)
  starting transfers between devices  10.3 us (10%)
  waiting for transfers between devices  8.65 us (8%)
  local copies, waits for them, and re-layouts  2.55 us (2%)
  between operations  1.54 us (1%)
    pallas_call x9, Pallas kernels, call(): pl.pallas_call(kernel, grid=(1,), in_specs=specs, out_specs=[block_of(out...  74.9 us
    ppermute x6, starting transfers between devices, shift(): return lax.ppermute(value, axis, pairs)  9.71 us
    ppermute x3, waiting for transfers between devices, shift_both(): return lax.ppermute(value, ('col', 'row'), pairs)  5.38 us
    pallas_call x2, Pallas kernels, arrange(): pl.pallas_call(arrange_kernel, in_specs=[vmem, vmem, vmem, pl.BlockSpec(m...  3.4 us
    ppermute x6, waiting for transfers between devices, shift(): return lax.ppermute(value, axis, pairs)  3.27 us
    unnamed x30, local copies, waits for them, and re-layouts  2.55 us
  transfers between devices with their start and end apart: 9, of which 3 were waited for; matrix products, arithmetic and copies ran while one was open for 0% of the time, Pallas kernels for 73%

profile of v1, /device:TPU:0, one launch (start us, length us, event | category | flops | bytes accessed | tf_op | source)
XLA Modules:
  0.0 103.0 jit_solution(435420864356814336)
XLA Ops:
  0.6 0.0 copy-start.1
  0.6 0.0 copy-start.10
  0.7 0.0 copy-start.2
  0.7 0.0 copy-start.3
  0.7 0.0 copy-start.7
  0.7 0.0 copy-start.6
  0.7 0.0 copy-start.8
  0.7 3.5 %shard_map.208 = (bf16[100,2560]{1,0:T(8,128)(2,1)}, bf16[100,2560]{1,0:T(8,128)(2,1)}) custom-call(bf16[100,100]{1,0:T(8,128)(2,1)} %c1.1, bf16[100,2500]{1,0:T(8,128)(2,1)} %t1.3, bf16[100,100]{1,0:T(8,128)(2,1)} %c4.1, bf16[100,2500]{1,0:T(8,128)(2,1)} %t3.1), custom_call_target="tpu_custom_call" | custom-call | flops 2000000000 | bytes 2000000 | tf_op jit(solution)/shard_map/pallas_call | solution.py:465
  4.2 4.5 %collective-permute-start = (bf16[100,2560]{1,0:T(8,128)(2,1)}, bf16[100,2560]{1,0:T(8,128)(2,1)S(1)}, u32[]{:S(2)}, u32[]{:S(2)}) collective-permute-start(bf16[100,2560]{1,0:T(8,128)(2,1)} %get-tuple-element.34.upper_packed.after), channel_id=1, source_target_pairs={{0,7},{1,0},{2,1},{3,2},{4,3},{5,4},{6,5},{7,6},{8,15},{9,8},{10,9... | collective-permute-start | bytes 1536008 | tf_op jit(solution)/shard_map/ppermute | solution.py:484
  8.7 0.0 copy-start
  8.7 0.0 collective-permute-start.1
  8.7 0.0 copy-done.1
  8.7 0.0 copy-done.10
  8.7 0.0 copy-done.2
  8.7 0.0 copy-done.3
  8.7 0.0 copy-done.7
  8.7 0.0 copy-done.6
  8.7 0.0 copy-done.8
  8.7 0.0 copy-start.4
  8.8 1.2 %copy-done.4 = bf16[100,2560]{1,0:T(8,128)(2,1)S(1)} copy-done((bf16[100,2560]{1,0:T(8,128)(2,1)S(1)}, bf16[100,2560]{1,0:T(8,128)(2,1)}, u32[]{:S(2)}) %copy-start.4) | copy-done | bytes 512024
  9.9 0.0 copy-start.5
  9.9 1.3 %copy-done.5 = bf16[100,2560]{1,0:T(8,128)(2,1)S(1)} copy-done((bf16[100,2560]{1,0:T(8,128)(2,1)S(1)}, bf16[100,2560]{1,0:T(8,128)(2,1)}, u32[]{:S(2)}) %copy-start.5) | copy-done | bytes 512024
  11.2 2.0 %shard_map.209 = (bf16[128,3200]{1,0:T(8,128)(2,1)S(1)}, bf16[100,2500]{1,0:T(8,128)(2,1)S(1)}, bf16[3200,128]{1,0:T(8,128)(2,1)S(1)}, f32[3200,128]{1,0:T(8,128...) custom-call(bf16[100,100]{1,0:T(8,128)(2,1)S(1)} %copy-done.10, ...), custom_call_target="tpu_custom_call" | custom-call | flops 2000000000 | bytes 2000000 | tf_op jit(solution)/shard_map/pallas_call | solution.py:465
  13.2 0.1 collective-permute-start.3
  13.3 0.1 collective-permute-start.4
  14.0 0.0 copy-done
  14.0 0.0 copy-start.12
  14.0 0.0 copy-start.14
  14.1 1.7 %shard_map.211.tensor = bf16[625,625]{1,0:T(8,128)(2,1)S(1)} custom-call(s32[1]{0:T(128)} %bitcast.2.pattern, bf16[625,8,625]{2,1,0:T(8,128)(2,1)S(1)} %bitcast.3), custom_call_target="tpu_custom_call" | custom-call | flops 2000000000 | bytes 2000000 | tf_op jit(solution)/shard_map/pallas_call | solution.py:519
  15.7 1.7 %collective-permute-start.8 = (bf16[625,625]{1,0:T(8,128)(2,1)S(1)}, bf16[625,625]{1,0:T(8,128)(2,1)S(1)}, u32[]{:S(2)}, u32[]{:S(2)}) collective-permute-start(bf16[625,625]{1,0:T(8,128)(2,1)S(1)} %shard_map.211.tensor), channel_id=1, source_target_pairs={{0,1},{1,2},{2,3},{3,4},{4,5},{5,6},{6,7},{7,0},{8,9},{9,10},{10,1... | collective-permute-start | bytes 2343758 | tf_op jit(solution)/shard_map/ppermute | solution.py:484
  17.4 0.0 copy-done.12
  17.4 0.0 copy-done.14
  17.4 1.7 %shard_map.212.tensor = bf16[640,640]{1,0:T(8,128)(2,1)S(1)} custom-call(bf16[625,625]{1,0:T(8,128)(2,1)S(1)} %shard_map.211.tensor, s32[640,1]{1,0:T(8,128)S(1)} %copy-done.12, s32[1,640]{1,0:T(1,128)S(1)} %copy-done.14, bf16[100,2560]{1,0:T(8,128)(2,1)S(1)} %copy-done.5), custom_call_target="tpu_custom_call" | custom-call | flops 2000000000 | bytes 2000000 | tf_op jit(solution)/shard_map/pallas_call | solution.py:536
  19.1 2.4 %collective-permute-done.upper_packed = bf16[100,2560]{1,0:T(8,128)(2,1)S(1)} collective-permute-done((bf16[100,2560]{1,0:T(8,128)(2,1)}, bf16[100,2560]{1,0:T(8,128)(2,1)S(1)}, u32[]{:S(2)}, u32[]{:S(2)}) %collective-permute-start) | collective-permute-done | bytes 512032 | tf_op jit(solution)/shard_map/ppermute | solution.py:484
  21.6 0.8 collective-permute-done.1.lower_packed
  22.4 7.9 %shard_map.210 = (bf16[2656,128]{1,0:T(8,128)(2,1)S(1)}, bf16[3200,128]{1,0:T(8,128)(2,1)S(1)}, bf16[100,100]{1,0:T(8,128)(2,1)S(1)}, bf16[100,100]{1,0:T(8,128)(2,1)S(1)}) custom-call(bf16[100,2560]{1,0:T(8,128)(2,1)S(1)} %collective-permute-done.upper_packed, bf16[100,2560]{1,0:T(8,128)(2,1)S(1)} %collective-permute-done.1.lower_packed, ...), custom_call_target="tpu_custom_call" | custom-call | flops 8000000000 | bytes 8000000 | tf_op jit(solution)/shard_map/pallas_call | solution.py:465
  30.4 0.0 copy-start.9
  30.4 24.9 %shard_map.213 = (bf16[100,2816]{1,0:T(8,128)(2,1)S(1)}, bf16[128,3200]{1,0:T(8,128)(2,1)S(1)}) custom-call(bf16[2656,128]{1,0:T(8,128)(2,1)S(1)} %get-tuple-element.40.rows_ref, bf16[128,3200]{1,0:T(8,128)(2,1)S(1)} %get-tuple-element.41.edge, bf16[640,640]{1,0:T(8,128)(2,1)S(1)} %shard_map.212.tensor, bf16[3200,128]{1,0:T(8,128)(2,1)S(1)} %get-tuple-element.42.frame, ...), custom_call_target="tpu_custom_call" | custom-call | flops 24999999488 | bytes 25000000 | tf_op jit(solution)/shard_map/pallas_call | solution.py:465
  55.3 0.1 collective-permute-start.2
  55.4 0.0 copy-done.9
  55.4 6.2 %shard_map.214 = (f32[112,128]{1,0:T(8,128)S(1)}, bf16[100,2688]{1,0:T(8,128)(2,1)S(1)}) custom-call(bf16[100,100]{1,0:T(8,128)(2,1)S(1)} %get-tuple-element.43.refs_0_.c1, bf16[128,3200]{1,0:T(8,128)(2,1)S(1)} %get-tuple-element.48.edge, f32[100,100]{1,0:T(8,128)S(1)} %copy-done.9, bf16[3200,128]{1,0:T(8,128)(2,1)S(1)} %get-tuple-element.49.side, ...), custom_call_target="tpu_custom_call" | custom-call | flops 5000000000 | bytes 5000000 | tf_op jit(solution)/shard_map/pallas_call | solution.py:465
  61.5 0.5 collective-permute-start.5
  62.0 0.0 collective-permute-done.4.t1
  62.0 0.0 copy-start.11
  62.1 0.0 copy-start.13
  62.1 0.2 collective-permute-start.7
  62.3 0.0 collective-permute-done.3.side_packed
  62.3 0.8 shard_map.215
  63.1 0.0 collective-permute-done.8.tensor
  63.1 0.0 copy-done.11
  63.1 0.0 copy-done.13
  63.1 1.7 %shard_map.218.tensor = bf16[640,640]{1,0:T(8,128)(2,1)S(1)} custom-call(bf16[625,625]{1,0:T(8,128)(2,1)S(1)} %collective-permute-done.8.tensor, s32[640,1]{1,0:T(8,128)S(1)} %copy-done.11, s32[1,640]{1,0:T(1,128)S(1)} %copy-done.13, f32[112,128]{1,0:T(8,128)S(1)} %get-tuple-element.51.after), custom_call_target="tpu_custom_call" | custom-call | flops 2000000000 | bytes 2000000 | tf_op jit(solution)/shard_map/pallas_call | solution.py:536
  64.8 5.4 %collective-permute-done.5.inverse_ref = f32[112,128]{1,0:T(8,128)S(1)} collective-permute-done((f32[112,128]{1,0:T(8,128)S(1)}, f32[112,128]{1,0:T(8,128)S(1)}, u32[]{:S(2)}, u32[]{:S(2)}) %collective-permute-start.5) | collective-permute-done | bytes 57376 | tf_op jit(solution)/shard_map/ppermute | solution.py:494
  70.2 0.0 collective-permute-done.2.payload
  70.2 3.1 %shard_map.216 = (bf16[2656,128]{1,0:T(8,128)(2,1)S(1)}, bf16[100,100]{1,0:T(8,128)(2,1)}, bf16[100,2816]{1,0:T(8,128)(2,1)S(1)}) custom-call(bf16[100,2816]{1,0:T(8,128)(2,1)S(1)} %collective-permute-done.2.payload, f32[3200,128]{1,0:T(8,128)S(1)} %get-tuple-element.52.side_sketch, f32[100,100]{1,0:T(8,128)S(1)} %copy-done.9, ...), custom_call_target="tpu_custom_call" | custom-call | flops 4000000000 | bytes 4000000 | tf_op jit(solution)/shard_map/pallas_call | solution.py:465
  73.3 3.2 %collective-permute-start.6 = (bf16[100,2816]{1,0:T(8,128)(2,1)S(1)}, bf16[100,2816]{1,0:T(8,128)(2,1)S(1)}, u32[]{:S(2)}, u32[]{:S(2)}) collective-permute-start(bf16[100,2816]{1,0:T(8,128)(2,1)S(1)} %get-tuple-element.53), channel_id=1, source_target_pairs={{0,7},{1,0},{2,1},{3,2},{4,3},{5,4},{6,5},{7,6},{8,15},{9,8},{10,9... | collective-permute-start | bytes 1689608 | tf_op jit(solution)/shard_map/ppermute | solution.py:484
  76.6 0.0 collective-permute-done.7.frame
  76.6 25.6 %shard_map.219 = bf16[100,2500]{1,0:T(8,128)(2,1)} custom-call(bf16[2656,128]{1,0:T(8,128)(2,1)S(1)} %get-tuple-element.59.rows_ref, bf16[128,3200]{1,0:T(8,128)(2,1)S(1)} %get-tuple-element.60.edge, bf16[640,640]{1,0:T(8,128)(2,1)S(1)} %shard_map.218.tensor, bf16[100,2688]{1,0:T(8,128)(2,1)S(1)} %collective-permute-done.7.frame), custom_call_target="tpu_custom_call" | custom-call | flops 24999999488 | bytes 25000000 | tf_op jit(solution)/shard_map/pallas_call | solution.py:465
  102.2 0.0 collective-permute-done.6.payload
  102.2 0.9 shard_map.217
Async XLA Ops:
  0.6 8.1 %copy-start.1 = (bf16[100,2500]{1,0:T(8,128)(2,1)S(1)}, bf16[100,2500]{1,0:T(8,128)(2,1)}, u32[]{:S(2)}) copy-start(bf16[100,2500]{1,0:T(8,128)(2,1)} %t1.3) | copy-start | bytes 1500004
  0.6 8.1 %copy-start.10 = (bf16[100,100]{1,0:T(8,128)(2,1)S(1)}, bf16[100,100]{1,0:T(8,128)(2,1)}, u32[]{:S(2)}) copy-start(bf16[100,100]{1,0:T(8,128)(2,1)} %c2.1) | copy-start | bytes 60004
  0.7 8.0 %copy-start.2 = (bf16[100,2500]{1,0:T(8,128)(2,1)S(1)}, bf16[100,2500]{1,0:T(8,128)(2,1)}, u32[]{:S(2)}) copy-start(bf16[100,2500]{1,0:T(8,128)(2,1)} %t2.1) | copy-start | bytes 1500004
  0.7 8.0 %copy-start.3 = (bf16[100,2500]{1,0:T(8,128)(2,1)S(1)}, bf16[100,2500]{1,0:T(8,128)(2,1)}, u32[]{:S(2)}) copy-start(bf16[100,2500]{1,0:T(8,128)(2,1)} %t4.1) | copy-start | bytes 1500004
  0.7 8.0 %copy-start.7 = (f32[100,100]{1,0:T(8,128)S(1)}, f32[100,100]{1,0:T(8,128)}, u32[]{:S(2)}) copy-start(f32[100,100]{1,0:T(8,128)} %below.3) | copy-start | bytes 120004
  0.7 8.0 %copy-start.6 = (f32[100,100]{1,0:T(8,128)S(1)}, f32[100,100]{1,0:T(8,128)}, u32[]{:S(2)}) copy-start(f32[100,100]{1,0:T(8,128)} %above.3) | copy-start | bytes 120004
  0.7 8.0 %copy-start.8 = (f32[100,100]{1,0:T(8,128)S(1)}, f32[100,100]{1,0:T(8,128)}, u32[]{:S(2)}) copy-start(f32[100,100]{1,0:T(8,128)} %right.3) | copy-start | bytes 120004
  4.2 17.4 %collective-permute-start = (bf16[100,2560]{1,0:T(8,128)(2,1)}, bf16[100,2560]{1,0:T(8,128)(2,1)S(1)}, u32[]{:S(2)}, u32[]{:S(2)}) collective-permute-start(bf16[100,2560]{1,0:T(8,128)(2,1)} %get-tuple-element.34.upper_packed.after), channel_id=1, source_target_pairs={{0,7},{1,0},{2,1},{3,2},{4,3},{5,4},{6,5},{7,6},{8,15},{9,8},{10,9... | collective-permute-start | bytes 1536008 | tf_op jit(solution)/shard_map/ppermute | solution.py:484
  8.7 5.3 %copy-start = (bf16[8,625,625]{2,0,1:T(8,128)(2,1)S(1)}, bf16[8,625,625]{2,0,1:T(8,128)(2,1)}, u32[]{:S(2)}) copy-start(bf16[8,625,625]{2,0,1:T(8,128)(2,1)} %param.24) | copy-start | bytes 18750004
  8.7 13.7 %collective-permute-start.1 = (bf16[100,2560]{1,0:T(8,128)(2,1)}, bf16[100,2560]{1,0:T(8,128)(2,1)S(1)}, u32[]{:S(2)}, u32[]{:S(2)}) collective-permute-start(bf16[100,2560]{1,0:T(8,128)(2,1)} %get-tuple-element.35.lower_packed), channel_id=1, source_target_pairs={{0,1},{1,2},{2,3},{3,4},{4,5},{5,6},{6,7},{7,0},{8,9},{9,10},{10,1... | collective-permute-start | bytes 1536008 | tf_op jit(solution)/shard_map/ppermute | solution.py:484
  8.7 1.2 %copy-start.4 = (bf16[100,2560]{1,0:T(8,128)(2,1)S(1)}, bf16[100,2560]{1,0:T(8,128)(2,1)}, u32[]{:S(2)}) copy-start(bf16[100,2560]{1,0:T(8,128)(2,1)} %get-tuple-element.35.lower_packed) | copy-start | bytes 1536004
  9.9 1.3 %copy-start.5 = (bf16[100,2560]{1,0:T(8,128)(2,1)S(1)}, bf16[100,2560]{1,0:T(8,128)(2,1)}, u32[]{:S(2)}) copy-start(bf16[100,2560]{1,0:T(8,128)(2,1)} %get-tuple-element.34.upper_packed.after) | copy-start | bytes 1536004
  13.2 49.0 %collective-permute-start.3 = (bf16[100,2560]{1,0:T(8,128)(2,1)S(1)}, bf16[100,2560]{1,0:T(8,128)(2,1)S(1)}, u32[]{:S(2)}, u32[]{:S(2)}) collective-permute-start(bf16[100,2560]{1,0:T(8,128)(2,1)S(1)} %get-tuple-element.46), channel_id=1, source_target_pairs={{0,9},{1,10},{2,11},{3,12},{4,13},{5,14},{6,15},{7,8},{8,17},{9,18... | collective-permute-start | bytes 1536008 | tf_op jit(solution)/shard_map/ppermute | solution.py:494
  13.3 48.7 %collective-permute-start.4 = (bf16[100,2500]{1,0:T(8,128)(2,1)S(1)}, bf16[100,2500]{1,0:T(8,128)(2,1)S(1)}, u32[]{:S(2)}, u32[]{:S(2)}) collective-permute-start(bf16[100,2500]{1,0:T(8,128)(2,1)S(1)} %get-tuple-element.47), channel_id=1, source_target_pairs={{0,1},{1,2},{2,3},{3,4},{4,5},{5,6},{6,7},{7,0},{8,9},{9,10},{10,1... | collective-permute-start | bytes 1500008 | tf_op jit(solution)/shard_map/ppermute | solution.py:484
  14.0 3.4 %copy-start.12 = (s32[640,1]{1,0:T(8,128)S(1)}, s32[640,1]{1,0:T(8,128)}, u32[]{:S(2)}) copy-start(s32[640,1]{1,0:T(8,128)} %constant.8.clone.rows) | copy-start | bytes 7684
  14.0 3.4 %copy-start.14 = (s32[1,640]{1,0:T(1,128)S(1)}, s32[1,640]{1,0:T(1,128)}, u32[]{:S(2)}) copy-start(s32[1,640]{1,0:T(1,128)} %constant.9.clone.columns) | copy-start | bytes 7684
  15.7 47.4 %collective-permute-start.8 = (bf16[625,625]{1,0:T(8,128)(2,1)S(1)}, bf16[625,625]{1,0:T(8,128)(2,1)S(1)}, u32[]{:S(2)}, u32[]{:S(2)}) collective-permute-start(bf16[625,625]{1,0:T(8,128)(2,1)S(1)} %shard_map.211.tensor), channel_id=1, source_target_pairs={{0,1},{1,2},{2,3},{3,4},{4,5},{5,6},{6,7},{7,0},{8,9},{9,10},{10,1... | collective-permute-start | bytes 2343758 | tf_op jit(solution)/shard_map/ppermute | solution.py:484
  30.4 25.0 %copy-start.9 = (f32[100,100]{1,0:T(8,128)S(1)}, f32[100,100]{1,0:T(8,128)}, u32[]{:S(2)}) copy-start(f32[100,100]{1,0:T(8,128)} %left.3) | copy-start | bytes 120004
  55.3 14.9 %collective-permute-start.2 = (bf16[100,2816]{1,0:T(8,128)(2,1)S(1)}, bf16[100,2816]{1,0:T(8,128)(2,1)S(1)}, u32[]{:S(2)}, u32[]{:S(2)}) collective-permute-start(bf16[100,2816]{1,0:T(8,128)(2,1)S(1)} %get-tuple-element.45), channel_id=1, source_target_pairs={{0,9},{1,10},{2,11},{3,12},{4,13},{5,14},{6,15},{7,8},{8,17},{9,18... | collective-permute-start | bytes 1689608 | tf_op jit(solution)/shard_map/ppermute | solution.py:494
  61.5 8.7 %collective-permute-start.5 = (f32[112,128]{1,0:T(8,128)S(1)}, f32[112,128]{1,0:T(8,128)S(1)}, u32[]{:S(2)}, u32[]{:S(2)}) collective-permute-start(f32[112,128]{1,0:T(8,128)S(1)} %get-tuple-element.51.after), channel_id=1, source_target_pairs={{0,9},{1,10},{2,11},{3,12},{4,13},{5,14},{6,15},{7,8},{8,17},{9,18... | collective-permute-start | bytes 172040 | tf_op jit(solution)/shard_map/ppermute | solution.py:494
  62.0 1.1 %copy-start.11 = (s32[640,1]{1,0:T(8,128)S(1)}, s32[640,1]{1,0:T(8,128)}, u32[]{:S(2)}) copy-start(s32[640,1]{1,0:T(8,128)} %constant.10.clone.rows) | copy-start | bytes 7684
  62.1 1.1 %copy-start.13 = (s32[1,640]{1,0:T(1,128)S(1)}, s32[1,640]{1,0:T(1,128)}, u32[]{:S(2)}) copy-start(s32[1,640]{1,0:T(1,128)} %constant.11.clone.columns) | copy-start | bytes 7684
  62.1 14.5 %collective-permute-start.7 = (bf16[100,2688]{1,0:T(8,128)(2,1)S(1)}, bf16[100,2688]{1,0:T(8,128)(2,1)S(1)}, u32[]{:S(2)}, u32[]{:S(2)}) collective-permute-start(bf16[100,2688]{1,0:T(8,128)(2,1)S(1)} %get-tuple-element.54), channel_id=1, source_target_pairs={{0,1},{1,2},{2,3},{3,4},{4,5},{5,6},{6,7},{7,0},{8,9},{9,10},{10,1... | collective-permute-start | bytes 1612808 | tf_op jit(solution)/shard_map/ppermute | solution.py:484
  73.3 28.8 %collective-permute-start.6 = (bf16[100,2816]{1,0:T(8,128)(2,1)S(1)}, bf16[100,2816]{1,0:T(8,128)(2,1)S(1)}, u32[]{:S(2)}, u32[]{:S(2)}) collective-permute-start(bf16[100,2816]{1,0:T(8,128)(2,1)S(1)} %get-tuple-element.53), channel_id=1, source_target_pairs={{0,7},{1,0},{2,1},{3,2},{4,3},{5,4},{6,5},{7,6},{8,15},{9,8},{10,9... | collective-permute-start | bytes 1689608 | tf_op jit(solution)/shard_map/ppermute | solution.py:484

commit v2 on v1

--- a/solution.py
+++ b/solution.py
@@ -55,16 +55,17 @@
     shape = (LANES, LANES)
     row, lane = index_of(shape, 0), index_of(shape, 1)
     keep = (row < bond) & (lane < bond)
+    zero = jnp.zeros(shape, BF16)
     pieces = []
     for k in range(site):
         tile, offset = divmod(k * bond, LANES)
-        piece = ref[:, tile * LANES : (tile + 1) * LANES].astype(F32)
+        piece = ref[:, tile * LANES : (tile + 1) * LANES]
         if offset:
             piece = pltpu.roll(piece, LANES - offset, 1)
         if offset + bond > LANES:
-            more = ref[:, (tile + 1) * LANES : (tile + 2) * LANES].astype(F32)
+            more = ref[:, (tile + 1) * LANES : (tile + 2) * LANES]
             piece = jnp.where(lane < LANES - offset, piece, pltpu.roll(more, LANES - offset, 1))
-        pieces.append(jnp.where(keep, piece, 0.0).astype(BF16))
+        pieces.append(jnp.where(keep, piece, zero))
     return pieces
 
 
@@ -78,19 +79,20 @@
             shift = k * bond - begin
             piece = pltpu.roll(tiles[k], shift % LANES, 1) if shift % LANES else tiles[k]
             value = piece if value is None else jnp.where(lane >= shift, piece, value)
-        ref[:, begin : begin + LANES] = value.astype(ref.dtype)
+        ref[:, begin : begin + LANES] = value
 
 
 def pack(tiles, ref, bond):
     quarter = bond // QUARTERS
     lane = index_of((LANES, LANES), 1)
+    tiles = [tile.astype(BF16) for tile in tiles]
     for group in range(len(tiles) // (QUARTERS + 1)):
         first = group * (QUARTERS + 1)
         for m in range(QUARTERS):
             piece = pltpu.roll(tiles[first + QUARTERS], bond - m * quarter, 1)
             slot = group * QUARTERS + m
             value = jnp.where(lane < bond, tiles[first + m], piece)
-            ref[:, slot * LANES : (slot + 1) * LANES] = value.astype(ref.dtype)
+            ref[:, slot * LANES : (slot + 1) * LANES] = value
 
 
 def unpack(ref, bond, site):
@@ -98,16 +100,17 @@
     shape = (LANES, LANES)
     row, lane = index_of(shape, 0), index_of(shape, 1)
     keep = (row < bond) & (lane < bond)
+    zero = jnp.zeros(shape, BF16)
     tiles = []
     for group in range(site // (QUARTERS + 1)):
         last = None
         for m in range(QUARTERS):
             slot = group * QUARTERS + m
-            value = ref[:, slot * LANES : (slot + 1) * LANES].astype(F32)
-            tiles.append(jnp.where(keep, value, 0.0).astype(BF16))
+            value = ref[:, slot * LANES : (slot + 1) * LANES]
+            tiles.append(jnp.where(keep, value, zero))
             piece = pltpu.roll(value, LANES - bond + m * quarter, 1)
             last = piece if last is None else jnp.where(lane >= m * quarter, piece, last)
-        tiles.append(jnp.where(keep, last, 0.0).astype(BF16))
+        tiles.append(jnp.where(keep, last, zero))
     return tiles
 
 
@@ -139,15 +142,20 @@
             )
             work[n] = jnp.where(block, start, matrix)
         pivots = [jnp.ones((ROWS, LANES), F32) for _ in work]
+        pivot = [column[0][:1, :] for column in columns]
         for j in range(ROWS):
             for n in range(len(work)):
                 column = columns[n]
-                pivot = column[j][j : j + 1, :]
-                factor = jnp.where(row > j, column[j] * (1.0 / pivot), 0.0)
-                work[n] = work[n] - factor * work[n][j : j + 1, :]
+                inverse = 1.0 / pivot[n]
+                pivots[n] = jnp.where(small_row == j, pivot[n], pivots[n])
+                if j + 1 < ROWS:
+                    at = slice(j + 1, j + 2)
+                    cross = column[j][at, :] * column[j + 1][j : j + 1, :]
+                    pivot[n] = column[j + 1][at, :] - cross * inverse
+                factor = jnp.where(row > j, column[j], 0.0) * inverse
                 for later in range(j + 1, ROWS):
                     column[later] = column[later] - factor * column[later][j : j + 1, :]
-                pivots[n] = jnp.where(small_row == j, pivot, pivots[n])
+                work[n] = work[n] - factor * work[n][j : j + 1, :]
         for n in range(len(work)):
             scaled = work[n][:ROWS] * lax.rsqrt(pivots[n])
             done[n].append(jnp.where(small_lane <= small_row + first, scaled, 0.0))
@@ -216,10 +224,9 @@
 
 
 def prepare_kernel(
-    bond, site, c2, t2, t4, t1, above, below, right, upper_packed, lower_packed,
-    t4_wide, t1_out, upper, upper_sketch, lower, lower_sketch, side_packed, side, side_sketch,
+    bond, site, c2, t2, t4, above, below, right, upper_packed, lower_packed,
+    t4_wide, upper, upper_sketch, lower, lower_sketch, side_packed, side, side_sketch,
 ):
-    t1_out[...] = t1[...]
     tiles = half_tiles(square_of(c2, bond).astype(BF16), spread(t2, bond, site))
     fill(side, tiles)
     pack(tiles, side_packed, bond)
@@ -400,17 +407,17 @@
     for tile in tiles[1:]:
         squares = squares + tile * tile
     scale = 1.0 / jnp.sqrt(jnp.sum(squares) / (bond * bond * site) + 1e-06)
-    tiles = [tile * scale for tile in tiles]
+    tiles = [(tile * scale).astype(BF16) for tile in tiles]
     gather_dense(tiles, dense, bond)
     if first:
         for k, tile in enumerate(tiles):
-            wide[:, k * LANES : (k + 1) * LANES] = tile.astype(BF16)
+            wide[:, k * LANES : (k + 1) * LANES] = tile
         start = dense.shape[1] - 2 * LANES
         dense[:, start : start + LANES] = square_of(corner, bond).astype(BF16)
         dense[:, start + LANES :] = square_of(bottom, bond).astype(BF16)
 
 
-def pick_kernel(pattern, tensors, out, *tiles):
+def pick_kernel(pattern, tensors, after, out, *tiles):
     height, count, width = tensors.shape
     values = tensors[...].astype(F32).reshape(height * count, width)
     for n, tile in enumerate(tiles):
@@ -420,7 +427,10 @@
         out[:, n * LANES : end] = rows[:, : end - n * LANES].astype(BF16)
 
 
-def arrange_kernel(tensor, rows, columns, after, out):
+def arrange_kernel(count, tensor, rows, columns, *refs):
+    held, out, copies = refs[:count], refs[-count - 1], refs[len(refs) - count :]
+    for source, target in zip(held, copies):
+        target[...] = source[...]
     square = tensor.shape[0]
     pick_rows = jnp.where(index_of((rows.shape[0], square), 1) == rows[...], 1.0, 0.0).astype(BF16)
     pick_columns = jnp.where(index_of((square, columns.shape[1]), 0) == columns[...], 1.0, 0.0)
@@ -514,7 +524,7 @@
     frame_scratch = [pltpu.VMEM((body_rows, LANES), F32), pltpu.VMEM((tail_rows, LANES), F32)]
     rows, columns = places(site)
 
-    def pick(index):
+    def pick(index, after):
         count = tensors.shape[0]
         return pl.pallas_call(
             pick_kernel,
@@ -522,28 +532,33 @@
             in_specs=[
                 pl.BlockSpec(memory_space=pltpu.SMEM),
                 pl.BlockSpec((LANES, count, square), lambda i: (i, 0, 0)),
+                pl.BlockSpec(memory_space=pl.ANY),
             ],
             out_specs=pl.BlockSpec((LANES, square), lambda i: (i, 0)),
             out_shape=shape_of((square, square)),
             scratch_shapes=[pltpu.VMEM((LANES * count, LANES), F32)] * -(-square // LANES),
             compiler_params=pltpu.CompilerParams(vmem_limit_bytes=16 * MIB),
             cost_estimate=cost(2),
-        )(index, tensors.transpose(1, 0, 2))
-
-    def arrange(which, tensor, after):
+        )(index, tensors.transpose(1, 0, 2), after)
+
+    def arrange(which, tensor, held, after):
         height, depth = rows.shape[1], columns.shape[1]
         vmem = pl.BlockSpec(memory_space=pltpu.VMEM)
         return pl.pallas_call(
-            arrange_kernel,
-            in_specs=[vmem, vmem, vmem, pl.BlockSpec(memory_space=pl.ANY)],
-            out_specs=vmem,
-            out_shape=shape_of((height, depth)),
+            functools.partial(arrange_kernel, len(held)),
+            grid=(1,),
+            in_specs=[vmem, vmem, vmem]
+            + [block_of(array) for array in held]
+            + [pl.BlockSpec(memory_space=pl.ANY)],
+            out_specs=[vmem] + [block_of(array) for array in held],
+            out_shape=[shape_of((height, depth))] + [shape_of(array.shape) for array in held],
             compiler_params=pltpu.CompilerParams(vmem_limit_bytes=16 * MIB),
             cost_estimate=cost(2),
         )(
             tensor,
             rows[which].reshape(height, 1),
             columns[which].reshape(1, depth),
+            *held,
             after,
         )
 
@@ -573,20 +588,20 @@
     )
     upper_next = shift(upper_packed, "row", -1)
     lower_back = shift(lower_packed, "row", 1)
-    tensor = pick(pattern.reshape(1))
-    tensor_left = arrange(0, tensor, upper_packed)
     prepared = call(
         functools.partial(prepare_kernel, bond, site),
-        (c2, t2, t4, t1, above, below, right, upper_packed, lower_packed),
-        [wide, dense, stack, stack_f32, stack, stack_f32, packed, stack, stack_f32],
+        (c2, t2, t4, above, below, right, upper_packed, lower_packed),
+        [wide, stack, stack_f32, stack, stack_f32, packed, stack, stack_f32],
         [],
         16,
         2,
     )
-    t4_wide, t1_held, upper, upper_sketch, lower, lower_sketch, side_packed, side, side_sketch = prepared
+    t4_wide, upper, upper_sketch, lower, lower_sketch, side_packed, side, side_sketch = prepared
+    tensor = pick(pattern.reshape(1), side)
+    tensor_left, t1_held, side_held, tensor_held = arrange(0, tensor, [t1, side_packed, tensor], side)
     t1_back = shift(t1_held, "row", 1)
-    side_back = shift_both(side_packed, 1, 1)
-    tensor_back = shift(tensor, "row", 1)
+    side_back = shift_both(side_held, 1, 1)
+    tensor_back = shift(tensor_held, "row", 1)
     rows_left, frame_below, corner_top, corner_bottom = call(
         functools.partial(vertical_kernel, bond, site),
         (upper_next, lower_back, above, below, upper, upper_sketch, lower, lower_sketch),
@@ -607,7 +622,7 @@
     )
     inverse_back = shift_both(inverse, 1, 1)
     frame_back = shift(frame_right, "row", 1)
-    tensor_top = arrange(1, tensor_back, inverse)
+    (tensor_top,) = arrange(1, tensor_back, [], inverse)
     early_sketch, t1_wide = call(
         functools.partial(early_kernel, bond, site),
         (side_back, right, t1_back, inverse),

time: 103 us -> 105 us (1.019)
  Pallas kernels: 80 us -> 81.2 us
    pallas_call x9, Pallas kernels: 74.9 us -> 76 us  [call(): pl.pallas_call(kernel, grid=(1,), in_specs=specs, out_specs=[block_of(out...]
  transfers between devices with their start and end apart: 9 -> 9, of which waited for: 3 -> 3; matrix products, arithmetic and copies ran while one was open for 0% -> 0% of each run, Pallas kernels for 73% -> 74%
where the time goes in v2:
time: 105 us; the launch traced here: 104 us
  Pallas kernels  81.2 us (77%)
  starting transfers between devices  10.7 us (10%)
  waiting for transfers between devices  7.97 us (8%)
  local copies, waits for them, and re-layouts  2.82 us (3%)
  between operations  1.54 us (1%)
    pallas_call x9, Pallas kernels, call(): pl.pallas_call(kernel, grid=(1,), in_specs=specs, out_specs=[block_of(out...  76 us
    ppermute x6, starting transfers between devices, shift(): return lax.ppermute(value, axis, pairs)  9.93 us
    ppermute x3, waiting for transfers between devices, shift_both(): return lax.ppermute(value, ('col', 'row'), pairs)  4.72 us
    pallas_call x2, Pallas kernels, arrange(): pl.pallas_call(functools.partial(arrange_kernel, len(held)), grid=(1,), i...  3.55 us
    ppermute x6, waiting for transfers between devices, shift(): return lax.ppermute(value, axis, pairs)  3.25 us
    unnamed x30, local copies, waits for them, and re-layouts  2.82 us
  transfers between devices with their start and end apart: 9, of which 3 were waited for; matrix products, arithmetic and copies ran while one was open for 0% of the time, Pallas kernels for 74%

profile of v2, /device:TPU:0, one launch (start us, length us, event | category | flops | bytes accessed | tf_op | source)
XLA Modules:
  0.0 104.2 jit_solution(13077120886322566192)
XLA Ops:
  0.6 0.0 copy-start.10
  0.6 0.0 copy-start.1
  0.7 0.0 copy-start.2
  0.7 0.0 copy-start.7
  0.7 0.0 copy-start.6
  0.7 0.0 copy-start.8
  0.7 3.6 %shard_map.208 = (bf16[100,2560]{1,0:T(8,128)(2,1)}, bf16[100,2560]{1,0:T(8,128)(2,1)}) custom-call(bf16[100,100]{1,0:T(8,128)(2,1)} %c1.1, bf16[100,2500]{1,0:T(8,128)(2,1)} %refs_0_.1, bf16[100,100]{1,0:T(8,128)(2,1)} %c4.1, bf16[100,2500]{1,0:T(8,128)(2,1)} %t3.1), custom_call_target="tpu_custom_call" | custom-call | flops 2000000000 | bytes 2000000 | tf_op jit(solution)/shard_map/pallas_call | solution.py:475
  4.3 4.5 %collective-permute-start = (bf16[100,2560]{1,0:T(8,128)(2,1)}, bf16[100,2560]{1,0:T(8,128)(2,1)S(1)}, u32[]{:S(2)}, u32[]{:S(2)}) collective-permute-start(bf16[100,2560]{1,0:T(8,128)(2,1)} %get-tuple-element.37.upper_packed), channel_id=1, source_target_pairs={{0,7},{1,0},{2,1},{3,2},{4,3},{5,4},{6,5},{7,6},{8,15},{9,8},{10,9... | collective-permute-start | bytes 1536008 | tf_op jit(solution)/shard_map/ppermute | solution.py:494
  8.8 0.0 collective-permute-start.1
  9.4 0.0 copy-done.10
  9.4 0.0 copy-done.1
  9.4 0.0 copy-done.2
  9.4 0.0 copy-done.7
  9.4 0.0 copy-done.6
  9.5 0.0 copy-done.8
  9.5 0.0 copy-start.4
  9.5 1.0 copy-done.4
  10.5 0.0 copy-start.5
  10.5 1.0 copy-done.5
  11.6 0.0 copy-start
  11.6 2.1 %shard_map.209 = (bf16[128,3200]{1,0:T(8,128)(2,1)S(1)}, bf16[3200,128]{1,0:T(8,128)(2,1)S(1)}, f32[3200,128]{1,0:T(8,128)S(1)}, bf16[3200,128]{1,0:T(8,128)(2,1...) custom-call(bf16[100,100]{1,0:T(8,128)(2,1)S(1)} %copy-done.10, ...), custom_call_target="tpu_custom_call" | custom-call | flops 2000000000 | bytes 2000000 | tf_op jit(solution)/shard_map/pallas_call | solution.py:475
  13.7 0.7 copy-done
  14.4 0.0 copy-start.3
  14.4 0.0 copy-start.12
  14.4 0.0 copy-start.14
  14.4 1.6 %shard_map.211.tensor.refs_2_ = bf16[625,625]{1,0:T(8,128)(2,1)S(1)} custom-call(s32[1]{0:T(128)} %bitcast.2.pattern, bf16[625,8,625]{2,1,0:T(8,128)(2,1)S(1)} %bitcast.3, bf16[3200,128]{1,0:T(8,128)(2,1)S(1)} %get-tuple-element.45.after.refs_3_.side), custom_call_target="tpu_custom_call" | custom-call | flops 2000000000 | bytes 2000000 | tf_op jit(solution)/shard_map/pallas_call | solution.py:529
  16.0 0.0 copy-done.3
  16.0 0.0 copy-done.12
  16.0 0.0 copy-done.14
  16.1 1.8 %shard_map.212 = (bf16[640,640]{1,0:T(8,128)(2,1)S(1)}, bf16[100,2500]{1,0:T(8,128)(2,1)S(1)}, bf16[100,2560]{1,0:T(8,128)(2,1)S(1)}, bf16[625,625]{1,0:T(8,128)(2,1)S(1)}) custom-call(bf16[625,625]{1,0:T(8,128)(2,1)S(1)} %shard_map.211.tensor.refs_2_, s32[640,1]{1,0:T(8,128)S(1)} %copy-done.12, s32[1,640]{1,0:T(1,128)S(1)} %copy-done.14, ...), custom_call_target="tpu_custom_call" | custom-call | flops 2000000000 | bytes 2000000 | tf_op jit(solution)/shard_map/pallas_call | solution.py:547
  17.9 0.1 collective-permute-start.8
  18.0 0.2 collective-permute-start.3
  18.2 1.0 collective-permute-start.4
  19.2 2.1 %collective-permute-done.upper_packed = bf16[100,2560]{1,0:T(8,128)(2,1)S(1)} collective-permute-done((bf16[100,2560]{1,0:T(8,128)(2,1)}, bf16[100,2560]{1,0:T(8,128)(2,1)S(1)}, u32[]{:S(2)}, u32[]{:S(2)}) %collective-permute-start) | collective-permute-done | bytes 512032 | tf_op jit(solution)/shard_map/ppermute | solution.py:494
  21.4 1.1 %collective-permute-done.1.lower_packed = bf16[100,2560]{1,0:T(8,128)(2,1)S(1)} collective-permute-done((bf16[100,2560]{1,0:T(8,128)(2,1)}, bf16[100,2560]{1,0:T(8,128)(2,1)S(1)}, u32[]{:S(2)}, u32[]{:S(2)}) %collective-permute-start.1) | collective-permute-done | bytes 512032 | tf_op jit(solution)/shard_map/ppermute | solution.py:494
  22.5 8.6 %shard_map.210 = (bf16[2656,128]{1,0:T(8,128)(2,1)S(1)}, bf16[3200,128]{1,0:T(8,128)(2,1)S(1)}, bf16[100,100]{1,0:T(8,128)(2,1)S(1)}, bf16[100,100]{1,0:T(8,128)(2,1)S(1)}) custom-call(bf16[100,2560]{1,0:T(8,128)(2,1)S(1)} %collective-permute-done.upper_packed, bf16[100,2560]{1,0:T(8,128)(2,1)S(1)} %collective-permute-done.1.lower_packed, ...), custom_call_target="tpu_custom_call" | custom-call | flops 8000000000 | bytes 8000000 | tf_op jit(solution)/shard_map/pallas_call | solution.py:475
  31.0 0.0 copy-start.9
  31.1 25.0 %shard_map.213 = (bf16[100,2816]{1,0:T(8,128)(2,1)S(1)}, bf16[128,3200]{1,0:T(8,128)(2,1)S(1)}) custom-call(bf16[2656,128]{1,0:T(8,128)(2,1)S(1)} %get-tuple-element.43.rows_ref, bf16[128,3200]{1,0:T(8,128)(2,1)S(1)} %get-tuple-element.44.edge, bf16[640,640]{1,0:T(8,128)(2,1)S(1)} %get-tuple-element.47.tensor, ...), custom_call_target="tpu_custom_call" | custom-call | flops 24999999488 | bytes 25000000 | tf_op jit(solution)/shard_map/pallas_call | solution.py:475
  56.1 0.1 collective-permute-start.2
  56.1 0.0 copy-done.9
  56.1 6.5 %shard_map.214 = (f32[112,128]{1,0:T(8,128)S(1)}, bf16[100,2688]{1,0:T(8,128)(2,1)S(1)}) custom-call(bf16[100,100]{1,0:T(8,128)(2,1)S(1)} %get-tuple-element.49.refs_0_.c1, bf16[128,3200]{1,0:T(8,128)(2,1)S(1)} %get-tuple-element.54.edge, f32[100,100]{1,0:T(8,128)S(1)} %copy-done.9, bf16[3200,128]{1,0:T(8,128)(2,1)S(1)} %get-tuple-element.45.after.refs_3_.side, ...), custom_call_target="tpu_custom_call" | custom-call | flops 5000000000 | bytes 5000000 | tf_op jit(solution)/shard_map/pallas_call | solution.py:475
  62.6 0.5 collective-permute-start.5
  63.1 0.0 collective-permute-done.4.t1
  63.1 0.0 copy-start.11
  63.1 0.0 copy-start.13
  63.1 0.7 collective-permute-start.7
  63.8 0.0 collective-permute-done.3.side_packed
  63.8 0.7 shard_map.215
  64.5 0.0 collective-permute-done.8.tensor
  64.5 0.0 copy-done.11
  64.6 0.0 copy-done.13
  64.6 1.7 %shard_map.218.tensor = bf16[640,640]{1,0:T(8,128)(2,1)S(1)} custom-call(bf16[625,625]{1,0:T(8,128)(2,1)S(1)} %collective-permute-done.8.tensor, s32[640,1]{1,0:T(8,128)S(1)} %copy-done.11, s32[1,640]{1,0:T(1,128)S(1)} %copy-done.13, f32[112,128]{1,0:T(8,128)S(1)} %get-tuple-element.56.after.refs_0_), custom_call_target="tpu_custom_call" | custom-call | flops 2000000000 | bytes 2000000 | tf_op jit(solution)/shard_map/pallas_call | solution.py:547
  66.3 4.7 %collective-permute-done.5.inverse_ref = f32[112,128]{1,0:T(8,128)S(1)} collective-permute-done((f32[112,128]{1,0:T(8,128)S(1)}, f32[112,128]{1,0:T(8,128)S(1)}, u32[]{:S(2)}, u32[]{:S(2)}) %collective-permute-start.5) | collective-permute-done | bytes 57376 | tf_op jit(solution)/shard_map/ppermute | solution.py:504
  71.0 0.0 collective-permute-done.2.payload
  71.0 3.1 %shard_map.216 = (bf16[2656,128]{1,0:T(8,128)(2,1)S(1)}, bf16[100,100]{1,0:T(8,128)(2,1)}, bf16[100,2816]{1,0:T(8,128)(2,1)S(1)}) custom-call(bf16[100,2816]{1,0:T(8,128)(2,1)S(1)} %collective-permute-done.2.payload, f32[3200,128]{1,0:T(8,128)S(1)} %get-tuple-element.57.side_sketch, f32[100,100]{1,0:T(8,128)S(1)} %copy-done.9, ...), custom_call_target="tpu_custom_call" | custom-call | flops 4000000000 | bytes 4000000 | tf_op jit(solution)/shard_map/pallas_call | solution.py:475
  74.1 3.7 %collective-permute-start.6 = (bf16[100,2816]{1,0:T(8,128)(2,1)S(1)}, bf16[100,2816]{1,0:T(8,128)(2,1)S(1)}, u32[]{:S(2)}, u32[]{:S(2)}) collective-permute-start(bf16[100,2816]{1,0:T(8,128)(2,1)S(1)} %get-tuple-element.58), channel_id=1, source_target_pairs={{0,7},{1,0},{2,1},{3,2},{4,3},{5,4},{6,5},{7,6},{8,15},{9,8},{10,9... | collective-permute-start | bytes 1689608 | tf_op jit(solution)/shard_map/ppermute | solution.py:494
  77.8 0.0 collective-permute-done.7.frame
  77.8 25.6 %shard_map.219 = bf16[100,2500]{1,0:T(8,128)(2,1)} custom-call(bf16[2656,128]{1,0:T(8,128)(2,1)S(1)} %get-tuple-element.64.rows_ref, bf16[128,3200]{1,0:T(8,128)(2,1)S(1)} %get-tuple-element.65.edge, bf16[640,640]{1,0:T(8,128)(2,1)S(1)} %shard_map.218.tensor, bf16[100,2688]{1,0:T(8,128)(2,1)S(1)} %collective-permute-done.7.frame), custom_call_target="tpu_custom_call" | custom-call | flops 24999999488 | bytes 25000000 | tf_op jit(solution)/shard_map/pallas_call | solution.py:475
  103.4 0.0 collective-permute-done.6.payload
  103.4 0.9 shard_map.217
Async XLA Ops:
  0.6 8.8 %copy-start.10 = (bf16[100,100]{1,0:T(8,128)(2,1)S(1)}, bf16[100,100]{1,0:T(8,128)(2,1)}, u32[]{:S(2)}) copy-start(bf16[100,100]{1,0:T(8,128)(2,1)} %c2.1) | copy-start | bytes 60004
  0.6 8.8 %copy-start.1 = (bf16[100,2500]{1,0:T(8,128)(2,1)S(1)}, bf16[100,2500]{1,0:T(8,128)(2,1)}, u32[]{:S(2)}) copy-start(bf16[100,2500]{1,0:T(8,128)(2,1)} %t2.1) | copy-start | bytes 1500004
  0.7 8.8 %copy-start.2 = (bf16[100,2500]{1,0:T(8,128)(2,1)S(1)}, bf16[100,2500]{1,0:T(8,128)(2,1)}, u32[]{:S(2)}) copy-start(bf16[100,2500]{1,0:T(8,128)(2,1)} %t4.1) | copy-start | bytes 1500004
  0.7 8.8 %copy-start.7 = (f32[100,100]{1,0:T(8,128)S(1)}, f32[100,100]{1,0:T(8,128)}, u32[]{:S(2)}) copy-start(f32[100,100]{1,0:T(8,128)} %below.3) | copy-start | bytes 120004
  0.7 8.8 %copy-start.6 = (f32[100,100]{1,0:T(8,128)S(1)}, f32[100,100]{1,0:T(8,128)}, u32[]{:S(2)}) copy-start(f32[100,100]{1,0:T(8,128)} %above.3) | copy-start | bytes 120004
  0.7 8.8 %copy-start.8 = (f32[100,100]{1,0:T(8,128)S(1)}, f32[100,100]{1,0:T(8,128)}, u32[]{:S(2)}) copy-start(f32[100,100]{1,0:T(8,128)} %right.3) | copy-start | bytes 120004
  4.3 17.1 %collective-permute-start = (bf16[100,2560]{1,0:T(8,128)(2,1)}, bf16[100,2560]{1,0:T(8,128)(2,1)S(1)}, u32[]{:S(2)}, u32[]{:S(2)}) collective-permute-start(bf16[100,2560]{1,0:T(8,128)(2,1)} %get-tuple-element.37.upper_packed), channel_id=1, source_target_pairs={{0,7},{1,0},{2,1},{3,2},{4,3},{5,4},{6,5},{7,6},{8,15},{9,8},{10,9... | collective-permute-start | bytes 1536008 | tf_op jit(solution)/shard_map/ppermute | solution.py:494
  8.8 13.7 %collective-permute-start.1 = (bf16[100,2560]{1,0:T(8,128)(2,1)}, bf16[100,2560]{1,0:T(8,128)(2,1)S(1)}, u32[]{:S(2)}, u32[]{:S(2)}) collective-permute-start(bf16[100,2560]{1,0:T(8,128)(2,1)} %get-tuple-element.38.lower_packed), channel_id=1, source_target_pairs={{0,1},{1,2},{2,3},{3,4},{4,5},{5,6},{6,7},{7,0},{8,9},{9,10},{10,1... | collective-permute-start | bytes 1536008 | tf_op jit(solution)/shard_map/ppermute | solution.py:494
  9.5 1.0 %copy-start.4 = (bf16[100,2560]{1,0:T(8,128)(2,1)S(1)}, bf16[100,2560]{1,0:T(8,128)(2,1)}, u32[]{:S(2)}) copy-start(bf16[100,2560]{1,0:T(8,128)(2,1)} %get-tuple-element.38.lower_packed) | copy-start | bytes 1536004
  10.5 1.0 %copy-start.5 = (bf16[100,2560]{1,0:T(8,128)(2,1)S(1)}, bf16[100,2560]{1,0:T(8,128)(2,1)}, u32[]{:S(2)}) copy-start(bf16[100,2560]{1,0:T(8,128)(2,1)} %get-tuple-element.37.upper_packed) | copy-start | bytes 1536004
  11.6 2.8 %copy-start = (bf16[8,625,625]{2,0,1:T(8,128)(2,1)S(1)}, bf16[8,625,625]{2,0,1:T(8,128)(2,1)}, u32[]{:S(2)}) copy-start(bf16[8,625,625]{2,0,1:T(8,128)(2,1)} %param.24) | copy-start | bytes 18750004
  14.4 1.7 %copy-start.3 = (bf16[100,2500]{1,0:T(8,128)(2,1)S(1)}, bf16[100,2500]{1,0:T(8,128)(2,1)}, u32[]{:S(2)}) copy-start(bf16[100,2500]{1,0:T(8,128)(2,1)} %refs_0_.1) | copy-start | bytes 1500004
  14.4 1.7 %copy-start.12 = (s32[640,1]{1,0:T(8,128)S(1)}, s32[640,1]{1,0:T(8,128)}, u32[]{:S(2)}) copy-start(s32[640,1]{1,0:T(8,128)} %constant.8.clone.rows) | copy-start | bytes 7684
  14.4 1.7 %copy-start.14 = (s32[1,640]{1,0:T(1,128)S(1)}, s32[1,640]{1,0:T(1,128)}, u32[]{:S(2)}) copy-start(s32[1,640]{1,0:T(1,128)} %constant.9.clone.columns) | copy-start | bytes 7684
  17.9 46.6 %collective-permute-start.8 = (bf16[625,625]{1,0:T(8,128)(2,1)S(1)}, bf16[625,625]{1,0:T(8,128)(2,1)S(1)}, u32[]{:S(2)}, u32[]{:S(2)}) collective-permute-start(bf16[625,625]{1,0:T(8,128)(2,1)S(1)} %get-tuple-element.66), channel_id=1, source_target_pairs={{0,1},{1,2},{2,3},{3,4},{4,5},{5,6},{6,7},{7,0},{8,9},{9,10},{10,1... | collective-permute-start | bytes 2343758 | tf_op jit(solution)/shard_map/ppermute | solution.py:494
  18.0 45.8 %collective-permute-start.3 = (bf16[100,2560]{1,0:T(8,128)(2,1)S(1)}, bf16[100,2560]{1,0:T(8,128)(2,1)S(1)}, u32[]{:S(2)}, u32[]{:S(2)}) collective-permute-start(bf16[100,2560]{1,0:T(8,128)(2,1)S(1)} %get-tuple-element.52), channel_id=1, source_target_pairs={{0,9},{1,10},{2,11},{3,12},{4,13},{5,14},{6,15},{7,8},{8,17},{9,18... | collective-permute-start | bytes 1536008 | tf_op jit(solution)/shard_map/ppermute | solution.py:504
  18.2 44.9 %collective-permute-start.4 = (bf16[100,2500]{1,0:T(8,128)(2,1)S(1)}, bf16[100,2500]{1,0:T(8,128)(2,1)S(1)}, u32[]{:S(2)}, u32[]{:S(2)}) collective-permute-start(bf16[100,2500]{1,0:T(8,128)(2,1)S(1)} %get-tuple-element.53), channel_id=1, source_target_pairs={{0,1},{1,2},{2,3},{3,4},{4,5},{5,6},{6,7},{7,0},{8,9},{9,10},{10,1... | collective-permute-start | bytes 1500008 | tf_op jit(solution)/shard_map/ppermute | solution.py:494
  31.0 25.1 %copy-start.9 = (f32[100,100]{1,0:T(8,128)S(1)}, f32[100,100]{1,0:T(8,128)}, u32[]{:S(2)}) copy-start(f32[100,100]{1,0:T(8,128)} %left.3) | copy-start | bytes 120004
  56.1 14.9 %collective-permute-start.2 = (bf16[100,2816]{1,0:T(8,128)(2,1)S(1)}, bf16[100,2816]{1,0:T(8,128)(2,1)S(1)}, u32[]{:S(2)}, u32[]{:S(2)}) collective-permute-start(bf16[100,2816]{1,0:T(8,128)(2,1)S(1)} %get-tuple-element.51), channel_id=1, source_target_pairs={{0,9},{1,10},{2,11},{3,12},{4,13},{5,14},{6,15},{7,8},{8,17},{9,18... | collective-permute-start | bytes 1689608 | tf_op jit(solution)/shard_map/ppermute | solution.py:504
  62.6 8.4 %collective-permute-start.5 = (f32[112,128]{1,0:T(8,128)S(1)}, f32[112,128]{1,0:T(8,128)S(1)}, u32[]{:S(2)}, u32[]{:S(2)}) collective-permute-start(f32[112,128]{1,0:T(8,128)S(1)} %get-tuple-element.56.after.refs_0_), channel_id=1, source_target_pairs={{0,9},{1,10},{2,11},{3,12},{4,13},{5,14},{6,15},{7,8},{8,17},{9,18... | collective-permute-start | bytes 172040 | tf_op jit(solution)/shard_map/ppermute | solution.py:504
  63.1 1.4 %copy-start.11 = (s32[640,1]{1,0:T(8,128)S(1)}, s32[640,1]{1,0:T(8,128)}, u32[]{:S(2)}) copy-start(s32[640,1]{1,0:T(8,128)} %constant.10.clone.rows) | copy-start | bytes 7684
  63.1 1.4 %copy-start.13 = (s32[1,640]{1,0:T(1,128)S(1)}, s32[1,640]{1,0:T(1,128)}, u32[]{:S(2)}) copy-start(s32[1,640]{1,0:T(1,128)} %constant.11.clone.columns) | copy-start | bytes 7684
  63.1 14.6 %collective-permute-start.7 = (bf16[100,2688]{1,0:T(8,128)(2,1)S(1)}, bf16[100,2688]{1,0:T(8,128)(2,1)S(1)}, u32[]{:S(2)}, u32[]{:S(2)}) collective-permute-start(bf16[100,2688]{1,0:T(8,128)(2,1)S(1)} %get-tuple-element.59), channel_id=1, source_target_pairs={{0,1},{1,2},{2,3},{3,4},{4,5},{5,6},{6,7},{7,0},{8,9},{9,10},{10,1... | collective-permute-start | bytes 1612808 | tf_op jit(solution)/shard_map/ppermute | solution.py:494
  74.1 29.3 %collective-permute-start.6 = (bf16[100,2816]{1,0:T(8,128)(2,1)S(1)}, bf16[100,2816]{1,0:T(8,128)(2,1)S(1)}, u32[]{:S(2)}, u32[]{:S(2)}) collective-permute-start(bf16[100,2816]{1,0:T(8,128)(2,1)S(1)} %get-tuple-element.58), channel_id=1, source_target_pairs={{0,7},{1,0},{2,1},{3,2},{4,3},{5,4},{6,5},{7,6},{8,15},{9,8},{10,9... | collective-permute-start | bytes 1689608 | tf_op jit(solution)/shard_map/ppermute | solution.py:494

commit v3 on v2

--- a/solution.py
+++ b/solution.py
@@ -119,48 +119,61 @@
 
 
 def inverse_factors(grams, bond):
-    count = -(-bond // ROWS) * ROWS
-    shape = (count, LANES)
+    count = -(-bond // ROWS)
+    tile = (ROWS, LANES)
+    small_row, small_lane = index_of(tile, 0), index_of(tile, 1)
+
+    def splat(blocks, row):
+        return jnp.broadcast_to(blocks[0, row : row + 1, :], tile)
+
+    shape = (count * ROWS, LANES)
     row, lane = index_of(shape, 0), index_of(shape, 1)
+    eye = jnp.where(row == lane, 1.0, 0.0)
     inside = (row < bond) & (lane < bond)
-    eye = jnp.where(row == lane, 1.0, 0.0)
-    work = [jnp.where(inside, gram[:count], eye) for gram in grams]
+    work = [
+        jnp.where(inside, gram[: count * ROWS], eye).reshape(count, ROWS, LANES) for gram in grams
+    ]
     done = [[] for _ in grams]
-    for first in range(0, count, ROWS):
-        height = count - first
-        row, lane = index_of((height, LANES), 0), index_of((height, LANES), 1)
-        block = (lane >= first) & (lane < first + ROWS)
-        start = jnp.where(row == lane - first, 1.0, 0.0)
-        small_row, small_lane = index_of((ROWS, LANES), 0), index_of((ROWS, LANES), 1)
+    for block in range(count):
+        first = block * ROWS
+        height = count - block
+        lane = index_of((height, ROWS, LANES), 2)
+        fresh = (lane >= first) & (lane < first + ROWS)
+        start = jnp.where(small_row == small_lane - first, 1.0, 0.0)
+        start = jnp.concatenate(
+            [start[None], jnp.zeros((height - 1, ROWS, LANES), F32)], 0
+        ) if height > 1 else start[None]
         columns = []
         for n, matrix in enumerate(work):
             columns.append(
                 [
-                    jnp.broadcast_to(matrix[:, first + j : first + j + 1], (height, LANES))
+                    jnp.broadcast_to(matrix[:, :, first + j : first + j + 1], matrix.shape)
                     for j in range(ROWS)
                 ]
             )
-            work[n] = jnp.where(block, start, matrix)
-        pivots = [jnp.ones((ROWS, LANES), F32) for _ in work]
-        pivot = [column[0][:1, :] for column in columns]
+            work[n] = jnp.where(fresh, start, matrix)
+        pivots = [jnp.ones(tile, F32) for _ in work]
+        pivot = [splat(column[0], 0) for column in columns]
         for j in range(ROWS):
             for n in range(len(work)):
                 column = columns[n]
                 inverse = 1.0 / pivot[n]
                 pivots[n] = jnp.where(small_row == j, pivot[n], pivots[n])
+                below = jnp.where(small_row > j, column[j][0], 0.0)[None]
+                if height > 1:
+                    below = jnp.concatenate([below, column[j][1:]], 0)
                 if j + 1 < ROWS:
-                    at = slice(j + 1, j + 2)
-                    cross = column[j][at, :] * column[j + 1][j : j + 1, :]
-                    pivot[n] = column[j + 1][at, :] - cross * inverse
-                factor = jnp.where(row > j, column[j], 0.0) * inverse
+                    cross = splat(column[j], j + 1) * splat(column[j + 1], j)
+                    pivot[n] = splat(column[j + 1], j + 1) - cross * inverse
+                factor = below * inverse[None]
                 for later in range(j + 1, ROWS):
-                    column[later] = column[later] - factor * column[later][j : j + 1, :]
-                work[n] = work[n] - factor * work[n][j : j + 1, :]
+                    column[later] = column[later] - factor * splat(column[later], j)[None]
+                work[n] = work[n] - factor * splat(work[n], j)[None]
         for n in range(len(work)):
-            scaled = work[n][:ROWS] * lax.rsqrt(pivots[n])
+            scaled = work[n][0] * lax.rsqrt(pivots[n])
             done[n].append(jnp.where(small_lane <= small_row + first, scaled, 0.0))
-            work[n] = work[n][ROWS:]
-    tail = jnp.zeros((LANES - count, LANES), F32)
+            work[n] = work[n][1:]
+    tail = jnp.zeros((LANES - count * ROWS, LANES), F32)
     keep = (index_of((LANES, LANES), 0) < bond) & (index_of((LANES, LANES), 1) < bond)
     return [jnp.where(keep, jnp.concatenate(parts + [tail], 0), 0.0) for parts in done]
 
@@ -303,7 +316,7 @@
     top_right[...] = frame[:, frame.shape[1] - LANES :]
 
 
-def absorb_kernel(bond, site, first, rows_ref, edge, tensor, frame, *refs):
+def absorb_kernel(bond, site, first, counts, rows_ref, edge, tensor, frame, *refs):
     mixed_even, mixed_odd, spare_even, spare_odd, pushed_even, pushed_odd, last, result = refs[-8:]
     if first:
         corner, bottom, dense, wide = refs[:4]
@@ -347,21 +360,22 @@
                 jnp.concatenate(parts, 0).astype(BF16)
             )
 
-    def push(group, mixed, pushed, pair):
-        out = product(tensor[...], mixed[:, 2 * pair * LANES : (2 * pair + 2) * LANES])
-        for k in range(site):
-            parts = [
-                out[k * main : (k + 1) * main, side * LANES : (side + 1) * LANES]
-                for side in range(2)
-            ]
-            pushed[2 * pair * main : (2 * pair + 2) * main, k * LANES : (k + 1) * LANES] = (
-                jnp.concatenate(parts, 0).astype(BF16)
-            )
-        for side in range(2):
-            place = group * GROUP + 2 * pair + side
-            last[pl.ds(place, site, stride=LANES), :] = out[
-                site * main : site * main + site, side * LANES : (side + 1) * LANES
-            ]
+    def push(group, mixed, pushed, begin, count):
+        out = product(tensor[...], mixed[:, begin * LANES : (begin + count) * LANES])
+        for pair in range(count // 2):
+            sides = (2 * pair, 2 * pair + 1)
+            rows = slice((begin + 2 * pair) * main, (begin + 2 * pair + 2) * main)
+            for k in range(site):
+                parts = [
+                    out[k * main : (k + 1) * main, side * LANES : (side + 1) * LANES]
+                    for side in sides
+                ]
+                pushed[rows, k * LANES : (k + 1) * LANES] = jnp.concatenate(parts, 0).astype(BF16)
+            for side in sides:
+                place = group * GROUP + begin + side
+                last[pl.ds(place, site, stride=LANES), :] = out[
+                    site * main : site * main + site, side * LANES : (side + 1) * LANES
+                ]
 
     def cuts():
         step = -(-site // CUTS) // 2 * 2
@@ -376,14 +390,15 @@
     def stage(group, mixed, pushed, mixed_next, spare_next, pushed_before):
         frames = frames_of(jnp.minimum(group + 1, groups - 1))
         total = jnp.zeros((tall, LANES), F32)
-        pairs = GROUP // 2
         parts = cuts()
-        for n in range(pairs):
-            push(group, mixed, pushed, n)
-            for unit in range(n * units // pairs, (n + 1) * units // pairs):
+        begin = 0
+        for n, count in enumerate(counts):
+            push(group, mixed, pushed, begin, count)
+            begin += count
+            for unit in range(n * units // len(counts), (n + 1) * units // len(counts)):
                 mix(frames, mixed_next, spare_next, unit)
-            if n < CUTS:
-                total = total + product(pushed_before[:, parts[n]], frame_out[parts[n], :])
+            for part in parts[n * CUTS // len(counts) : (n + 1) * CUTS // len(counts)]:
+                total = total + product(pushed_before[:, part], frame_out[part, :])
         close(group - 1, total)
 
     frames = frames_of(0)
@@ -568,7 +583,7 @@
         spare = pltpu.VMEM((HALF_TILE * (-(-site // ROWS) * ROWS), LANES), F32)
         pushed = pltpu.VMEM((GROUP * main, tall), BF16)
         return call(
-            functools.partial(absorb_kernel, bond, site, first),
+            functools.partial(absorb_kernel, bond, site, first, (4, 4, 2) if first else (6, 4)),
             (rows_in, edge, tensor, frame) + more,
             [payload, wide] if first else [dense],
             ([] if first else [half_bf16])

time: 105 us -> 104 us (level)
  transfers between devices with their start and end apart: 9 -> 9, of which waited for: 3 -> 3; matrix products, arithmetic and copies ran while one was open for 0% -> 0% of each run, Pallas kernels for 74% -> 73%
where the time goes in v3:
time: 104 us
  Pallas kernels  80.7 us (78%)
  starting transfers between devices  10.7 us (10%)
  waiting for transfers between devices  8.19 us (8%)
  local copies, waits for them, and re-layouts  2.82 us (3%)
  between operations  1.54 us (1%)
    pallas_call x9, Pallas kernels, call(): pl.pallas_call(kernel, grid=(1,), in_specs=specs, out_specs=[block_of(out...  75.5 us
    ppermute x6, starting transfers between devices, shift(): return lax.ppermute(value, axis, pairs)  9.91 us
    ppermute x3, waiting for transfers between devices, shift_both(): return lax.ppermute(value, ('col', 'row'), pairs)  4.93 us
    pallas_call x2, Pallas kernels, arrange(): pl.pallas_call(functools.partial(arrange_kernel, len(held)), grid=(1,), i...  3.55 us
    ppermute x6, waiting for transfers between devices, shift(): return lax.ppermute(value, axis, pairs)  3.25 us
    unnamed x30, local copies, waits for them, and re-layouts  2.82 us
  transfers between devices with their start and end apart: 9, of which 3 were waited for; matrix products, arithmetic and copies ran while one was open for 0% of the time, Pallas kernels for 73%

profile of v3, /device:TPU:0, one launch (start us, length us, event | category | flops | bytes accessed | tf_op | source)
XLA Modules:
  0.0 103.9 jit_solution(9922831170762185174)
XLA Ops:
  0.6 0.0 copy-start.10
  0.6 0.0 copy-start.1
  0.7 0.0 copy-start.2
  0.7 0.0 copy-start.7
  0.7 0.0 copy-start.6
  0.7 0.0 copy-start.8
  0.7 3.6 %shard_map.208 = (bf16[100,2560]{1,0:T(8,128)(2,1)}, bf16[100,2560]{1,0:T(8,128)(2,1)}) custom-call(bf16[100,100]{1,0:T(8,128)(2,1)} %c1.1, bf16[100,2500]{1,0:T(8,128)(2,1)} %refs_0_.1, bf16[100,100]{1,0:T(8,128)(2,1)} %c4.1, bf16[100,2500]{1,0:T(8,128)(2,1)} %t3.1), custom_call_target="tpu_custom_call" | custom-call | flops 2000000000 | bytes 2000000 | tf_op jit(solution)/shard_map/pallas_call | solution.py:490
  4.3 4.5 %collective-permute-start = (bf16[100,2560]{1,0:T(8,128)(2,1)}, bf16[100,2560]{1,0:T(8,128)(2,1)S(1)}, u32[]{:S(2)}, u32[]{:S(2)}) collective-permute-start(bf16[100,2560]{1,0:T(8,128)(2,1)} %get-tuple-element.37.upper_packed), channel_id=1, source_target_pairs={{0,7},{1,0},{2,1},{3,2},{4,3},{5,4},{6,5},{7,6},{8,15},{9,8},{10,9... | collective-permute-start | bytes 1536008 | tf_op jit(solution)/shard_map/ppermute | solution.py:509
  8.8 0.0 collective-permute-start.1
  9.4 0.0 copy-done.10
  9.4 0.0 copy-done.1
  9.4 0.0 copy-done.2
  9.4 0.0 copy-done.7
  9.4 0.0 copy-done.6
  9.5 0.0 copy-done.8
  9.5 0.0 copy-start.4
  9.5 1.0 copy-done.4
  10.5 0.0 copy-start.5
  10.5 1.0 %copy-done.5 = bf16[100,2560]{1,0:T(8,128)(2,1)S(1)} copy-done((bf16[100,2560]{1,0:T(8,128)(2,1)S(1)}, bf16[100,2560]{1,0:T(8,128)(2,1)}, u32[]{:S(2)}) %copy-start.5) | copy-done | bytes 512024
  11.6 0.0 copy-start
  11.6 2.1 %shard_map.209 = (bf16[128,3200]{1,0:T(8,128)(2,1)S(1)}, bf16[3200,128]{1,0:T(8,128)(2,1)S(1)}, f32[3200,128]{1,0:T(8,128)S(1)}, bf16[3200,128]{1,0:T(8,128)(2,1...) custom-call(bf16[100,100]{1,0:T(8,128)(2,1)S(1)} %copy-done.10, ...), custom_call_target="tpu_custom_call" | custom-call | flops 2000000000 | bytes 2000000 | tf_op jit(solution)/shard_map/pallas_call | solution.py:490
  13.7 0.7 copy-done
  14.4 0.0 copy-start.3
  14.4 0.0 copy-start.12
  14.4 0.0 copy-start.14
  14.4 1.6 %shard_map.211.tensor.refs_2_ = bf16[625,625]{1,0:T(8,128)(2,1)S(1)} custom-call(s32[1]{0:T(128)} %bitcast.2.pattern, bf16[625,8,625]{2,1,0:T(8,128)(2,1)S(1)} %bitcast.3, bf16[3200,128]{1,0:T(8,128)(2,1)S(1)} %get-tuple-element.45.after.refs_3_.side), custom_call_target="tpu_custom_call" | custom-call | flops 2000000000 | bytes 2000000 | tf_op jit(solution)/shard_map/pallas_call | solution.py:544
  16.0 0.0 copy-done.3
  16.0 0.0 copy-done.12
  16.0 0.0 copy-done.14
  16.1 1.8 %shard_map.212 = (bf16[640,640]{1,0:T(8,128)(2,1)S(1)}, bf16[100,2500]{1,0:T(8,128)(2,1)S(1)}, bf16[100,2560]{1,0:T(8,128)(2,1)S(1)}, bf16[625,625]{1,0:T(8,128)(2,1)S(1)}) custom-call(bf16[625,625]{1,0:T(8,128)(2,1)S(1)} %shard_map.211.tensor.refs_2_, s32[640,1]{1,0:T(8,128)S(1)} %copy-done.12, s32[1,640]{1,0:T(1,128)S(1)} %copy-done.14, ...), custom_call_target="tpu_custom_call" | custom-call | flops 2000000000 | bytes 2000000 | tf_op jit(solution)/shard_map/pallas_call | solution.py:562
  17.9 0.1 collective-permute-start.8
  18.0 0.2 collective-permute-start.3
  18.2 1.0 collective-permute-start.4
  19.2 2.1 %collective-permute-done.upper_packed = bf16[100,2560]{1,0:T(8,128)(2,1)S(1)} collective-permute-done((bf16[100,2560]{1,0:T(8,128)(2,1)}, bf16[100,2560]{1,0:T(8,128)(2,1)S(1)}, u32[]{:S(2)}, u32[]{:S(2)}) %collective-permute-start) | collective-permute-done | bytes 512032 | tf_op jit(solution)/shard_map/ppermute | solution.py:509
  21.4 1.1 %collective-permute-done.1.lower_packed = bf16[100,2560]{1,0:T(8,128)(2,1)S(1)} collective-permute-done((bf16[100,2560]{1,0:T(8,128)(2,1)}, bf16[100,2560]{1,0:T(8,128)(2,1)S(1)}, u32[]{:S(2)}, u32[]{:S(2)}) %collective-permute-start.1) | collective-permute-done | bytes 512032 | tf_op jit(solution)/shard_map/ppermute | solution.py:509
  22.5 8.3 %shard_map.210 = (bf16[2656,128]{1,0:T(8,128)(2,1)S(1)}, bf16[3200,128]{1,0:T(8,128)(2,1)S(1)}, bf16[100,100]{1,0:T(8,128)(2,1)S(1)}, bf16[100,100]{1,0:T(8,128)(2,1)S(1)}) custom-call(bf16[100,2560]{1,0:T(8,128)(2,1)S(1)} %collective-permute-done.upper_packed, bf16[100,2560]{1,0:T(8,128)(2,1)S(1)} %collective-permute-done.1.lower_packed, ...), custom_call_target="tpu_custom_call" | custom-call | flops 8000000000 | bytes 8000000 | tf_op jit(solution)/shard_map/pallas_call | solution.py:490
  30.7 0.0 copy-start.9
  30.8 25.0 %shard_map.213 = (bf16[100,2816]{1,0:T(8,128)(2,1)S(1)}, bf16[128,3200]{1,0:T(8,128)(2,1)S(1)}) custom-call(bf16[2656,128]{1,0:T(8,128)(2,1)S(1)} %get-tuple-element.43.rows_ref, bf16[128,3200]{1,0:T(8,128)(2,1)S(1)} %get-tuple-element.44.edge, bf16[640,640]{1,0:T(8,128)(2,1)S(1)} %get-tuple-element.47.tensor, ...), custom_call_target="tpu_custom_call" | custom-call | flops 24999999488 | bytes 25000000 | tf_op jit(solution)/shard_map/pallas_call | solution.py:490
  55.8 0.1 collective-permute-start.2
  55.8 0.0 copy-done.9
  55.8 6.3 %shard_map.214 = (f32[112,128]{1,0:T(8,128)S(1)}, bf16[100,2688]{1,0:T(8,128)(2,1)S(1)}) custom-call(bf16[100,100]{1,0:T(8,128)(2,1)S(1)} %get-tuple-element.49.refs_0_.c1, bf16[128,3200]{1,0:T(8,128)(2,1)S(1)} %get-tuple-element.54.edge, f32[100,100]{1,0:T(8,128)S(1)} %copy-done.9, bf16[3200,128]{1,0:T(8,128)(2,1)S(1)} %get-tuple-element.45.after.refs_3_.side, ...), custom_call_target="tpu_custom_call" | custom-call | flops 5000000000 | bytes 5000000 | tf_op jit(solution)/shard_map/pallas_call | solution.py:490
  62.1 0.5 collective-permute-start.5
  62.6 0.0 collective-permute-done.4.t1
  62.6 0.0 copy-start.11
  62.6 0.0 copy-start.13
  62.6 0.6 collective-permute-start.7
  63.3 0.0 collective-permute-done.3.side_packed
  63.3 0.7 shard_map.215
  64.0 0.0 collective-permute-done.8.tensor
  64.0 0.0 copy-done.11
  64.0 0.0 copy-done.13
  64.0 1.7 %shard_map.218.tensor = bf16[640,640]{1,0:T(8,128)(2,1)S(1)} custom-call(bf16[625,625]{1,0:T(8,128)(2,1)S(1)} %collective-permute-done.8.tensor, s32[640,1]{1,0:T(8,128)S(1)} %copy-done.11, s32[1,640]{1,0:T(1,128)S(1)} %copy-done.13, f32[112,128]{1,0:T(8,128)S(1)} %get-tuple-element.56.after.refs_0_), custom_call_target="tpu_custom_call" | custom-call | flops 2000000000 | bytes 2000000 | tf_op jit(solution)/shard_map/pallas_call | solution.py:562
  65.7 4.9 %collective-permute-done.5.inverse_ref = f32[112,128]{1,0:T(8,128)S(1)} collective-permute-done((f32[112,128]{1,0:T(8,128)S(1)}, f32[112,128]{1,0:T(8,128)S(1)}, u32[]{:S(2)}, u32[]{:S(2)}) %collective-permute-start.5) | collective-permute-done | bytes 57376 | tf_op jit(solution)/shard_map/ppermute | solution.py:519
  70.7 0.0 collective-permute-done.2.payload
  70.7 3.1 %shard_map.216 = (bf16[2656,128]{1,0:T(8,128)(2,1)S(1)}, bf16[100,100]{1,0:T(8,128)(2,1)}, bf16[100,2816]{1,0:T(8,128)(2,1)S(1)}) custom-call(bf16[100,2816]{1,0:T(8,128)(2,1)S(1)} %collective-permute-done.2.payload, f32[3200,128]{1,0:T(8,128)S(1)} %get-tuple-element.57.side_sketch, f32[100,100]{1,0:T(8,128)S(1)} %copy-done.9, ...), custom_call_target="tpu_custom_call" | custom-call | flops 4000000000 | bytes 4000000 | tf_op jit(solution)/shard_map/pallas_call | solution.py:490
  73.8 3.7 %collective-permute-start.6 = (bf16[100,2816]{1,0:T(8,128)(2,1)S(1)}, bf16[100,2816]{1,0:T(8,128)(2,1)S(1)}, u32[]{:S(2)}, u32[]{:S(2)}) collective-permute-start(bf16[100,2816]{1,0:T(8,128)(2,1)S(1)} %get-tuple-element.58), channel_id=1, source_target_pairs={{0,7},{1,0},{2,1},{3,2},{4,3},{5,4},{6,5},{7,6},{8,15},{9,8},{10,9... | collective-permute-start | bytes 1689608 | tf_op jit(solution)/shard_map/ppermute | solution.py:509
  77.5 0.0 collective-permute-done.7.frame
  77.5 25.6 %shard_map.219 = bf16[100,2500]{1,0:T(8,128)(2,1)} custom-call(bf16[2656,128]{1,0:T(8,128)(2,1)S(1)} %get-tuple-element.64.rows_ref, bf16[128,3200]{1,0:T(8,128)(2,1)S(1)} %get-tuple-element.65.edge, bf16[640,640]{1,0:T(8,128)(2,1)S(1)} %shard_map.218.tensor, bf16[100,2688]{1,0:T(8,128)(2,1)S(1)} %collective-permute-done.7.frame), custom_call_target="tpu_custom_call" | custom-call | flops 24999999488 | bytes 25000000 | tf_op jit(solution)/shard_map/pallas_call | solution.py:490
  103.0 0.0 collective-permute-done.6.payload
  103.0 0.9 shard_map.217
Async XLA Ops:
  0.6 8.8 %copy-start.10 = (bf16[100,100]{1,0:T(8,128)(2,1)S(1)}, bf16[100,100]{1,0:T(8,128)(2,1)}, u32[]{:S(2)}) copy-start(bf16[100,100]{1,0:T(8,128)(2,1)} %c2.1) | copy-start | bytes 60004
  0.6 8.8 %copy-start.1 = (bf16[100,2500]{1,0:T(8,128)(2,1)S(1)}, bf16[100,2500]{1,0:T(8,128)(2,1)}, u32[]{:S(2)}) copy-start(bf16[100,2500]{1,0:T(8,128)(2,1)} %t2.1) | copy-start | bytes 1500004
  0.7 8.8 %copy-start.2 = (bf16[100,2500]{1,0:T(8,128)(2,1)S(1)}, bf16[100,2500]{1,0:T(8,128)(2,1)}, u32[]{:S(2)}) copy-start(bf16[100,2500]{1,0:T(8,128)(2,1)} %t4.1) | copy-start | bytes 1500004
  0.7 8.8 %copy-start.7 = (f32[100,100]{1,0:T(8,128)S(1)}, f32[100,100]{1,0:T(8,128)}, u32[]{:S(2)}) copy-start(f32[100,100]{1,0:T(8,128)} %below.3) | copy-start | bytes 120004
  0.7 8.8 %copy-start.6 = (f32[100,100]{1,0:T(8,128)S(1)}, f32[100,100]{1,0:T(8,128)}, u32[]{:S(2)}) copy-start(f32[100,100]{1,0:T(8,128)} %above.3) | copy-start | bytes 120004
  0.7 8.8 %copy-start.8 = (f32[100,100]{1,0:T(8,128)S(1)}, f32[100,100]{1,0:T(8,128)}, u32[]{:S(2)}) copy-start(f32[100,100]{1,0:T(8,128)} %right.3) | copy-start | bytes 120004
  4.3 17.1 %collective-permute-start = (bf16[100,2560]{1,0:T(8,128)(2,1)}, bf16[100,2560]{1,0:T(8,128)(2,1)S(1)}, u32[]{:S(2)}, u32[]{:S(2)}) collective-permute-start(bf16[100,2560]{1,0:T(8,128)(2,1)} %get-tuple-element.37.upper_packed), channel_id=1, source_target_pairs={{0,7},{1,0},{2,1},{3,2},{4,3},{5,4},{6,5},{7,6},{8,15},{9,8},{10,9... | collective-permute-start | bytes 1536008 | tf_op jit(solution)/shard_map/ppermute | solution.py:509
  8.8 13.7 %collective-permute-start.1 = (bf16[100,2560]{1,0:T(8,128)(2,1)}, bf16[100,2560]{1,0:T(8,128)(2,1)S(1)}, u32[]{:S(2)}, u32[]{:S(2)}) collective-permute-start(bf16[100,2560]{1,0:T(8,128)(2,1)} %get-tuple-element.38.lower_packed), channel_id=1, source_target_pairs={{0,1},{1,2},{2,3},{3,4},{4,5},{5,6},{6,7},{7,0},{8,9},{9,10},{10,1... | collective-permute-start | bytes 1536008 | tf_op jit(solution)/shard_map/ppermute | solution.py:509
  9.5 1.0 %copy-start.4 = (bf16[100,2560]{1,0:T(8,128)(2,1)S(1)}, bf16[100,2560]{1,0:T(8,128)(2,1)}, u32[]{:S(2)}) copy-start(bf16[100,2560]{1,0:T(8,128)(2,1)} %get-tuple-element.38.lower_packed) | copy-start | bytes 1536004
  10.5 1.0 %copy-start.5 = (bf16[100,2560]{1,0:T(8,128)(2,1)S(1)}, bf16[100,2560]{1,0:T(8,128)(2,1)}, u32[]{:S(2)}) copy-start(bf16[100,2560]{1,0:T(8,128)(2,1)} %get-tuple-element.37.upper_packed) | copy-start | bytes 1536004
  11.6 2.8 %copy-start = (bf16[8,625,625]{2,0,1:T(8,128)(2,1)S(1)}, bf16[8,625,625]{2,0,1:T(8,128)(2,1)}, u32[]{:S(2)}) copy-start(bf16[8,625,625]{2,0,1:T(8,128)(2,1)} %param.24) | copy-start | bytes 18750004
  14.4 1.7 %copy-start.3 = (bf16[100,2500]{1,0:T(8,128)(2,1)S(1)}, bf16[100,2500]{1,0:T(8,128)(2,1)}, u32[]{:S(2)}) copy-start(bf16[100,2500]{1,0:T(8,128)(2,1)} %refs_0_.1) | copy-start | bytes 1500004
  14.4 1.7 %copy-start.12 = (s32[640,1]{1,0:T(8,128)S(1)}, s32[640,1]{1,0:T(8,128)}, u32[]{:S(2)}) copy-start(s32[640,1]{1,0:T(8,128)} %constant.8.clone.rows) | copy-start | bytes 7684
  14.4 1.7 %copy-start.14 = (s32[1,640]{1,0:T(1,128)S(1)}, s32[1,640]{1,0:T(1,128)}, u32[]{:S(2)}) copy-start(s32[1,640]{1,0:T(1,128)} %constant.9.clone.columns) | copy-start | bytes 7684
  17.9 46.1 %collective-permute-start.8 = (bf16[625,625]{1,0:T(8,128)(2,1)S(1)}, bf16[625,625]{1,0:T(8,128)(2,1)S(1)}, u32[]{:S(2)}, u32[]{:S(2)}) collective-permute-start(bf16[625,625]{1,0:T(8,128)(2,1)S(1)} %get-tuple-element.66), channel_id=1, source_target_pairs={{0,1},{1,2},{2,3},{3,4},{4,5},{5,6},{6,7},{7,0},{8,9},{9,10},{10,1... | collective-permute-start | bytes 2343758 | tf_op jit(solution)/shard_map/ppermute | solution.py:509
  18.0 45.3 %collective-permute-start.3 = (bf16[100,2560]{1,0:T(8,128)(2,1)S(1)}, bf16[100,2560]{1,0:T(8,128)(2,1)S(1)}, u32[]{:S(2)}, u32[]{:S(2)}) collective-permute-start(bf16[100,2560]{1,0:T(8,128)(2,1)S(1)} %get-tuple-element.52), channel_id=1, source_target_pairs={{0,9},{1,10},{2,11},{3,12},{4,13},{5,14},{6,15},{7,8},{8,17},{9,18... | collective-permute-start | bytes 1536008 | tf_op jit(solution)/shard_map/ppermute | solution.py:519
  18.2 44.4 %collective-permute-start.4 = (bf16[100,2500]{1,0:T(8,128)(2,1)S(1)}, bf16[100,2500]{1,0:T(8,128)(2,1)S(1)}, u32[]{:S(2)}, u32[]{:S(2)}) collective-permute-start(bf16[100,2500]{1,0:T(8,128)(2,1)S(1)} %get-tuple-element.53), channel_id=1, source_target_pairs={{0,1},{1,2},{2,3},{3,4},{4,5},{5,6},{6,7},{7,0},{8,9},{9,10},{10,1... | collective-permute-start | bytes 1500008 | tf_op jit(solution)/shard_map/ppermute | solution.py:509
  30.7 25.1 %copy-start.9 = (f32[100,100]{1,0:T(8,128)S(1)}, f32[100,100]{1,0:T(8,128)}, u32[]{:S(2)}) copy-start(f32[100,100]{1,0:T(8,128)} %left.3) | copy-start | bytes 120004
  55.8 14.9 %collective-permute-start.2 = (bf16[100,2816]{1,0:T(8,128)(2,1)S(1)}, bf16[100,2816]{1,0:T(8,128)(2,1)S(1)}, u32[]{:S(2)}, u32[]{:S(2)}) collective-permute-start(bf16[100,2816]{1,0:T(8,128)(2,1)S(1)} %get-tuple-element.51), channel_id=1, source_target_pairs={{0,9},{1,10},{2,11},{3,12},{4,13},{5,14},{6,15},{7,8},{8,17},{9,18... | collective-permute-start | bytes 1689608 | tf_op jit(solution)/shard_map/ppermute | solution.py:519
  62.1 8.6 %collective-permute-start.5 = (f32[112,128]{1,0:T(8,128)S(1)}, f32[112,128]{1,0:T(8,128)S(1)}, u32[]{:S(2)}, u32[]{:S(2)}) collective-permute-start(f32[112,128]{1,0:T(8,128)S(1)} %get-tuple-element.56.after.refs_0_), channel_id=1, source_target_pairs={{0,9},{1,10},{2,11},{3,12},{4,13},{5,14},{6,15},{7,8},{8,17},{9,18... | collective-permute-start | bytes 172040 | tf_op jit(solution)/shard_map/ppermute | solution.py:519
  62.6 1.4 %copy-start.11 = (s32[640,1]{1,0:T(8,128)S(1)}, s32[640,1]{1,0:T(8,128)}, u32[]{:S(2)}) copy-start(s32[640,1]{1,0:T(8,128)} %constant.10.clone.rows) | copy-start | bytes 7684
  62.6 1.4 %copy-start.13 = (s32[1,640]{1,0:T(1,128)S(1)}, s32[1,640]{1,0:T(1,128)}, u32[]{:S(2)}) copy-start(s32[1,640]{1,0:T(1,128)} %constant.11.clone.columns) | copy-start | bytes 7684
  62.6 14.8 %collective-permute-start.7 = (bf16[100,2688]{1,0:T(8,128)(2,1)S(1)}, bf16[100,2688]{1,0:T(8,128)(2,1)S(1)}, u32[]{:S(2)}, u32[]{:S(2)}) collective-permute-start(bf16[100,2688]{1,0:T(8,128)(2,1)S(1)} %get-tuple-element.59), channel_id=1, source_target_pairs={{0,1},{1,2},{2,3},{3,4},{4,5},{5,6},{6,7},{7,0},{8,9},{9,10},{10,1... | collective-permute-start | bytes 1612808 | tf_op jit(solution)/shard_map/ppermute | solution.py:509
  73.8 29.3 %collective-permute-start.6 = (bf16[100,2816]{1,0:T(8,128)(2,1)S(1)}, bf16[100,2816]{1,0:T(8,128)(2,1)S(1)}, u32[]{:S(2)}, u32[]{:S(2)}) collective-permute-start(bf16[100,2816]{1,0:T(8,128)(2,1)S(1)} %get-tuple-element.58), channel_id=1, source_target_pairs={{0,7},{1,0},{2,1},{3,2},{4,3},{5,4},{6,5},{7,6},{8,15},{9,8},{10,9... | collective-permute-start | bytes 1689608 | tf_op jit(solution)/shard_map/ppermute | solution.py:509

commit v4 on v1

--- a/solution.py
+++ b/solution.py
@@ -11,6 +11,7 @@
 LANES = 128
 ROWS = 8
 HALF_TILE = 16
+TAIL = 16
 GROUP = 10
 CUTS = 4
 QUARTERS = 4
@@ -55,16 +56,17 @@
     shape = (LANES, LANES)
     row, lane = index_of(shape, 0), index_of(shape, 1)
     keep = (row < bond) & (lane < bond)
+    zero = jnp.zeros(shape, BF16)
     pieces = []
     for k in range(site):
         tile, offset = divmod(k * bond, LANES)
-        piece = ref[:, tile * LANES : (tile + 1) * LANES].astype(F32)
+        piece = ref[:, tile * LANES : (tile + 1) * LANES]
         if offset:
             piece = pltpu.roll(piece, LANES - offset, 1)
         if offset + bond > LANES:
-            more = ref[:, (tile + 1) * LANES : (tile + 2) * LANES].astype(F32)
+            more = ref[:, (tile + 1) * LANES : (tile + 2) * LANES]
             piece = jnp.where(lane < LANES - offset, piece, pltpu.roll(more, LANES - offset, 1))
-        pieces.append(jnp.where(keep, piece, 0.0).astype(BF16))
+        pieces.append(jnp.where(keep, piece, zero))
     return pieces
 
 
@@ -78,19 +80,20 @@
             shift = k * bond - begin
             piece = pltpu.roll(tiles[k], shift % LANES, 1) if shift % LANES else tiles[k]
             value = piece if value is None else jnp.where(lane >= shift, piece, value)
-        ref[:, begin : begin + LANES] = value.astype(ref.dtype)
+        ref[:, begin : begin + LANES] = value
 
 
 def pack(tiles, ref, bond):
     quarter = bond // QUARTERS
     lane = index_of((LANES, LANES), 1)
+    tiles = [tile.astype(BF16) for tile in tiles]
     for group in range(len(tiles) // (QUARTERS + 1)):
         first = group * (QUARTERS + 1)
         for m in range(QUARTERS):
             piece = pltpu.roll(tiles[first + QUARTERS], bond - m * quarter, 1)
             slot = group * QUARTERS + m
             value = jnp.where(lane < bond, tiles[first + m], piece)
-            ref[:, slot * LANES : (slot + 1) * LANES] = value.astype(ref.dtype)
+            ref[:, slot * LANES : (slot + 1) * LANES] = value
 
 
 def unpack(ref, bond, site):
@@ -98,16 +101,17 @@
     shape = (LANES, LANES)
     row, lane = index_of(shape, 0), index_of(shape, 1)
     keep = (row < bond) & (lane < bond)
+    zero = jnp.zeros(shape, BF16)
     tiles = []
     for group in range(site // (QUARTERS + 1)):
         last = None
         for m in range(QUARTERS):
             slot = group * QUARTERS + m
-            value = ref[:, slot * LANES : (slot + 1) * LANES].astype(F32)
-            tiles.append(jnp.where(keep, value, 0.0).astype(BF16))
+            value = ref[:, slot * LANES : (slot + 1) * LANES]
+            tiles.append(jnp.where(keep, value, zero))
             piece = pltpu.roll(value, LANES - bond + m * quarter, 1)
             last = piece if last is None else jnp.where(lane >= m * quarter, piece, last)
-        tiles.append(jnp.where(keep, last, 0.0).astype(BF16))
+        tiles.append(jnp.where(keep, last, zero))
     return tiles
 
 
@@ -161,10 +165,12 @@
     high[...], low[...] = halves(values)
 
 
-def gram_of(high, low):
-    both = product(high[...], jnp.concatenate([high[...], low[...]], 1), TN)
-    mixed = both[:, LANES:]
-    return both[:, :LANES] + mixed + mixed.T
+def gram_and_overlap(other, high, low):
+    left = jnp.concatenate([high[...], other], 1)
+    both = product(left, jnp.concatenate([high[...], low[...]], 1), TN)
+    mixed = both[:LANES, LANES:]
+    gram = both[:LANES, :LANES] + mixed + mixed.T
+    return gram, both[LANES:, :LANES] + both[LANES:, LANES:]
 
 
 def overlap(other, high, low):
@@ -203,21 +209,20 @@
         if k < main:
             plain[pl.ds(k, bond_rows, stride=main), :] = tile
         else:
-            for group in range(tail.shape[0] // HALF_TILE):
-                begin = group * HALF_TILE
+            for group in range(tail.shape[0] // TAIL):
+                begin = group * TAIL
                 tail[begin : begin + GROUP, :] = tile[group * GROUP : (group + 1) * GROUP]
     rows_ref[: plain.shape[0], :] = plain[...].astype(BF16)
     rows_ref[plain.shape[0] :, :] = tail[...].astype(BF16)
 
 
-def halves_kernel(bond, site, c1, t1, c4, t3, upper_packed, lower_packed):
-    for corner, edge, packed in ((c1, t1, upper_packed), (c4, t3, lower_packed)):
-        pack(half_tiles(square_of(corner, bond).astype(BF16), spread(edge, bond, site)), packed, bond)
+def half_kernel(bond, site, corner, edge, packed):
+    pack(half_tiles(square_of(corner, bond).astype(BF16), spread(edge, bond, site)), packed, bond)
 
 
 def prepare_kernel(
-    bond, site, c2, t2, t4, t1, above, below, right, upper_packed, lower_packed,
-    t4_wide, t1_out, upper, upper_sketch, lower, lower_sketch, side_packed, side, side_sketch,
+    bond, site, c2, t2, t4, t1, above, below, upper_packed, lower_packed,
+    t4_wide, t1_out, upper, upper_sketch, lower, lower_sketch, side_packed, side,
 ):
     t1_out[...] = t1[...]
     tiles = half_tiles(square_of(c2, bond).astype(BF16), spread(t2, bond, site))
@@ -227,7 +232,6 @@
     fill(lower, unpack(lower_packed, bond, site))
     upper_sketch[...] = sketched(upper[...], square_of(above, bond))
     lower_sketch[...] = sketched(lower[...], square_of(below, bond))
-    side_sketch[...] = sketched(side[...], square_of(right, bond))
     for k, piece in enumerate(spread(t4, bond, site)):
         t4_wide[:, k * LANES : (k + 1) * LANES] = piece
 
@@ -240,10 +244,9 @@
     store_halves(lower_sketch[...] + sketched(stack[...], square_of(above, bond)), under, under_low)
     fill(stack, unpack(lower_packed, bond, site))
     store_halves(upper_sketch[...] + sketched(stack[...], square_of(below, bond)), over, over_low)
-    grams = [gram_of(over, over_low), gram_of(under, under_low)]
-    mixed_over = overlap(upper[...], over, over_low)
-    mixed_under = overlap(lower[...], under, under_low)
-    inverse_over, inverse_under = inverse_factors(grams, bond)
+    gram_over, mixed_over = gram_and_overlap(upper[...], over, over_low)
+    gram_under, mixed_under = gram_and_overlap(lower[...], under, under_low)
+    inverse_over, inverse_under = inverse_factors([gram_over, gram_under], bond)
     store_frame_rows(over, over_low, inverse_over, rows_ref, plain, tail, site)
     frame_out[...] = frame_from(under, under_low, inverse_under).astype(BF16)
     corner_top[...] = scaled_corner(product_split(inverse_over, mixed_over, NT), bond)
@@ -251,13 +254,15 @@
 
 
 def horizontal_kernel(
-    bond, site, c1, edge, left, side, side_sketch, inverse_ref, frame_out, half, total, total_low
+    bond, site, c1, edge, left, right, side, inverse_ref, frame_out, half, total, total_low
 ):
     corner = square_of(c1, bond).T.astype(BF16)
     fill(half, half_tiles(corner, [edge[:, k * LANES : (k + 1) * LANES] for k in range(site)]))
-    store_halves(side_sketch[...] + sketched(half[...], square_of(left, bond)), total, total_low)
-    mixed = overlap(side[...], total, total_low)
-    (inverse,) = inverse_factors([gram_of(total, total_low)], bond)
+    stacks = jnp.concatenate([half[...], half[...], side[...], side[...]], 1)
+    sketches = halves(square_of(left, bond)) + halves(square_of(right, bond))
+    store_halves(product(stacks, jnp.concatenate(sketches, 0)), total, total_low)
+    gram, mixed = gram_and_overlap(side[...], total, total_low)
+    (inverse,) = inverse_factors([gram], bond)
     inverse_ref[...] = inverse[: inverse_ref.shape[0]]
     frame = frame_from(total, total_low, inverse)
     pack([frame[k * LANES : (k + 1) * LANES, :] for k in range(site)], frame_out, bond)
@@ -296,7 +301,7 @@
     top_right[...] = frame[:, frame.shape[1] - LANES :]
 
 
-def absorb_kernel(bond, site, first, rows_ref, edge, tensor, frame, *refs):
+def absorb_kernel(bond, site, first, counts, rows_ref, edge, tensor, frame, *refs):
     mixed_even, mixed_odd, spare_even, spare_odd, pushed_even, pushed_odd, last, result = refs[-8:]
     if first:
         corner, bottom, dense, wide = refs[:4]
@@ -307,7 +312,7 @@
     main = site - 1
     groups = bond // GROUP
     tall = GROUP * main
-    slot = spare_even.shape[0] // HALF_TILE
+    slot = spare_even.shape[0] // TAIL
     spare_even[...] = jnp.zeros_like(spare_even)
     spare_odd[...] = jnp.zeros_like(spare_odd)
     ahead = tall + bond * main
@@ -315,8 +320,8 @@
 
     def frames_of(group):
         body = rows_ref[pl.ds(pl.multiple_of(group * tall, tall), tall), :]
-        begin = rows_ref.shape[0] - groups * HALF_TILE + group * HALF_TILE
-        tail = rows_ref[pl.ds(pl.multiple_of(begin, HALF_TILE), HALF_TILE), :]
+        begin = rows_ref.shape[0] - groups * TAIL + group * TAIL
+        tail = rows_ref[pl.ds(pl.multiple_of(begin, TAIL), TAIL), :]
         return jnp.concatenate([body, tail], 0)
 
     def mix(frames, mixed, spare, unit):
@@ -325,7 +330,7 @@
         both = product(frames, edge[:, j * LANES : (j + sides) * LANES])
         for side in range(sides):
             lanes = slice(side * LANES, (side + 1) * LANES)
-            spare[pl.ds(j + side, HALF_TILE, stride=slot), :] = both[tall:, lanes]
+            spare[pl.ds(j + side, TAIL, stride=slot), :] = both[tall:, lanes]
         for p in range(GROUP):
             parts = [
                 both[p * main : (p + 1) * main, side * LANES : (side + 1) * LANES]
@@ -340,21 +345,22 @@
                 jnp.concatenate(parts, 0).astype(BF16)
             )
 
-    def push(group, mixed, pushed, pair):
-        out = product(tensor[...], mixed[:, 2 * pair * LANES : (2 * pair + 2) * LANES])
-        for k in range(site):
-            parts = [
-                out[k * main : (k + 1) * main, side * LANES : (side + 1) * LANES]
-                for side in range(2)
-            ]
-            pushed[2 * pair * main : (2 * pair + 2) * main, k * LANES : (k + 1) * LANES] = (
-                jnp.concatenate(parts, 0).astype(BF16)
-            )
-        for side in range(2):
-            place = group * GROUP + 2 * pair + side
-            last[pl.ds(place, site, stride=LANES), :] = out[
-                site * main : site * main + site, side * LANES : (side + 1) * LANES
-            ]
+    def push(group, mixed, pushed, begin, count):
+        out = product(tensor[...], mixed[:, begin * LANES : (begin + count) * LANES])
+        for pair in range(count // 2):
+            sides = (2 * pair, 2 * pair + 1)
+            rows = slice((begin + 2 * pair) * main, (begin + 2 * pair + 2) * main)
+            for k in range(site):
+                parts = [
+                    out[k * main : (k + 1) * main, side * LANES : (side + 1) * LANES]
+                    for side in sides
+                ]
+                pushed[rows, k * LANES : (k + 1) * LANES] = jnp.concatenate(parts, 0).astype(BF16)
+            for side in sides:
+                place = group * GROUP + begin + side
+                last[pl.ds(place, site, stride=LANES), :] = out[
+                    site * main : site * main + site, side * LANES : (side + 1) * LANES
+                ]
 
     def cuts():
         step = -(-site // CUTS) // 2 * 2
@@ -369,14 +375,15 @@
     def stage(group, mixed, pushed, mixed_next, spare_next, pushed_before):
         frames = frames_of(jnp.minimum(group + 1, groups - 1))
         total = jnp.zeros((tall, LANES), F32)
-        pairs = GROUP // 2
         parts = cuts()
-        for n in range(pairs):
-            push(group, mixed, pushed, n)
-            for unit in range(n * units // pairs, (n + 1) * units // pairs):
+        begin = 0
+        for n, count in enumerate(counts):
+            push(group, mixed, pushed, begin, count)
+            begin += count
+            for unit in range(n * units // len(counts), (n + 1) * units // len(counts)):
                 mix(frames, mixed_next, spare_next, unit)
-            if n < CUTS:
-                total = total + product(pushed_before[:, parts[n]], frame_out[parts[n], :])
+            for part in parts[n * CUTS // len(counts) : (n + 1) * CUTS // len(counts)]:
+                total = total + product(pushed_before[:, part], frame_out[part, :])
         close(group - 1, total)
 
     frames = frames_of(0)
@@ -400,17 +407,17 @@
     for tile in tiles[1:]:
         squares = squares + tile * tile
     scale = 1.0 / jnp.sqrt(jnp.sum(squares) / (bond * bond * site) + 1e-06)
-    tiles = [tile * scale for tile in tiles]
+    tiles = [(tile * scale).astype(BF16) for tile in tiles]
     gather_dense(tiles, dense, bond)
     if first:
         for k, tile in enumerate(tiles):
-            wide[:, k * LANES : (k + 1) * LANES] = tile.astype(BF16)
+            wide[:, k * LANES : (k + 1) * LANES] = tile
         start = dense.shape[1] - 2 * LANES
         dense[:, start : start + LANES] = square_of(corner, bond).astype(BF16)
         dense[:, start + LANES :] = square_of(bottom, bond).astype(BF16)
 
 
-def pick_kernel(pattern, tensors, out, *tiles):
+def pick_kernel(pattern, tensors, after, out, *tiles):
     height, count, width = tensors.shape
     values = tensors[...].astype(F32).reshape(height * count, width)
     for n, tile in enumerate(tiles):
@@ -501,7 +508,7 @@
     tall = site * LANES
     bond_rows = -(-bond // ROWS) * ROWS
     body_rows = bond_rows * (site - 1)
-    tail_rows = bond // GROUP * HALF_TILE
+    tail_rows = bond // GROUP * TAIL
     frame_rows = shape_of((body_rows + tail_rows, LANES))
     packed = shape_of((bond, site // (QUARTERS + 1) * QUARTERS * LANES))
     dense = shape_of((bond, site * bond))
@@ -514,7 +521,7 @@
     frame_scratch = [pltpu.VMEM((body_rows, LANES), F32), pltpu.VMEM((tail_rows, LANES), F32)]
     rows, columns = places(site)
 
-    def pick(index):
+    def pick(index, after):
         count = tensors.shape[0]
         return pl.pallas_call(
             pick_kernel,
@@ -522,13 +529,14 @@
             in_specs=[
                 pl.BlockSpec(memory_space=pltpu.SMEM),
                 pl.BlockSpec((LANES, count, square), lambda i: (i, 0, 0)),
+                pl.BlockSpec(memory_space=pl.ANY),
             ],
             out_specs=pl.BlockSpec((LANES, square), lambda i: (i, 0)),
             out_shape=shape_of((square, square)),
             scratch_shapes=[pltpu.VMEM((LANES * count, LANES), F32)] * -(-square // LANES),
             compiler_params=pltpu.CompilerParams(vmem_limit_bytes=16 * MIB),
             cost_estimate=cost(2),
-        )(index, tensors.transpose(1, 0, 2))
+        )(index, tensors.transpose(1, 0, 2), after)
 
     def arrange(which, tensor, after):
         height, depth = rows.shape[1], columns.shape[1]
@@ -550,10 +558,10 @@
     def absorb(first, rows_in, edge, tensor, frame, *more):
         main = site - 1
         mixed = pltpu.VMEM((tensor.shape[1], GROUP * LANES), BF16)
-        spare = pltpu.VMEM((HALF_TILE * (-(-site // ROWS) * ROWS), LANES), F32)
+        spare = pltpu.VMEM((TAIL * (-(-site // ROWS) * ROWS), LANES), F32)
         pushed = pltpu.VMEM((GROUP * main, tall), BF16)
         return call(
-            functools.partial(absorb_kernel, bond, site, first),
+            functools.partial(absorb_kernel, bond, site, first, (2,) * (GROUP // 2)),
             (rows_in, edge, tensor, frame) + more,
             [payload, wide] if first else [dense],
             ([] if first else [half_bf16])
@@ -563,27 +571,24 @@
             25,
         )
 
-    upper_packed, lower_packed = call(
-        functools.partial(halves_kernel, bond, site),
-        (c1, t1, c4, t3),
-        [packed, packed],
-        [],
-        60,
-        2,
-    )
+    def half_of(corner, edge):
+        return call(functools.partial(half_kernel, bond, site), (corner, edge), [packed], [], 60, 2)[0]
+
+    upper_packed = half_of(c1, t1)
     upper_next = shift(upper_packed, "row", -1)
+    lower_packed = half_of(c4, t3)
     lower_back = shift(lower_packed, "row", 1)
-    tensor = pick(pattern.reshape(1))
-    tensor_left = arrange(0, tensor, upper_packed)
     prepared = call(
         functools.partial(prepare_kernel, bond, site),
-        (c2, t2, t4, t1, above, below, right, upper_packed, lower_packed),
-        [wide, dense, stack, stack_f32, stack, stack_f32, packed, stack, stack_f32],
+        (c2, t2, t4, t1, above, below, upper_packed, lower_packed),
+        [wide, dense, stack, stack_f32, stack, stack_f32, packed, stack],
         [],
         16,
         2,
     )
-    t4_wide, t1_held, upper, upper_sketch, lower, lower_sketch, side_packed, side, side_sketch = prepared
+    t4_wide, t1_held, upper, upper_sketch, lower, lower_sketch, side_packed, side = prepared
+    tensor = pick(pattern.reshape(1), side)
+    tensor_left = arrange(0, tensor, side)
     t1_back = shift(t1_held, "row", 1)
     side_back = shift_both(side_packed, 1, 1)
     tensor_back = shift(tensor, "row", 1)
@@ -599,7 +604,7 @@
     left_back = shift_both(left_new, 1, 1)
     inverse, frame_right = call(
         functools.partial(horizontal_kernel, bond, site),
-        (corner_top, edge_wide, left, side, side_sketch),
+        (corner_top, edge_wide, left, right, side),
         [shape_of((-(-bond // HALF_TILE) * HALF_TILE, LANES), F32), shape_of((bond, packed.shape[1] + LANES))],
         [half_bf16] * 3,
         16,

time: 103 us -> 105 us (1.019)
  waiting for transfers between devices: 8.65 us -> 3.71 us
  starting transfers between devices: 10.3 us -> 15.1 us
  Pallas kernels: 80 us -> 81.8 us
    ppermute x3, waiting for transfers between devices: 5.38 us -> 1.93 us  [shift_both(): return lax.ppermute(value, ('col', 'row'), pairs)]
    ppermute x3, starting transfers between devices: 0.62 us -> 3.93 us  [shift_both(): return lax.ppermute(value, ('col', 'row'), pairs)]
    pallas_call x9 -> x10, Pallas kernels: 74.9 us -> 76.8 us  [call(): pl.pallas_call(kernel, grid=(1,), in_specs=specs, out_specs=[block_of(out...]
    ppermute x6, waiting for transfers between devices: 3.27 us -> 1.78 us  [shift(): return lax.ppermute(value, axis, pairs)]
    ppermute x6, starting transfers between devices: 9.71 us -> 11.2 us  [shift(): return lax.ppermute(value, axis, pairs)]
  transfers between devices with their start and end apart: 9 -> 9, of which waited for: 3 -> 3; matrix products, arithmetic and copies ran while one was open for 0% -> 0% of each run, Pallas kernels for 73% -> 75%
where the time goes in v4:
time: 105 us
  Pallas kernels  81.8 us (78%)
  starting transfers between devices  15.1 us (14%)
  waiting for transfers between devices  3.71 us (4%)
  local copies, waits for them, and re-layouts  2.45 us (2%)
  between operations  1.5 us (1%)
    pallas_call x10, Pallas kernels, call(): pl.pallas_call(kernel, grid=(1,), in_specs=specs, out_specs=[block_of(out...  76.8 us
    ppermute x6, starting transfers between devices, shift(): return lax.ppermute(value, axis, pairs)  11.2 us
    ppermute x3, starting transfers between devices, shift_both(): return lax.ppermute(value, ('col', 'row'), pairs)  3.93 us
    pallas_call x2, Pallas kernels, arrange(): pl.pallas_call(arrange_kernel, in_specs=[vmem, vmem, vmem, pl.BlockSpec(m...  3.4 us
    unnamed x30, local copies, waits for them, and re-layouts  2.45 us
  transfers between devices with their start and end apart: 9, of which 3 were waited for; matrix products, arithmetic and copies ran while one was open for 0% of the time, Pallas kernels for 75%

profile of v4, /device:TPU:0, one launch (start us, length us, event | category | flops | bytes accessed | tf_op | source)
XLA Modules:
  0.0 104.6 jit_solution(13469843409134483750)
XLA Ops:
  0.6 2.5 %shard_map.208.upper_packed = bf16[100,2560]{1,0:T(8,128)(2,1)} custom-call(bf16[100,100]{1,0:T(8,128)(2,1)} %corner.2, bf16[100,2500]{1,0:T(8,128)(2,1)} %t1.1), custom_call_target="tpu_custom_call" | custom-call | flops 2000000000 | bytes 2000000 | tf_op jit(solution)/shard_map/pallas_call | solution.py:472
  3.2 0.0 copy-start.1
  3.2 0.0 copy-start.2
  3.2 0.0 copy-start.3
  3.2 0.0 copy-start.4
  3.2 0.0 copy-start.6
  3.2 0.0 copy-start.7
  3.2 0.0 copy-start.10
  3.2 4.5 %collective-permute-start = (bf16[100,2560]{1,0:T(8,128)(2,1)}, bf16[100,2560]{1,0:T(8,128)(2,1)S(1)}, u32[]{:S(2)}, u32[]{:S(2)}) collective-permute-start(bf16[100,2560]{1,0:T(8,128)(2,1)} %shard_map.208.upper_packed), channel_id=1, source_target_pairs={{0,7},{1,0},{2,1},{3,2},{4,3},{5,4},{6,5},{7,6},{8,15},{9,8},{10,9... | collective-permute-start | bytes 1536008 | tf_op jit(solution)/shard_map/ppermute | solution.py:491
  7.8 2.5 %shard_map.209.lower_packed = bf16[100,2560]{1,0:T(8,128)(2,1)} custom-call(bf16[100,100]{1,0:T(8,128)(2,1)} %corner.3, bf16[100,2500]{1,0:T(8,128)(2,1)} %edge.3), custom_call_target="tpu_custom_call" | custom-call | flops 2000000000 | bytes 2000000 | tf_op jit(solution)/shard_map/pallas_call | solution.py:472
  10.3 0.0 collective-permute-start.1
  11.0 0.0 copy-done.1
  11.0 0.0 copy-done.2
  11.0 0.0 copy-done.3
  11.0 0.0 copy-done.4
  11.0 0.0 copy-done.6
  11.0 0.0 copy-done.7
  11.0 0.0 copy-done.10
  11.0 0.0 copy-start.5
  11.1 1.0 copy-done.5
  12.1 0.0 copy-start
  12.1 1.7 %shard_map.210 = (bf16[128,3200]{1,0:T(8,128)(2,1)S(1)}, bf16[100,2500]{1,0:T(8,128)(2,1)S(1)}, bf16[3200,128]{1,0:T(8,128)(2,1)S(1)}, f32[3200,128]{1,0:T(8,128...) custom-call(bf16[100,100]{1,0:T(8,128)(2,1)S(1)} %copy-done.10, ...), custom_call_target="tpu_custom_call" | custom-call | flops 2000000000 | bytes 2000000 | tf_op jit(solution)/shard_map/pallas_call | solution.py:472
  13.8 1.1 %copy-done = bf16[8,625,625]{2,0,1:T(8,128)(2,1)S(1)} copy-done((bf16[8,625,625]{2,0,1:T(8,128)(2,1)S(1)}, bf16[8,625,625]{2,0,1:T(8,128)(2,1)}, u32[]{:S(2)}) %copy-start) | copy-done | bytes 6250024
  14.9 0.0 copy-start.12
  14.9 0.0 copy-start.14
  14.9 1.6 %shard_map.212.tensor = bf16[625,625]{1,0:T(8,128)(2,1)S(1)} custom-call(s32[1]{0:T(128)} %bitcast.2.pattern, bf16[625,8,625]{2,1,0:T(8,128)(2,1)S(1)} %bitcast.3, bf16[3200,128]{1,0:T(8,128)(2,1)S(1)} %get-tuple-element.37.after.side), custom_call_target="tpu_custom_call" | custom-call | flops 2000000000 | bytes 2000000 | tf_op jit(solution)/shard_map/pallas_call | solution.py:526
  16.6 0.1 collective-permute-start.8
  16.6 0.2 collective-permute-start.3
  16.9 1.2 %collective-permute-start.4 = (bf16[100,2500]{1,0:T(8,128)(2,1)S(1)}, bf16[100,2500]{1,0:T(8,128)(2,1)S(1)}, u32[]{:S(2)}, u32[]{:S(2)}) collective-permute-start(bf16[100,2500]{1,0:T(8,128)(2,1)S(1)} %get-tuple-element.43), channel_id=1, source_target_pairs={{0,1},{1,2},{2,3},{3,4},{4,5},{5,6},{6,7},{7,0},{8,9},{9,10},{10,1... | collective-permute-start | bytes 1500008 | tf_op jit(solution)/shard_map/ppermute | solution.py:491
  18.0 0.0 copy-done.12
  18.0 0.0 copy-done.14
  18.0 1.7 %shard_map.213.tensor = bf16[640,640]{1,0:T(8,128)(2,1)S(1)} custom-call(bf16[625,625]{1,0:T(8,128)(2,1)S(1)} %shard_map.212.tensor, s32[640,1]{1,0:T(8,128)S(1)} %copy-done.12, s32[1,640]{1,0:T(1,128)S(1)} %copy-done.14, bf16[3200,128]{1,0:T(8,128)(2,1)S(1)} %get-tuple-element.37.after.side), custom_call_target="tpu_custom_call" | custom-call | flops 2000000000 | bytes 2000000 | tf_op jit(solution)/shard_map/pallas_call | solution.py:544
  19.7 0.2 collective-permute-done.upper_packed
  20.0 1.5 %collective-permute-done.1.lower_packed = bf16[100,2560]{1,0:T(8,128)(2,1)S(1)} collective-permute-done((bf16[100,2560]{1,0:T(8,128)(2,1)}, bf16[100,2560]{1,0:T(8,128)(2,1)S(1)}, u32[]{:S(2)}, u32[]{:S(2)}) %collective-permute-start.1) | collective-permute-done | bytes 512032 | tf_op jit(solution)/shard_map/ppermute | solution.py:491
  21.5 7.8 %shard_map.211 = (bf16[2656,128]{1,0:T(8,128)(2,1)S(1)}, bf16[3200,128]{1,0:T(8,128)(2,1)S(1)}, bf16[100,100]{1,0:T(8,128)(2,1)S(1)}, bf16[100,100]{1,0:T(8,128)(2,1)S(1)}) custom-call(bf16[100,2560]{1,0:T(8,128)(2,1)S(1)} %collective-permute-done.upper_packed, bf16[100,2560]{1,0:T(8,128)(2,1)S(1)} %collective-permute-done.1.lower_packed, ...), custom_call_target="tpu_custom_call" | custom-call | flops 8000000000 | bytes 8000000 | tf_op jit(solution)/shard_map/pallas_call | solution.py:472
  29.3 0.0 copy-start.8
  29.3 0.0 copy-start.9
  29.3 25.1 %shard_map.214 = (bf16[100,2816]{1,0:T(8,128)(2,1)S(1)}, bf16[128,3200]{1,0:T(8,128)(2,1)S(1)}) custom-call(bf16[2656,128]{1,0:T(8,128)(2,1)S(1)} %get-tuple-element.35.rows_ref, bf16[128,3200]{1,0:T(8,128)(2,1)S(1)} %get-tuple-element.36.edge, bf16[640,640]{1,0:T(8,128)(2,1)S(1)} %shard_map.213.tensor, bf16[3200,128]{1,0:T(8,128)(2,1)S(1)} %get-tuple-element.38.frame, ...), custom_call_target="tpu_custom_call" | custom-call | flops 24999999488 | bytes 25000000 | tf_op jit(solution)/shard_map/pallas_call | solution.py:472
  54.5 0.3 collective-permute-start.2
  54.8 0.0 copy-done.8
  54.8 0.0 copy-done.9
  54.8 6.9 %shard_map.215 = (f32[112,128]{1,0:T(8,128)S(1)}, bf16[100,2688]{1,0:T(8,128)(2,1)S(1)}) custom-call(bf16[100,100]{1,0:T(8,128)(2,1)S(1)} %get-tuple-element.39.refs_0_.c1, bf16[128,3200]{1,0:T(8,128)(2,1)S(1)} %get-tuple-element.44.edge, f32[100,100]{1,0:T(8,128)S(1)} %copy-done.9, f32[100,100]{1,0:T(8,128)S(1)} %copy-done.8, ...), custom_call_target="tpu_custom_call" | custom-call | flops 5000000000 | bytes 5000000 | tf_op jit(solution)/shard_map/pallas_call | solution.py:472
  61.7 3.4 %collective-permute-start.5 = (f32[112,128]{1,0:T(8,128)S(1)}, f32[112,128]{1,0:T(8,128)S(1)}, u32[]{:S(2)}, u32[]{:S(2)}) collective-permute-start(f32[112,128]{1,0:T(8,128)S(1)} %get-tuple-element.45.after), channel_id=1, source_target_pairs={{0,9},{1,10},{2,11},{3,12},{4,13},{5,14},{6,15},{7,8},{8,17},{9,18... | collective-permute-start | bytes 172040 | tf_op jit(solution)/shard_map/ppermute | solution.py:501
  65.1 0.0 collective-permute-done.4.t1
  65.1 0.0 copy-start.11
  65.1 0.0 copy-start.13
  65.1 0.0 collective-permute-start.7
  65.1 0.0 collective-permute-done.3.side_packed
  65.1 0.7 shard_map.216
  65.8 0.0 collective-permute-done.8.tensor
  65.8 0.2 copy-done.11
  66.0 0.0 copy-done.13
  66.0 1.7 %shard_map.219.tensor = bf16[640,640]{1,0:T(8,128)(2,1)S(1)} custom-call(bf16[625,625]{1,0:T(8,128)(2,1)S(1)} %collective-permute-done.8.tensor, s32[640,1]{1,0:T(8,128)S(1)} %copy-done.11, s32[1,640]{1,0:T(1,128)S(1)} %copy-done.13, f32[112,128]{1,0:T(8,128)S(1)} %get-tuple-element.45.after), custom_call_target="tpu_custom_call" | custom-call | flops 2000000000 | bytes 2000000 | tf_op jit(solution)/shard_map/pallas_call | solution.py:544
  67.7 1.9 %collective-permute-done.5.inverse_ref = f32[112,128]{1,0:T(8,128)S(1)} collective-permute-done((f32[112,128]{1,0:T(8,128)S(1)}, f32[112,128]{1,0:T(8,128)S(1)}, u32[]{:S(2)}, u32[]{:S(2)}) %collective-permute-start.5) | collective-permute-done | bytes 57376 | tf_op jit(solution)/shard_map/ppermute | solution.py:501
  69.7 0.0 collective-permute-done.2.payload
  69.7 3.1 %shard_map.217 = (bf16[2656,128]{1,0:T(8,128)(2,1)S(1)}, bf16[100,100]{1,0:T(8,128)(2,1)}, bf16[100,2816]{1,0:T(8,128)(2,1)S(1)}) custom-call(bf16[100,2816]{1,0:T(8,128)(2,1)S(1)} %collective-permute-done.2.payload, f32[3200,128]{1,0:T(8,128)S(1)} %get-tuple-element.46.side_sketch, f32[100,100]{1,0:T(8,128)S(1)} %copy-done.9, ...), custom_call_target="tpu_custom_call" | custom-call | flops 4000000000 | bytes 4000000 | tf_op jit(solution)/shard_map/pallas_call | solution.py:472
  72.8 5.4 %collective-permute-start.6 = (bf16[100,2816]{1,0:T(8,128)(2,1)S(1)}, bf16[100,2816]{1,0:T(8,128)(2,1)S(1)}, u32[]{:S(2)}, u32[]{:S(2)}) collective-permute-start(bf16[100,2816]{1,0:T(8,128)(2,1)S(1)} %get-tuple-element.47), channel_id=1, source_target_pairs={{0,7},{1,0},{2,1},{3,2},{4,3},{5,4},{6,5},{7,6},{8,15},{9,8},{10,9... | collective-permute-start | bytes 1689608 | tf_op jit(solution)/shard_map/ppermute | solution.py:491
  78.2 0.0 collective-permute-done.7.frame
  78.2 25.5 %shard_map.220 = bf16[100,2500]{1,0:T(8,128)(2,1)} custom-call(bf16[2656,128]{1,0:T(8,128)(2,1)S(1)} %get-tuple-element.53.rows_ref, bf16[128,3200]{1,0:T(8,128)(2,1)S(1)} %get-tuple-element.54.edge, bf16[640,640]{1,0:T(8,128)(2,1)S(1)} %shard_map.219.tensor, bf16[100,2688]{1,0:T(8,128)(2,1)S(1)} %collective-permute-done.7.frame), custom_call_target="tpu_custom_call" | custom-call | flops 24999999488 | bytes 25000000 | tf_op jit(solution)/shard_map/pallas_call | solution.py:472
  103.7 0.0 collective-permute-done.6.payload
  103.7 0.9 shard_map.218
Async XLA Ops:
  3.2 7.8 %copy-start.1 = (bf16[100,2500]{1,0:T(8,128)(2,1)S(1)}, bf16[100,2500]{1,0:T(8,128)(2,1)}, u32[]{:S(2)}) copy-start(bf16[100,2500]{1,0:T(8,128)(2,1)} %t1.1) | copy-start | bytes 1500004
  3.2 7.8 %copy-start.2 = (bf16[100,2500]{1,0:T(8,128)(2,1)S(1)}, bf16[100,2500]{1,0:T(8,128)(2,1)}, u32[]{:S(2)}) copy-start(bf16[100,2500]{1,0:T(8,128)(2,1)} %t2.1) | copy-start | bytes 1500004
  3.2 7.8 %copy-start.3 = (bf16[100,2500]{1,0:T(8,128)(2,1)S(1)}, bf16[100,2500]{1,0:T(8,128)(2,1)}, u32[]{:S(2)}) copy-start(bf16[100,2500]{1,0:T(8,128)(2,1)} %t4.1) | copy-start | bytes 1500004
  3.2 7.8 %copy-start.4 = (bf16[100,2560]{1,0:T(8,128)(2,1)S(1)}, bf16[100,2560]{1,0:T(8,128)(2,1)}, u32[]{:S(2)}) copy-start(bf16[100,2560]{1,0:T(8,128)(2,1)} %shard_map.208.upper_packed) | copy-start | bytes 1536004
  3.2 7.8 %copy-start.6 = (f32[100,100]{1,0:T(8,128)S(1)}, f32[100,100]{1,0:T(8,128)}, u32[]{:S(2)}) copy-start(f32[100,100]{1,0:T(8,128)} %above.3) | copy-start | bytes 120004
  3.2 7.8 %copy-start.7 = (f32[100,100]{1,0:T(8,128)S(1)}, f32[100,100]{1,0:T(8,128)}, u32[]{:S(2)}) copy-start(f32[100,100]{1,0:T(8,128)} %below.3) | copy-start | bytes 120004
  3.2 7.8 %copy-start.10 = (bf16[100,100]{1,0:T(8,128)(2,1)S(1)}, bf16[100,100]{1,0:T(8,128)(2,1)}, u32[]{:S(2)}) copy-start(bf16[100,100]{1,0:T(8,128)(2,1)} %c2.1) | copy-start | bytes 60004
  3.2 16.7 %collective-permute-start = (bf16[100,2560]{1,0:T(8,128)(2,1)}, bf16[100,2560]{1,0:T(8,128)(2,1)S(1)}, u32[]{:S(2)}, u32[]{:S(2)}) collective-permute-start(bf16[100,2560]{1,0:T(8,128)(2,1)} %shard_map.208.upper_packed), channel_id=1, source_target_pairs={{0,7},{1,0},{2,1},{3,2},{4,3},{5,4},{6,5},{7,6},{8,15},{9,8},{10,9... | collective-permute-start | bytes 1536008 | tf_op jit(solution)/shard_map/ppermute | solution.py:491
  10.3 11.2 %collective-permute-start.1 = (bf16[100,2560]{1,0:T(8,128)(2,1)}, bf16[100,2560]{1,0:T(8,128)(2,1)S(1)}, u32[]{:S(2)}, u32[]{:S(2)}) collective-permute-start(bf16[100,2560]{1,0:T(8,128)(2,1)} %shard_map.209.lower_packed), channel_id=1, source_target_pairs={{0,1},{1,2},{2,3},{3,4},{4,5},{5,6},{6,7},{7,0},{8,9},{9,10},{10,1... | collective-permute-start | bytes 1536008 | tf_op jit(solution)/shard_map/ppermute | solution.py:491
  11.0 1.0 copy-start.5
  12.1 2.8 %copy-start = (bf16[8,625,625]{2,0,1:T(8,128)(2,1)S(1)}, bf16[8,625,625]{2,0,1:T(8,128)(2,1)}, u32[]{:S(2)}) copy-start(bf16[8,625,625]{2,0,1:T(8,128)(2,1)} %param.24) | copy-start | bytes 18750004
  14.9 3.1 %copy-start.12 = (s32[640,1]{1,0:T(8,128)S(1)}, s32[640,1]{1,0:T(8,128)}, u32[]{:S(2)}) copy-start(s32[640,1]{1,0:T(8,128)} %constant.8.clone.rows) | copy-start | bytes 7684
  14.9 3.1 %copy-start.14 = (s32[1,640]{1,0:T(1,128)S(1)}, s32[1,640]{1,0:T(1,128)}, u32[]{:S(2)}) copy-start(s32[1,640]{1,0:T(1,128)} %constant.9.clone.columns) | copy-start | bytes 7684
  16.6 49.3 %collective-permute-start.8 = (bf16[625,625]{1,0:T(8,128)(2,1)S(1)}, bf16[625,625]{1,0:T(8,128)(2,1)S(1)}, u32[]{:S(2)}, u32[]{:S(2)}) collective-permute-start(bf16[625,625]{1,0:T(8,128)(2,1)S(1)} %shard_map.212.tensor), channel_id=1, source_target_pairs={{0,1},{1,2},{2,3},{3,4},{4,5},{5,6},{6,7},{7,0},{8,9},{9,10},{10,1... | collective-permute-start | bytes 2343758 | tf_op jit(solution)/shard_map/ppermute | solution.py:491
  16.6 48.5 %collective-permute-start.3 = (bf16[100,2560]{1,0:T(8,128)(2,1)S(1)}, bf16[100,2560]{1,0:T(8,128)(2,1)S(1)}, u32[]{:S(2)}, u32[]{:S(2)}) collective-permute-start(bf16[100,2560]{1,0:T(8,128)(2,1)S(1)} %get-tuple-element.42), channel_id=1, source_target_pairs={{0,9},{1,10},{2,11},{3,12},{4,13},{5,14},{6,15},{7,8},{8,17},{9,18... | collective-permute-start | bytes 1536008 | tf_op jit(solution)/shard_map/ppermute | solution.py:501
  16.9 48.2 %collective-permute-start.4 = (bf16[100,2500]{1,0:T(8,128)(2,1)S(1)}, bf16[100,2500]{1,0:T(8,128)(2,1)S(1)}, u32[]{:S(2)}, u32[]{:S(2)}) collective-permute-start(bf16[100,2500]{1,0:T(8,128)(2,1)S(1)} %get-tuple-element.43), channel_id=1, source_target_pairs={{0,1},{1,2},{2,3},{3,4},{4,5},{5,6},{6,7},{7,0},{8,9},{9,10},{10,1... | collective-permute-start | bytes 1500008 | tf_op jit(solution)/shard_map/ppermute | solution.py:491
  29.3 25.5 %copy-start.8 = (f32[100,100]{1,0:T(8,128)S(1)}, f32[100,100]{1,0:T(8,128)}, u32[]{:S(2)}) copy-start(f32[100,100]{1,0:T(8,128)} %right.3) | copy-start | bytes 120004
  29.3 25.5 %copy-start.9 = (f32[100,100]{1,0:T(8,128)S(1)}, f32[100,100]{1,0:T(8,128)}, u32[]{:S(2)}) copy-start(f32[100,100]{1,0:T(8,128)} %left.3) | copy-start | bytes 120004
  54.5 15.2 %collective-permute-start.2 = (bf16[100,2816]{1,0:T(8,128)(2,1)S(1)}, bf16[100,2816]{1,0:T(8,128)(2,1)S(1)}, u32[]{:S(2)}, u32[]{:S(2)}) collective-permute-start(bf16[100,2816]{1,0:T(8,128)(2,1)S(1)} %get-tuple-element.41), channel_id=1, source_target_pairs={{0,9},{1,10},{2,11},{3,12},{4,13},{5,14},{6,15},{7,8},{8,17},{9,18... | collective-permute-start | bytes 1689608 | tf_op jit(solution)/shard_map/ppermute | solution.py:501
  61.7 8.0 %collective-permute-start.5 = (f32[112,128]{1,0:T(8,128)S(1)}, f32[112,128]{1,0:T(8,128)S(1)}, u32[]{:S(2)}, u32[]{:S(2)}) collective-permute-start(f32[112,128]{1,0:T(8,128)S(1)} %get-tuple-element.45.after), channel_id=1, source_target_pairs={{0,9},{1,10},{2,11},{3,12},{4,13},{5,14},{6,15},{7,8},{8,17},{9,18... | collective-permute-start | bytes 172040 | tf_op jit(solution)/shard_map/ppermute | solution.py:501
  65.1 1.0 copy-start.11
  65.1 1.0 copy-start.13
  65.1 13.1 %collective-permute-start.7 = (bf16[100,2688]{1,0:T(8,128)(2,1)S(1)}, bf16[100,2688]{1,0:T(8,128)(2,1)S(1)}, u32[]{:S(2)}, u32[]{:S(2)}) collective-permute-start(bf16[100,2688]{1,0:T(8,128)(2,1)S(1)} %get-tuple-element.48), channel_id=1, source_target_pairs={{0,1},{1,2},{2,3},{3,4},{4,5},{5,6},{6,7},{7,0},{8,9},{9,10},{10,1... | collective-permute-start | bytes 1612808 | tf_op jit(solution)/shard_map/ppermute | solution.py:491
  72.8 31.0 %collective-permute-start.6 = (bf16[100,2816]{1,0:T(8,128)(2,1)S(1)}, bf16[100,2816]{1,0:T(8,128)(2,1)S(1)}, u32[]{:S(2)}, u32[]{:S(2)}) collective-permute-start(bf16[100,2816]{1,0:T(8,128)(2,1)S(1)} %get-tuple-element.47), channel_id=1, source_target_pairs={{0,7},{1,0},{2,1},{3,2},{4,3},{5,4},{6,5},{7,6},{8,15},{9,8},{10,9... | collective-permute-start | bytes 1689608 | tf_op jit(solution)/shard_map/ppermute | solution.py:491

commit v5 on v1

--- a/solution.py
+++ b/solution.py
@@ -161,10 +161,12 @@
     high[...], low[...] = halves(values)
 
 
-def gram_of(high, low):
-    both = product(high[...], jnp.concatenate([high[...], low[...]], 1), TN)
-    mixed = both[:, LANES:]
-    return both[:, :LANES] + mixed + mixed.T
+def gram_and_overlap(other, high, low):
+    left = jnp.concatenate([high[...], other], 1)
+    both = product(left, jnp.concatenate([high[...], low[...]], 1), TN)
+    mixed = both[:LANES, LANES:]
+    gram = both[:LANES, :LANES] + mixed + mixed.T
+    return gram, both[LANES:, :LANES] + both[LANES:, LANES:]
 
 
 def overlap(other, high, low):
@@ -240,10 +242,9 @@
     store_halves(lower_sketch[...] + sketched(stack[...], square_of(above, bond)), under, under_low)
     fill(stack, unpack(lower_packed, bond, site))
     store_halves(upper_sketch[...] + sketched(stack[...], square_of(below, bond)), over, over_low)
-    grams = [gram_of(over, over_low), gram_of(under, under_low)]
-    mixed_over = overlap(upper[...], over, over_low)
-    mixed_under = overlap(lower[...], under, under_low)
-    inverse_over, inverse_under = inverse_factors(grams, bond)
+    gram_over, mixed_over = gram_and_overlap(upper[...], over, over_low)
+    gram_under, mixed_under = gram_and_overlap(lower[...], under, under_low)
+    inverse_over, inverse_under = inverse_factors([gram_over, gram_under], bond)
     store_frame_rows(over, over_low, inverse_over, rows_ref, plain, tail, site)
     frame_out[...] = frame_from(under, under_low, inverse_under).astype(BF16)
     corner_top[...] = scaled_corner(product_split(inverse_over, mixed_over, NT), bond)
@@ -256,8 +257,8 @@
     corner = square_of(c1, bond).T.astype(BF16)
     fill(half, half_tiles(corner, [edge[:, k * LANES : (k + 1) * LANES] for k in range(site)]))
     store_halves(side_sketch[...] + sketched(half[...], square_of(left, bond)), total, total_low)
-    mixed = overlap(side[...], total, total_low)
-    (inverse,) = inverse_factors([gram_of(total, total_low)], bond)
+    gram, mixed = gram_and_overlap(side[...], total, total_low)
+    (inverse,) = inverse_factors([gram], bond)
     inverse_ref[...] = inverse[: inverse_ref.shape[0]]
     frame = frame_from(total, total_low, inverse)
     pack([frame[k * LANES : (k + 1) * LANES, :] for k in range(site)], frame_out, bond)

time: 103 us -> 103 us (level)
  no operation moved by 1% of the time
where the time goes in v5:
time: 103 us
  Pallas kernels  79.7 us (77%)
  starting transfers between devices  10.3 us (10%)
  waiting for transfers between devices  8.88 us (9%)
  local copies, waits for them, and re-layouts  2.55 us (2%)
  between operations  1.54 us (1%)
    pallas_call x9, Pallas kernels, call(): pl.pallas_call(kernel, grid=(1,), in_specs=specs, out_specs=[block_of(out...  74.6 us
    ppermute x6, starting transfers between devices, shift(): return lax.ppermute(value, axis, pairs)  9.71 us
    ppermute x3, waiting for transfers between devices, shift_both(): return lax.ppermute(value, ('col', 'row'), pairs)  5.61 us
    pallas_call x2, Pallas kernels, arrange(): pl.pallas_call(arrange_kernel, in_specs=[vmem, vmem, vmem, pl.BlockSpec(m...  3.4 us
    ppermute x6, waiting for transfers between devices, shift(): return lax.ppermute(value, axis, pairs)  3.27 us
    unnamed x30, local copies, waits for them, and re-layouts  2.55 us
  transfers between devices with their start and end apart: 9, of which 3 were waited for; matrix products, arithmetic and copies ran while one was open for 0% of the time, Pallas kernels for 73%

profile of v5, /device:TPU:0, one launch (start us, length us, event | category | flops | bytes accessed | tf_op | source)
XLA Modules:
  0.0 103.0 jit_solution(15429643641317989209)
XLA Ops:
  0.6 0.0 copy-start.1
  0.6 0.0 copy-start.10
  0.7 0.0 copy-start.2
  0.7 0.0 copy-start.3
  0.7 0.0 copy-start.7
  0.7 0.0 copy-start.6
  0.7 0.0 copy-start.8
  0.7 3.5 %shard_map.208 = (bf16[100,2560]{1,0:T(8,128)(2,1)}, bf16[100,2560]{1,0:T(8,128)(2,1)}) custom-call(bf16[100,100]{1,0:T(8,128)(2,1)} %c1.1, bf16[100,2500]{1,0:T(8,128)(2,1)} %t1.3, bf16[100,100]{1,0:T(8,128)(2,1)} %c4.1, bf16[100,2500]{1,0:T(8,128)(2,1)} %t3.1), custom_call_target="tpu_custom_call" | custom-call | flops 2000000000 | bytes 2000000 | tf_op jit(solution)/shard_map/pallas_call | solution.py:466
  4.2 4.5 %collective-permute-start = (bf16[100,2560]{1,0:T(8,128)(2,1)}, bf16[100,2560]{1,0:T(8,128)(2,1)S(1)}, u32[]{:S(2)}, u32[]{:S(2)}) collective-permute-start(bf16[100,2560]{1,0:T(8,128)(2,1)} %get-tuple-element.34.upper_packed.after), channel_id=1, source_target_pairs={{0,7},{1,0},{2,1},{3,2},{4,3},{5,4},{6,5},{7,6},{8,15},{9,8},{10,9... | collective-permute-start | bytes 1536008 | tf_op jit(solution)/shard_map/ppermute | solution.py:485
  8.7 0.0 copy-start
  8.7 0.0 collective-permute-start.1
  8.7 0.0 copy-done.1
  8.7 0.0 copy-done.10
  8.7 0.0 copy-done.2
  8.7 0.0 copy-done.3
  8.7 0.0 copy-done.7
  8.7 0.0 copy-done.6
  8.7 0.0 copy-done.8
  8.7 0.0 copy-start.4
  8.8 1.2 %copy-done.4 = bf16[100,2560]{1,0:T(8,128)(2,1)S(1)} copy-done((bf16[100,2560]{1,0:T(8,128)(2,1)S(1)}, bf16[100,2560]{1,0:T(8,128)(2,1)}, u32[]{:S(2)}) %copy-start.4) | copy-done | bytes 512024
  9.9 0.0 copy-start.5
  9.9 1.3 %copy-done.5 = bf16[100,2560]{1,0:T(8,128)(2,1)S(1)} copy-done((bf16[100,2560]{1,0:T(8,128)(2,1)S(1)}, bf16[100,2560]{1,0:T(8,128)(2,1)}, u32[]{:S(2)}) %copy-start.5) | copy-done | bytes 512024
  11.2 2.0 %shard_map.209 = (bf16[128,3200]{1,0:T(8,128)(2,1)S(1)}, bf16[100,2500]{1,0:T(8,128)(2,1)S(1)}, bf16[3200,128]{1,0:T(8,128)(2,1)S(1)}, f32[3200,128]{1,0:T(8,128...) custom-call(bf16[100,100]{1,0:T(8,128)(2,1)S(1)} %copy-done.10, ...), custom_call_target="tpu_custom_call" | custom-call | flops 2000000000 | bytes 2000000 | tf_op jit(solution)/shard_map/pallas_call | solution.py:466
  13.2 0.1 collective-permute-start.3
  13.3 0.1 collective-permute-start.4
  14.0 0.0 copy-done
  14.0 0.0 copy-start.12
  14.0 0.0 copy-start.14
  14.1 1.7 %shard_map.211.tensor = bf16[625,625]{1,0:T(8,128)(2,1)S(1)} custom-call(s32[1]{0:T(128)} %bitcast.2.pattern, bf16[625,8,625]{2,1,0:T(8,128)(2,1)S(1)} %bitcast.3), custom_call_target="tpu_custom_call" | custom-call | flops 2000000000 | bytes 2000000 | tf_op jit(solution)/shard_map/pallas_call | solution.py:520
  15.7 1.7 %collective-permute-start.8 = (bf16[625,625]{1,0:T(8,128)(2,1)S(1)}, bf16[625,625]{1,0:T(8,128)(2,1)S(1)}, u32[]{:S(2)}, u32[]{:S(2)}) collective-permute-start(bf16[625,625]{1,0:T(8,128)(2,1)S(1)} %shard_map.211.tensor), channel_id=1, source_target_pairs={{0,1},{1,2},{2,3},{3,4},{4,5},{5,6},{6,7},{7,0},{8,9},{9,10},{10,1... | collective-permute-start | bytes 2343758 | tf_op jit(solution)/shard_map/ppermute | solution.py:485
  17.4 0.0 copy-done.12
  17.4 0.0 copy-done.14
  17.4 1.7 %shard_map.212.tensor = bf16[640,640]{1,0:T(8,128)(2,1)S(1)} custom-call(bf16[625,625]{1,0:T(8,128)(2,1)S(1)} %shard_map.211.tensor, s32[640,1]{1,0:T(8,128)S(1)} %copy-done.12, s32[1,640]{1,0:T(1,128)S(1)} %copy-done.14, bf16[100,2560]{1,0:T(8,128)(2,1)S(1)} %copy-done.5), custom_call_target="tpu_custom_call" | custom-call | flops 2000000000 | bytes 2000000 | tf_op jit(solution)/shard_map/pallas_call | solution.py:537
  19.1 2.4 %collective-permute-done.upper_packed = bf16[100,2560]{1,0:T(8,128)(2,1)S(1)} collective-permute-done((bf16[100,2560]{1,0:T(8,128)(2,1)}, bf16[100,2560]{1,0:T(8,128)(2,1)S(1)}, u32[]{:S(2)}, u32[]{:S(2)}) %collective-permute-start) | collective-permute-done | bytes 512032 | tf_op jit(solution)/shard_map/ppermute | solution.py:485
  21.6 0.8 collective-permute-done.1.lower_packed
  22.4 7.9 %shard_map.210 = (bf16[2656,128]{1,0:T(8,128)(2,1)S(1)}, bf16[3200,128]{1,0:T(8,128)(2,1)S(1)}, bf16[100,100]{1,0:T(8,128)(2,1)S(1)}, bf16[100,100]{1,0:T(8,128)(2,1)S(1)}) custom-call(bf16[100,2560]{1,0:T(8,128)(2,1)S(1)} %collective-permute-done.upper_packed, bf16[100,2560]{1,0:T(8,128)(2,1)S(1)} %collective-permute-done.1.lower_packed, ...), custom_call_target="tpu_custom_call" | custom-call | flops 8000000000 | bytes 8000000 | tf_op jit(solution)/shard_map/pallas_call | solution.py:466
  30.3 0.0 copy-start.9
  30.3 24.9 %shard_map.213 = (bf16[100,2816]{1,0:T(8,128)(2,1)S(1)}, bf16[128,3200]{1,0:T(8,128)(2,1)S(1)}) custom-call(bf16[2656,128]{1,0:T(8,128)(2,1)S(1)} %get-tuple-element.40.rows_ref, bf16[128,3200]{1,0:T(8,128)(2,1)S(1)} %get-tuple-element.41.edge, bf16[640,640]{1,0:T(8,128)(2,1)S(1)} %shard_map.212.tensor, bf16[3200,128]{1,0:T(8,128)(2,1)S(1)} %get-tuple-element.42.frame, ...), custom_call_target="tpu_custom_call" | custom-call | flops 24999999488 | bytes 25000000 | tf_op jit(solution)/shard_map/pallas_call | solution.py:466
  55.2 0.1 collective-permute-start.2
  55.3 0.0 copy-done.9
  55.3 5.9 %shard_map.214 = (f32[112,128]{1,0:T(8,128)S(1)}, bf16[100,2688]{1,0:T(8,128)(2,1)S(1)}) custom-call(bf16[100,100]{1,0:T(8,128)(2,1)S(1)} %get-tuple-element.43.refs_0_.c1, bf16[128,3200]{1,0:T(8,128)(2,1)S(1)} %get-tuple-element.48.edge, f32[100,100]{1,0:T(8,128)S(1)} %copy-done.9, bf16[3200,128]{1,0:T(8,128)(2,1)S(1)} %get-tuple-element.49.side, ...), custom_call_target="tpu_custom_call" | custom-call | flops 5000000000 | bytes 5000000 | tf_op jit(solution)/shard_map/pallas_call | solution.py:466
  61.3 0.5 collective-permute-start.5
  61.8 0.0 collective-permute-done.4.t1
  61.8 0.0 copy-start.11
  61.8 0.0 copy-start.13
  61.8 0.2 collective-permute-start.7
  62.0 0.0 collective-permute-done.3.side_packed
  62.0 0.8 shard_map.215
  62.8 0.0 collective-permute-done.8.tensor
  62.8 0.0 copy-done.11
  62.8 0.0 copy-done.13
  62.8 1.7 %shard_map.218.tensor = bf16[640,640]{1,0:T(8,128)(2,1)S(1)} custom-call(bf16[625,625]{1,0:T(8,128)(2,1)S(1)} %collective-permute-done.8.tensor, s32[640,1]{1,0:T(8,128)S(1)} %copy-done.11, s32[1,640]{1,0:T(1,128)S(1)} %copy-done.13, f32[112,128]{1,0:T(8,128)S(1)} %get-tuple-element.51.after), custom_call_target="tpu_custom_call" | custom-call | flops 2000000000 | bytes 2000000 | tf_op jit(solution)/shard_map/pallas_call | solution.py:537
  64.6 5.6 %collective-permute-done.5.inverse_ref = f32[112,128]{1,0:T(8,128)S(1)} collective-permute-done((f32[112,128]{1,0:T(8,128)S(1)}, f32[112,128]{1,0:T(8,128)S(1)}, u32[]{:S(2)}, u32[]{:S(2)}) %collective-permute-start.5) | collective-permute-done | bytes 57376 | tf_op jit(solution)/shard_map/ppermute | solution.py:495
  70.2 0.0 collective-permute-done.2.payload
  70.2 3.1 %shard_map.216 = (bf16[2656,128]{1,0:T(8,128)(2,1)S(1)}, bf16[100,100]{1,0:T(8,128)(2,1)}, bf16[100,2816]{1,0:T(8,128)(2,1)S(1)}) custom-call(bf16[100,2816]{1,0:T(8,128)(2,1)S(1)} %collective-permute-done.2.payload, f32[3200,128]{1,0:T(8,128)S(1)} %get-tuple-element.52.side_sketch, f32[100,100]{1,0:T(8,128)S(1)} %copy-done.9, ...), custom_call_target="tpu_custom_call" | custom-call | flops 4000000000 | bytes 4000000 | tf_op jit(solution)/shard_map/pallas_call | solution.py:466
  73.3 3.2 %collective-permute-start.6 = (bf16[100,2816]{1,0:T(8,128)(2,1)S(1)}, bf16[100,2816]{1,0:T(8,128)(2,1)S(1)}, u32[]{:S(2)}, u32[]{:S(2)}) collective-permute-start(bf16[100,2816]{1,0:T(8,128)(2,1)S(1)} %get-tuple-element.53), channel_id=1, source_target_pairs={{0,7},{1,0},{2,1},{3,2},{4,3},{5,4},{6,5},{7,6},{8,15},{9,8},{10,9... | collective-permute-start | bytes 1689608 | tf_op jit(solution)/shard_map/ppermute | solution.py:485
  76.5 0.0 collective-permute-done.7.frame
  76.5 25.6 %shard_map.219 = bf16[100,2500]{1,0:T(8,128)(2,1)} custom-call(bf16[2656,128]{1,0:T(8,128)(2,1)S(1)} %get-tuple-element.59.rows_ref, bf16[128,3200]{1,0:T(8,128)(2,1)S(1)} %get-tuple-element.60.edge, bf16[640,640]{1,0:T(8,128)(2,1)S(1)} %shard_map.218.tensor, bf16[100,2688]{1,0:T(8,128)(2,1)S(1)} %collective-permute-done.7.frame), custom_call_target="tpu_custom_call" | custom-call | flops 24999999488 | bytes 25000000 | tf_op jit(solution)/shard_map/pallas_call | solution.py:466
  102.1 0.0 collective-permute-done.6.payload
  102.1 0.9 shard_map.217
Async XLA Ops:
  0.6 8.1 %copy-start.1 = (bf16[100,2500]{1,0:T(8,128)(2,1)S(1)}, bf16[100,2500]{1,0:T(8,128)(2,1)}, u32[]{:S(2)}) copy-start(bf16[100,2500]{1,0:T(8,128)(2,1)} %t1.3) | copy-start | bytes 1500004
  0.6 8.1 %copy-start.10 = (bf16[100,100]{1,0:T(8,128)(2,1)S(1)}, bf16[100,100]{1,0:T(8,128)(2,1)}, u32[]{:S(2)}) copy-start(bf16[100,100]{1,0:T(8,128)(2,1)} %c2.1) | copy-start | bytes 60004
  0.7 8.0 %copy-start.2 = (bf16[100,2500]{1,0:T(8,128)(2,1)S(1)}, bf16[100,2500]{1,0:T(8,128)(2,1)}, u32[]{:S(2)}) copy-start(bf16[100,2500]{1,0:T(8,128)(2,1)} %t2.1) | copy-start | bytes 1500004
  0.7 8.0 %copy-start.3 = (bf16[100,2500]{1,0:T(8,128)(2,1)S(1)}, bf16[100,2500]{1,0:T(8,128)(2,1)}, u32[]{:S(2)}) copy-start(bf16[100,2500]{1,0:T(8,128)(2,1)} %t4.1) | copy-start | bytes 1500004
  0.7 8.0 %copy-start.7 = (f32[100,100]{1,0:T(8,128)S(1)}, f32[100,100]{1,0:T(8,128)}, u32[]{:S(2)}) copy-start(f32[100,100]{1,0:T(8,128)} %below.3) | copy-start | bytes 120004
  0.7 8.0 %copy-start.6 = (f32[100,100]{1,0:T(8,128)S(1)}, f32[100,100]{1,0:T(8,128)}, u32[]{:S(2)}) copy-start(f32[100,100]{1,0:T(8,128)} %above.3) | copy-start | bytes 120004
  0.7 8.0 %copy-start.8 = (f32[100,100]{1,0:T(8,128)S(1)}, f32[100,100]{1,0:T(8,128)}, u32[]{:S(2)}) copy-start(f32[100,100]{1,0:T(8,128)} %right.3) | copy-start | bytes 120004
  4.2 17.4 %collective-permute-start = (bf16[100,2560]{1,0:T(8,128)(2,1)}, bf16[100,2560]{1,0:T(8,128)(2,1)S(1)}, u32[]{:S(2)}, u32[]{:S(2)}) collective-permute-start(bf16[100,2560]{1,0:T(8,128)(2,1)} %get-tuple-element.34.upper_packed.after), channel_id=1, source_target_pairs={{0,7},{1,0},{2,1},{3,2},{4,3},{5,4},{6,5},{7,6},{8,15},{9,8},{10,9... | collective-permute-start | bytes 1536008 | tf_op jit(solution)/shard_map/ppermute | solution.py:485
  8.7 5.3 %copy-start = (bf16[8,625,625]{2,0,1:T(8,128)(2,1)S(1)}, bf16[8,625,625]{2,0,1:T(8,128)(2,1)}, u32[]{:S(2)}) copy-start(bf16[8,625,625]{2,0,1:T(8,128)(2,1)} %param.24) | copy-start | bytes 18750004
  8.7 13.7 %collective-permute-start.1 = (bf16[100,2560]{1,0:T(8,128)(2,1)}, bf16[100,2560]{1,0:T(8,128)(2,1)S(1)}, u32[]{:S(2)}, u32[]{:S(2)}) collective-permute-start(bf16[100,2560]{1,0:T(8,128)(2,1)} %get-tuple-element.35.lower_packed), channel_id=1, source_target_pairs={{0,1},{1,2},{2,3},{3,4},{4,5},{5,6},{6,7},{7,0},{8,9},{9,10},{10,1... | collective-permute-start | bytes 1536008 | tf_op jit(solution)/shard_map/ppermute | solution.py:485
  8.7 1.2 %copy-start.4 = (bf16[100,2560]{1,0:T(8,128)(2,1)S(1)}, bf16[100,2560]{1,0:T(8,128)(2,1)}, u32[]{:S(2)}) copy-start(bf16[100,2560]{1,0:T(8,128)(2,1)} %get-tuple-element.35.lower_packed) | copy-start | bytes 1536004
  9.9 1.3 %copy-start.5 = (bf16[100,2560]{1,0:T(8,128)(2,1)S(1)}, bf16[100,2560]{1,0:T(8,128)(2,1)}, u32[]{:S(2)}) copy-start(bf16[100,2560]{1,0:T(8,128)(2,1)} %get-tuple-element.34.upper_packed.after) | copy-start | bytes 1536004
  13.2 48.7 %collective-permute-start.3 = (bf16[100,2560]{1,0:T(8,128)(2,1)S(1)}, bf16[100,2560]{1,0:T(8,128)(2,1)S(1)}, u32[]{:S(2)}, u32[]{:S(2)}) collective-permute-start(bf16[100,2560]{1,0:T(8,128)(2,1)S(1)} %get-tuple-element.46), channel_id=1, source_target_pairs={{0,9},{1,10},{2,11},{3,12},{4,13},{5,14},{6,15},{7,8},{8,17},{9,18... | collective-permute-start | bytes 1536008 | tf_op jit(solution)/shard_map/ppermute | solution.py:495
  13.3 48.5 %collective-permute-start.4 = (bf16[100,2500]{1,0:T(8,128)(2,1)S(1)}, bf16[100,2500]{1,0:T(8,128)(2,1)S(1)}, u32[]{:S(2)}, u32[]{:S(2)}) collective-permute-start(bf16[100,2500]{1,0:T(8,128)(2,1)S(1)} %get-tuple-element.47), channel_id=1, source_target_pairs={{0,1},{1,2},{2,3},{3,4},{4,5},{5,6},{6,7},{7,0},{8,9},{9,10},{10,1... | collective-permute-start | bytes 1500008 | tf_op jit(solution)/shard_map/ppermute | solution.py:485
  14.0 3.4 %copy-start.12 = (s32[640,1]{1,0:T(8,128)S(1)}, s32[640,1]{1,0:T(8,128)}, u32[]{:S(2)}) copy-start(s32[640,1]{1,0:T(8,128)} %constant.8.clone.rows) | copy-start | bytes 7684
  14.0 3.4 %copy-start.14 = (s32[1,640]{1,0:T(1,128)S(1)}, s32[1,640]{1,0:T(1,128)}, u32[]{:S(2)}) copy-start(s32[1,640]{1,0:T(1,128)} %constant.9.clone.columns) | copy-start | bytes 7684
  15.7 47.1 %collective-permute-start.8 = (bf16[625,625]{1,0:T(8,128)(2,1)S(1)}, bf16[625,625]{1,0:T(8,128)(2,1)S(1)}, u32[]{:S(2)}, u32[]{:S(2)}) collective-permute-start(bf16[625,625]{1,0:T(8,128)(2,1)S(1)} %shard_map.211.tensor), channel_id=1, source_target_pairs={{0,1},{1,2},{2,3},{3,4},{4,5},{5,6},{6,7},{7,0},{8,9},{9,10},{10,1... | collective-permute-start | bytes 2343758 | tf_op jit(solution)/shard_map/ppermute | solution.py:485
  30.3 25.0 %copy-start.9 = (f32[100,100]{1,0:T(8,128)S(1)}, f32[100,100]{1,0:T(8,128)}, u32[]{:S(2)}) copy-start(f32[100,100]{1,0:T(8,128)} %left.3) | copy-start | bytes 120004
  55.2 14.9 %collective-permute-start.2 = (bf16[100,2816]{1,0:T(8,128)(2,1)S(1)}, bf16[100,2816]{1,0:T(8,128)(2,1)S(1)}, u32[]{:S(2)}, u32[]{:S(2)}) collective-permute-start(bf16[100,2816]{1,0:T(8,128)(2,1)S(1)} %get-tuple-element.45), channel_id=1, source_target_pairs={{0,9},{1,10},{2,11},{3,12},{4,13},{5,14},{6,15},{7,8},{8,17},{9,18... | collective-permute-start | bytes 1689608 | tf_op jit(solution)/shard_map/ppermute | solution.py:495
  61.3 8.9 %collective-permute-start.5 = (f32[112,128]{1,0:T(8,128)S(1)}, f32[112,128]{1,0:T(8,128)S(1)}, u32[]{:S(2)}, u32[]{:S(2)}) collective-permute-start(f32[112,128]{1,0:T(8,128)S(1)} %get-tuple-element.51.after), channel_id=1, source_target_pairs={{0,9},{1,10},{2,11},{3,12},{4,13},{5,14},{6,15},{7,8},{8,17},{9,18... | collective-permute-start | bytes 172040 | tf_op jit(solution)/shard_map/ppermute | solution.py:495
  61.8 1.1 %copy-start.11 = (s32[640,1]{1,0:T(8,128)S(1)}, s32[640,1]{1,0:T(8,128)}, u32[]{:S(2)}) copy-start(s32[640,1]{1,0:T(8,128)} %constant.10.clone.rows) | copy-start | bytes 7684
  61.8 1.1 %copy-start.13 = (s32[1,640]{1,0:T(1,128)S(1)}, s32[1,640]{1,0:T(1,128)}, u32[]{:S(2)}) copy-start(s32[1,640]{1,0:T(1,128)} %constant.11.clone.columns) | copy-start | bytes 7684
  61.8 14.8 %collective-permute-start.7 = (bf16[100,2688]{1,0:T(8,128)(2,1)S(1)}, bf16[100,2688]{1,0:T(8,128)(2,1)S(1)}, u32[]{:S(2)}, u32[]{:S(2)}) collective-permute-start(bf16[100,2688]{1,0:T(8,128)(2,1)S(1)} %get-tuple-element.54), channel_id=1, source_target_pairs={{0,1},{1,2},{2,3},{3,4},{4,5},{5,6},{6,7},{7,0},{8,9},{9,10},{10,1... | collective-permute-start | bytes 1612808 | tf_op jit(solution)/shard_map/ppermute | solution.py:485
  73.3 28.8 %collective-permute-start.6 = (bf16[100,2816]{1,0:T(8,128)(2,1)S(1)}, bf16[100,2816]{1,0:T(8,128)(2,1)S(1)}, u32[]{:S(2)}, u32[]{:S(2)}) collective-permute-start(bf16[100,2816]{1,0:T(8,128)(2,1)S(1)} %get-tuple-element.53), channel_id=1, source_target_pairs={{0,7},{1,0},{2,1},{3,2},{4,3},{5,4},{6,5},{7,6},{8,15},{9,8},{10,9... | collective-permute-start | bytes 1689608 | tf_op jit(solution)/shard_map/ppermute | solution.py:485
